TPU v7x, 32 devices: a whole 2x2x4 slice. The times are simulated.
32 devices in a mesh: dp: 4 (over y, x), row: 4 (over z), col: 2 (over core).
Axes of the slice: x: 2, y: 2, z: 4, core: 2. Of those that a mesh axis runs over, the one named last changes fastest.
Arguments:
- hidden_in: bfloat16 [2, 4096, 2048], P(None, ('dp', 'row'), 'col'), may hold values from -6 to 6
- attn_gain: float32 [2048], P('col'), may hold values from 0.25 to 1.75
- ffn_gain: float32 [2048], P('col'), may hold values from 0.25 to 1.75
- query_weight: bfloat16 [2048, 2048], P('col', 'row'), may hold values from -0.1875 to 0.1875
- key_weight: bfloat16 [2048, 1024], P('col', 'row'), may hold values from -0.1875 to 0.1875
- value_weight: bfloat16 [2048, 1024], P('col', 'row'), may hold values from -0.125 to 0.125
- output_weight: bfloat16 [2048, 2048], P('row', 'col'), may hold values from -0.5 to 0.5
- gate_weight: bfloat16 [2048, 8192], P('col', 'row'), may hold values from -0.125 to 0.125
- up_weight: bfloat16 [2048, 8192], P('col', 'row'), may hold values from -0.125 to 0.125
- down_weight: bfloat16 [8192, 2048], P('row', 'col'), may hold values from -0.125 to 0.125
- prefix_len: int32 [2, 4], P(None, 'dp'), may hold values from 102 to 512
- out_grad: bfloat16 [2, 4096, 2048], P(None, ('dp', 'row'), 'col'), may hold values from -6 to 6
Outputs:
- output: bfloat16 [2, 4096, 2048], P(None, ('dp', 'row'), 'col')
- input_grad: float32 [2, 4096, 2048], P(None, ('dp', 'row'), 'col')
- grad_attn_gain: float32 [2048], P('col')
- grad_ffn_gain: float32 [2048], P('col')
- grad_query_weight: float32 [2048, 2048], P('col', 'row')
- grad_key_weight: float32 [2048, 1024], P('col', 'row')
- grad_value_weight: float32 [2048, 1024], P('col', 'row')
- grad_output_weight: float32 [2048, 2048], P('row', 'col')
- grad_gate_weight: float32 [2048, 8192], P('col', 'row')
- grad_up_weight: float32 [2048, 8192], P('col', 'row')
- grad_down_weight: float32 [8192, 2048], P('row', 'col')
All inputs are finite; a program needn't handle non-finite values.
Results may differ from a plain program's by a relative error of at most 0.025.
Values may be sent and summed in bfloat16 or wider, within the bound.
A program may use at most 320 MiB of HBM per device.

v0:
```python
import math

import jax
import jax.numpy as jnp
from jax import lax
from jax.sharding import PartitionSpec as P

WIDTH = 2048
HEADS = 16
KV_HEADS = 8
HEAD_DIM = 128


epsilon = 1e-05
rope_base = 1000000.0
masked_score = -1e30


def rope_tables(length, size):
    half_size = size // 2
    inverse = rope_base ** (-(jnp.arange(half_size, dtype=jnp.float32) * 2.0 / size))
    angle = jnp.arange(length, dtype=jnp.float32)[:, None] * inverse[None, :]
    cosine = jnp.concatenate([jnp.cos(angle), jnp.cos(angle)], axis=1)[:, None, :]
    sine = jnp.concatenate([jnp.sin(angle), jnp.sin(angle)], axis=1)[:, None, :]
    return (cosine, sine)


def rotate(values):
    half_size = values.shape[-1] // 2
    return jnp.concatenate([-values[..., half_size:], values[..., :half_size]], axis=-1)


def rotate_back(values):
    half_size = values.shape[-1] // 2
    return jnp.concatenate([values[..., half_size:], -values[..., :half_size]], axis=-1)


def rope(values, cosine, sine):
    return values * cosine + rotate(values) * sine


def rope_back(gradient, cosine, sine):
    return gradient * cosine + rotate_back(gradient * sine)


def width_total(values):
    return lax.psum(values, "col")


def gather_tokens(shard_rows):
    return lax.all_gather(shard_rows, "row", axis=0, tiled=True)


def contract_rows(left_side, right_side):
    return lax.dot_general(
        left_side, right_side, (((0,), (0,)), ((), ())), preferred_element_type=jnp.float32
    )


def scatter_tokens(left_side, right_side, transposed):
    contracted = ((1,), (1,)) if transposed else ((1,), (0,))
    return lax.psum_scatter(
        lax.dot_general(
            left_side, right_side, (contracted, ((), ())), preferred_element_type=jnp.float32
        ).astype(jnp.bfloat16),
        "row",
        scatter_dimension=0,
        tiled=True,
    ).astype(jnp.float32)


def allowed_mask(first_row, block, length, prefix_one):
    columns = jnp.arange(length, dtype=jnp.int32)
    positions = first_row + jnp.arange(block, dtype=jnp.int32)
    return (columns[None, :] <= positions[:, None]) | (columns[None, :] < prefix_one)


def attend(queries, keys_wide, values_wide, prefix_one, block):
    length = keys_wide.shape[0]
    scale = 1.0 / math.sqrt(queries.shape[-1])
    starts = jnp.arange(length // block, dtype=jnp.int32) * block

    def one_block(first_row):
        query_block = lax.dynamic_slice_in_dim(queries, first_row, block, 0)
        raw = jnp.einsum("qhd,khd->hqk", query_block, keys_wide, preferred_element_type=jnp.float32)
        allowed = allowed_mask(first_row, block, length, prefix_one)
        scores = jnp.where(allowed[None], raw * scale, masked_score)
        topmost = jnp.max(scores, axis=-1, keepdims=True)
        exponent = jnp.exp(scores - topmost)
        total = jnp.sum(exponent, axis=-1, keepdims=True)
        weights = (exponent / total).astype(jnp.bfloat16)
        attended = jnp.einsum(
            "hqk,khd->qhd", weights, values_wide, preferred_element_type=jnp.float32
        )
        return (attended, (topmost + jnp.log(total))[..., 0])

    attended, log_sums = lax.map(one_block, starts)
    return (attended.reshape(length, queries.shape[1], queries.shape[2]), log_sums)


def attend_back(queries, keys_wide, values_wide, head_grads, log_sums, prefix_one, block):
    length = keys_wide.shape[0]
    scale = 1.0 / math.sqrt(queries.shape[-1])
    starts = jnp.arange(length // block, dtype=jnp.int32) * block

    def one_block(carry, inputs):
        key_grad, value_grad = carry
        first_row, log_block = inputs
        query_block = lax.dynamic_slice_in_dim(queries, first_row, block, 0)
        grad_block = lax.dynamic_slice_in_dim(head_grads, first_row, block, 0)
        raw = jnp.einsum("qhd,khd->hqk", query_block, keys_wide, preferred_element_type=jnp.float32)
        allowed = allowed_mask(first_row, block, length, prefix_one)
        scores = jnp.where(allowed[None], raw * scale, masked_score)
        probs = jnp.exp(scores - log_block[..., None])
        weights = probs.astype(jnp.bfloat16)
        value_grad = value_grad + jnp.einsum(
            "hqk,qhd->khd", weights, grad_block, preferred_element_type=jnp.float32
        )
        prob_grad = jnp.einsum(
            "qhd,khd->hqk", grad_block, values_wide, preferred_element_type=jnp.float32
        )
        score_grad = probs * (prob_grad - jnp.sum(probs * prob_grad, axis=-1, keepdims=True))
        rounded = (score_grad * scale).astype(jnp.bfloat16)
        query_grad = jnp.einsum(
            "hqk,khd->qhd", rounded, keys_wide, preferred_element_type=jnp.float32
        )
        key_grad = key_grad + jnp.einsum(
            "hqk,qhd->khd", rounded, query_block, preferred_element_type=jnp.float32
        )
        return ((key_grad, value_grad), query_grad)

    zeros = jnp.zeros(keys_wide.shape, jnp.float32)
    (key_grad, value_grad), query_grads = lax.scan(one_block, (zeros, zeros), (starts, log_sums))
    return (query_grads.reshape(queries.shape), key_grad, value_grad)


def body(
    hidden_in,
    attn_gain,
    ffn_gain,
    query_weight,
    key_weight,
    value_weight,
    output_weight,
    gate_weight,
    up_weight,
    down_weight,
    prefix_len,
    out_grad,
):
    col_count = lax.axis_size("col")
    col_index = lax.axis_index("col")
    length = hidden_in.shape[1] * lax.axis_size("row")
    head_size = HEAD_DIM
    group = HEADS // KV_HEADS
    row_heads = query_weight.shape[1] // head_size
    row_kv = key_weight.shape[1] // head_size
    my_heads = row_heads // col_count
    q_width = row_heads * head_size
    kv_width = row_kv * head_size
    row_units = gate_weight.shape[1]
    share = row_units // col_count
    block = min(512, length)
    cosine, sine = rope_tables(length, head_size)
    qkv_weight = jnp.concatenate([query_weight, key_weight, value_weight], axis=1)
    unit_weight = jnp.concatenate([gate_weight, up_weight], axis=1)
    qkv_acc = jnp.zeros(qkv_weight.shape, jnp.float32)
    output_acc = jnp.zeros(output_weight.shape, jnp.float32)
    unit_acc = jnp.zeros(unit_weight.shape, jnp.float32)
    down_acc = jnp.zeros(down_weight.shape, jnp.float32)
    attn_gain_acc = jnp.zeros(attn_gain.shape, jnp.float32)
    ffn_gain_acc = jnp.zeros(ffn_gain.shape, jnp.float32)
    results = []
    in_grads = []

    def fold_heads(expanded):
        spread_out = lax.dynamic_update_slice_in_dim(
            jnp.zeros((length, row_heads, head_size), jnp.float32),
            expanded,
            col_index * my_heads,
            1,
        )
        return spread_out.reshape(length, row_kv, group, head_size).sum(axis=2)

    for batch_index in range(hidden_in.shape[0]):
        prefix_one = prefix_len[batch_index, 0]
        resid = hidden_in[batch_index].astype(jnp.float32)
        scale_one = lax.rsqrt(width_total(jnp.sum(resid * resid, axis=1)) / WIDTH + epsilon)[
            :, None
        ]
        normed_one = gather_tokens((resid * scale_one * attn_gain).astype(jnp.bfloat16))
        projected = lax.psum(
            jnp.dot(normed_one, qkv_weight, preferred_element_type=jnp.float32), "col"
        )
        query_all = projected[:, :q_width].reshape(length, row_heads, head_size)
        query_mine = lax.dynamic_slice_in_dim(query_all, col_index * my_heads, my_heads, 1)
        queries = rope(query_mine, cosine, sine).astype(jnp.bfloat16)
        keys = rope(
            projected[:, q_width : q_width + kv_width].reshape(length, row_kv, head_size),
            cosine,
            sine,
        ).astype(jnp.bfloat16)
        values = (
            projected[:, q_width + kv_width :]
            .reshape(length, row_kv, head_size)
            .astype(jnp.bfloat16)
        )
        keys_wide = lax.dynamic_slice_in_dim(
            jnp.repeat(keys, group, axis=1), col_index * my_heads, my_heads, 1
        )
        values_wide = lax.dynamic_slice_in_dim(
            jnp.repeat(values, group, axis=1), col_index * my_heads, my_heads, 1
        )
        attended, log_sums = attend(queries, keys_wide, values_wide, prefix_one, block)
        head_out = lax.all_gather(
            attended.astype(jnp.bfloat16).reshape(length, my_heads * head_size),
            "col",
            axis=1,
            tiled=True,
        )
        middle = resid + scatter_tokens(head_out, output_weight, False)
        scale_two = lax.rsqrt(width_total(jnp.sum(middle * middle, axis=1)) / WIDTH + epsilon)[
            :, None
        ]
        normed_two = gather_tokens((middle * scale_two * ffn_gain).astype(jnp.bfloat16))
        partial_units = jnp.dot(
            normed_two, unit_weight, preferred_element_type=jnp.float32
        ).reshape(length, 2, row_units)
        summed = lax.psum(partial_units.astype(jnp.bfloat16), "col").astype(jnp.float32)
        activated = (jax.nn.silu(summed[:, 0]) * summed[:, 1]).astype(jnp.bfloat16)
        gate_share = lax.dynamic_slice_in_dim(summed[:, 0], col_index * share, share, 1)
        up_share = lax.dynamic_slice_in_dim(summed[:, 1], col_index * share, share, 1)
        result = middle + scatter_tokens(activated, down_weight, False)
        results.append(result.astype(jnp.bfloat16))
        top_grad = out_grad[batch_index]
        top_rows = gather_tokens(top_grad)
        down_acc = down_acc + contract_rows(activated, top_rows)
        act_part = lax.dot_general(
            top_rows, down_weight, (((1,), (1,)), ((), ())), preferred_element_type=jnp.float32
        )
        act_share = lax.psum_scatter(
            act_part.astype(jnp.bfloat16), "col", scatter_dimension=1, tiled=True
        ).astype(jnp.float32)
        sigmoid = jax.nn.sigmoid(gate_share)
        gate_grad = act_share * up_share * sigmoid * (1.0 + gate_share * (1.0 - sigmoid))
        up_grad = act_share * gate_share * sigmoid
        unit_grads = lax.all_gather(
            jnp.stack([gate_grad, up_grad], axis=1).astype(jnp.bfloat16), "col", axis=2, tiled=True
        )
        unit_flat = unit_grads.reshape(length, 2 * row_units)
        unit_acc = unit_acc + contract_rows(normed_two, unit_flat)
        normed_grad = scatter_tokens(unit_flat, unit_weight, True)
        ffn_gain_acc = ffn_gain_acc + jnp.sum(normed_grad * middle * scale_two, axis=0)
        weighted = normed_grad * ffn_gain
        inner = width_total(jnp.sum(weighted * middle, axis=1))[:, None]
        middle_grad = (
            top_grad.astype(jnp.float32)
            + weighted * scale_two
            - middle * (scale_two * scale_two * scale_two) * inner / WIDTH
        )
        middle_rows = gather_tokens(middle_grad.astype(jnp.bfloat16))
        output_acc = output_acc + contract_rows(head_out, middle_rows)
        head_part = lax.dot_general(
            middle_rows, output_weight, (((1,), (1,)), ((), ())), preferred_element_type=jnp.float32
        )
        head_grad = lax.psum_scatter(
            head_part.astype(jnp.bfloat16), "col", scatter_dimension=1, tiled=True
        )
        grad_heads = head_grad.reshape(length, my_heads, head_size)
        query_grad, key_grad_wide, value_grad_wide = attend_back(
            queries, keys_wide, values_wide, grad_heads, log_sums, prefix_one, block
        )
        key_grad = rope_back(fold_heads(key_grad_wide), cosine, sine)
        value_grad = fold_heads(value_grad_wide)
        query_grad = rope_back(query_grad, cosine, sine)
        packed = jnp.concatenate([query_grad, key_grad, value_grad], axis=1)
        gathered = (
            lax.all_gather(packed.astype(jnp.bfloat16), "col", axis=1, tiled=True)
            .astype(packed.dtype)
            .reshape(length, col_count, my_heads + 2 * row_kv, head_size)
        )
        query_all_grad = gathered[:, :, :my_heads].reshape(length, q_width)
        key_all_grad = jnp.sum(gathered[:, :, my_heads : my_heads + row_kv], axis=1).reshape(
            length, kv_width
        )
        value_all_grad = jnp.sum(gathered[:, :, my_heads + row_kv :], axis=1).reshape(
            length, kv_width
        )
        proj_grad = jnp.concatenate([query_all_grad, key_all_grad, value_all_grad], axis=1).astype(
            jnp.bfloat16
        )
        qkv_acc = qkv_acc + contract_rows(normed_one, proj_grad)
        first_grad = scatter_tokens(proj_grad, qkv_weight, True)
        attn_gain_acc = attn_gain_acc + jnp.sum(first_grad * resid * scale_one, axis=0)
        weighted_one = first_grad * attn_gain
        inner_one = width_total(jnp.sum(weighted_one * resid, axis=1))[:, None]
        in_grads.append(
            middle_grad
            + weighted_one * scale_one
            - resid * (scale_one * scale_one * scale_one) * inner_one / WIDTH
        )
    qkv_sum, output_sum, unit_sum, down_sum = (
        lax.psum(qkv_acc.astype(jnp.bfloat16), "dp").astype(jnp.float32),
        lax.psum(output_acc.astype(jnp.bfloat16), "dp").astype(jnp.float32),
        lax.psum(unit_acc.astype(jnp.bfloat16), "dp").astype(jnp.float32),
        lax.psum(down_acc.astype(jnp.bfloat16), "dp").astype(jnp.float32),
    )
    gain_one, gain_two = lax.psum((attn_gain_acc, ffn_gain_acc), ("dp", "row"))
    return (
        jnp.stack(results),
        jnp.stack(in_grads),
        gain_one,
        gain_two,
        qkv_sum[:, :q_width],
        qkv_sum[:, q_width : q_width + kv_width],
        qkv_sum[:, q_width + kv_width :],
        output_sum,
        unit_sum[:, :row_units],
        unit_sum[:, row_units:],
        down_sum,
    )


def solution(mesh):
    return jax.shard_map(
        body,
        mesh=mesh,
        in_specs=(
            P(None, ("dp", "row"), "col"),
            P("col"),
            P("col"),
            P("col", "row"),
            P("col", "row"),
            P("col", "row"),
            P("row", "col"),
            P("col", "row"),
            P("col", "row"),
            P("row", "col"),
            P(None, "dp"),
            P(None, ("dp", "row"), "col"),
        ),
        out_specs=(
            P(None, ("dp", "row"), "col"),
            P(None, ("dp", "row"), "col"),
            P("col"),
            P("col"),
            P("col", "row"),
            P("col", "row"),
            P("col", "row"),
            P("row", "col"),
            P("col", "row"),
            P("col", "row"),
            P("row", "col"),
        ),
        check_vma=False,
    )
```

profile of v0, /device:TPU:0, one launch (start us, length us, event | category | flops | bytes accessed | tf_op | source)
XLA Modules:
  0.0 1596.5 jit_solution(7165157778319276072)
XLA Ops:
  18.7 45.2 %all-gather.23.cloned.1.call-done = bf16[1024,1024]{1,0:T(8,128)(2,1)} async-done(((bf16[256,1024]{1,0:T(8,128)(2,1)}), bf16[1024,1024]{1,0:T(8,128)(2,1)}) %all-gather.23.cloned.1.call-update) | async-done | bytes 2097168 | tf_op jit(solution)/shard_map/all_gather | solution.py:51
  70.4 40.3 %all-gather.17.cloned.1.call-done = bf16[1024,1024]{1,0:T(8,128)(2,1)} async-done(((bf16[256,1024]{1,0:T(8,128)(2,1)}), bf16[1024,1024]{1,0:T(8,128)(2,1)}) %all-gather.17.cloned.1.call-update) | async-done | bytes 2097168 | tf_op jit(solution)/shard_map/all_gather | solution.py:51
  120.6 34.4 %all-reduce.12.cloned.1.call-done = (f32[1024,1024]{1,0:T(8,128)}, f32[1024,1024]{1,0:T(8,128)}) async-done(((f32[1024,1024]{1,0:T(8,128)}, f32[1024,1024]{1,0:T(8,128)}), (f32[1024,1024]{1,0:T(8,128)}, f32[1024,1024]{1,0:T(8,128)})) %all-reduce.12.cloned.1.call-update) | async-done | bytes 8388624 | tf_op jit(solution)/shard_map/psum | solution.py:192
  186.0 18.3 %while.54 = (s32[]{:T(128)}, bf16[2,512,2,128]{3,1,2,0:T(8,128)(2,1)}, f32[2,2,512]{2,1,0:T(2,128)S(1)}, s32[2]{0:T(128)S(1)}, s32[]{:T(128)}, /*index=5*/bf16[1...) while((s32[]{:T(128)}, ...), condition=%wide.region_6.7_spmd, body=%wide.region_3.6_spmd.sunk | while | flops 550502912 | bytes 20748528 | solution.py:97
  213.2 18.3 %while.55 = (s32[]{:T(128)}, bf16[2,512,2,128]{3,1,2,0:T(8,128)(2,1)}, f32[2,2,512]{2,1,0:T(2,128)S(1)}, s32[2]{0:T(128)S(1)}, s32[]{:T(128)}, /*index=5*/bf16[1...) while((s32[]{:T(128)}, ...), condition=%wide.region_18.19_spmd, body=%wide.region_15.18_spmd.sunk | while | flops 550502912 | bytes 20748528 | solution.py:97
  248.7 43.9 %reduce-scatter.13.cloned.1.call-done = bf16[256,1024]{1,0:T(8,128)(2,1)} async-done(((bf16[1024,1024]{1,0:T(8,128)(2,1)}), bf16[256,1024]{1,0:T(8,128)(2,1)}) %reduce-scatter.13.cloned.1.call-update) | async-done | bytes 524304 | tf_op jit(solution)/shard_map/reduce_scatter | solution.py:62
  292.6 46.2 %reduce-scatter.17.cloned.1.call-done = bf16[256,1024]{1,0:T(8,128)(2,1)} async-done(((bf16[1024,1024]{1,0:T(8,128)(2,1)}), bf16[256,1024]{1,0:T(8,128)(2,1)}) %reduce-scatter.17.cloned.1.call-update) | async-done | bytes 524304 | tf_op jit(solution)/shard_map/reduce_scatter | solution.py:62
  357.1 35.0 %all-gather.27.cloned.1.call-done = bf16[1024,1024]{1,0:T(8,128)(2,1)} async-done(((bf16[256,1024]{1,0:T(8,128)(2,1)}), bf16[1024,1024]{1,0:T(8,128)(2,1)}) %all-gather.27.cloned.1.call-update) | async-done | bytes 2097168 | tf_op jit(solution)/shard_map/all_gather | solution.py:51
  415.3 23.5 %all-gather.21.cloned.1.call-done = bf16[1024,1024]{1,0:T(8,128)(2,1)} async-done(((bf16[256,1024]{1,0:T(8,128)(2,1)}), bf16[1024,1024]{1,0:T(8,128)(2,1)}) %all-gather.21.cloned.1.call-update) | async-done | bytes 2097168 | tf_op jit(solution)/shard_map/all_gather | solution.py:51
  468.3 17.3 %all-gather.41.cloned.1.call-done = bf16[1,1024,1024]{2,1,0:T(8,128)(2,1)} async-done(((bf16[1,256,1024]{2,1,0:T(8,128)(2,1)}), bf16[1,1024,1024]{2,1,0:T(8,128)(2,1)}) %all-gather.41.cloned.1.call-update) | async-done | bytes 2097168 | tf_op jit(solution)/shard_map/all_gather | solution.py:51
  495.1 37.3 %all-gather.43.cloned.1.call-done = bf16[1,1024,1024]{2,1,0:T(8,128)(2,1)} async-done(((bf16[1,256,1024]{2,1,0:T(8,128)(2,1)}), bf16[1,1024,1024]{2,1,0:T(8,128)(2,1)}) %all-gather.43.cloned.1.call-update) | async-done | bytes 2097168 | tf_op jit(solution)/shard_map/all_gather | solution.py:51
  542.1 52.1 %all-reduce.16.cloned.1.call-done = (bf16[1024,2,2048]{2,0,1:T(8,128)(2,1)}, bf16[1024,2,2048]{2,1,0:T(2,128)(2,1)}) async-done(((bf16[1024,2,2048]{2,0,1:T(8,128)(2,1)}, bf16[1024,2,2048]{2,1,0:T(2,128)(2,1)}), (bf16[1024,2,2048]{2,0,1:T(8,128)(2,1)}, bf16[1024,2,2048]{2,1,0:T(2,128)(2,1)})) %all-reduce.16.cloned.1.call-update) | async-done | bytes 16777232 | tf_op jit(solution)/shard_map/psum | solution.py:229
  594.2 17.1 %fusion.209 = (f32[1024,1,2048]{2,1,0:T(1,128)S(1)}, f32[1024,1,2048]{2,1,0:T(1,128)}) fusion(bf16[1024,2,2048]{2,1,0:T(2,128)(2,1)} %get-tuple-element.530), kind=kLoop, calls=%fused_computation.331 | loop fusion | bytes 33554432 | tf_op jit(solution)/shard_map/slice | solution.py:230
  668.7 16.7 %convolution_convert_fusion.5 = bf16[1024,1024]{1,0:T(8,128)(2,1)} fusion(bf16[1024,4096]{0,1:T(8,128)(2,1)} %bitcast.366, bf16[1024,4096]{1,0:T(8,128)(2,1)} %constant_dynamic-update-slice_fusion.3), kind=kOutput, calls=%fused_computation.187 | convolution fusion | flops 8590983168 | bytes 18874368 | tf_op jit(solution)/shard_map/dot_general | solution.py:63
  781.8 40.4 %reduce-scatter.19.cloned.1.call-done = bf16[256,1024]{1,0:T(8,128)(2,1)} async-done(((bf16[1024,1024]{1,0:T(8,128)(2,1)}), bf16[256,1024]{1,0:T(8,128)(2,1)}) %reduce-scatter.19.cloned.1.call-update) | async-done | bytes 524304 | tf_op jit(solution)/shard_map/reduce_scatter | solution.py:62
  822.2 45.9 %reduce-scatter.15.cloned.1.call-done = bf16[256,1024]{1,0:T(8,128)(2,1)} async-done(((bf16[1024,1024]{1,0:T(8,128)(2,1)}), bf16[256,1024]{1,0:T(8,128)(2,1)}) %reduce-scatter.15.cloned.1.call-update) | async-done | bytes 524304 | tf_op jit(solution)/shard_map/reduce_scatter | solution.py:62
  873.7 44.6 %all-gather.31.cloned.1.call-done = bf16[1024,1024]{1,0:T(8,128)(2,1)} async-done(((bf16[256,1024]{1,0:T(8,128)(2,1)}), bf16[1024,1024]{1,0:T(8,128)(2,1)}) %all-gather.31.cloned.1.call-update) | async-done | bytes 2097168 | tf_op jit(solution)/shard_map/all_gather | solution.py:51
  922.3 42.3 %all-gather.37.cloned.1.call-done = bf16[1024,1024]{1,0:T(8,128)(2,1)} async-done(((bf16[256,1024]{1,0:T(8,128)(2,1)}), bf16[1024,1024]{1,0:T(8,128)(2,1)}) %all-gather.37.cloned.1.call-update) | async-done | bytes 2097168 | tf_op jit(solution)/shard_map/all_gather | solution.py:51
  976.8 86.3 %while.56 = (s32[]{:T(128)}, f32[1024,2,128]{0,2,1:T(8,128)}, f32[1024,2,128]{0,2,1:T(8,128)}, f32[2,512,2,128]{1,0,3,2:T(2,128)}, s32[2]{0:T(128)S(1)}, /*index...) while((s32[]{:T(128)}, f32[1024,2,128]{0,2,1:T(8,128)}, ...), condition=%wide.region_31.32_spmd.clone, body=%wide.region_29.31_spmd.clone.sunk | while | flops 1358960128 | bytes 52971800 | solution.py:133
  1072.3 61.5 %while.57 = (s32[]{:T(128)}, f32[1024,2,128]{0,2,1:T(8,128)}, f32[1024,2,128]{0,2,1:T(8,128)S(1)}, f32[2,512,2,128]{3,1,0,2:T(8,128)}, s32[2]{0:T(128)S(1)}, /*i...) while((s32[]{:T(128)}, f32[1024,2,128]{0,2,1:T(8,128)}, ...), condition=%wide.region_46.47_spmd.clone, body=%wide.region_44.46_spmd.clone.sunk | while | flops 1358960128 | bytes 59263256 | solution.py:133
  1205.1 16.5 %fusion.220 = f32[1024,4096]{1,0:T(8,128)} fusion(bf16[1024,1024]{1,0:T(8,128)(2,1)} %all-gather.21.cloned.1.call-done, bf16[1024,4096]{0,1:T(8,128)(2,1)} %bitcast.367), kind=kOutput, calls=%fused_computation.342 | convolution fusion | flops 8589934592 | bytes 27262976 | tf_op jit(solution)/shard_map/dot_general | solution.py:55
  1221.6 17.8 %add_convert_fusion = bf16[1024,4096]{1,0:T(8,128)(2,1)} fusion(f32[1024,4096]{1,0:T(8,128)} %fusion.220, bf16[1024,1024]{1,0:T(8,128)(2,1)} %all-gather.27.cloned.1.call-done, bf16[1024,4096]{0,1:T(8,128)(2,1)} %bitcast.369), kind=kOutput, calls=%fused_computation.103 | convolution fusion | flops 8598323200 | bytes 35651584 | tf_op jit(solution)/shard_map/dot_general | solution.py:55
  1272.8 42.3 %all-reduce = (f32[1024]{0:T(1024)}, f32[1024]{0:T(1024)}) all-reduce(f32[1024]{0:T(1024)S(1)} %add.311, f32[1024]{0:T(1024)S(1)} %add.312), channel_id=1, replica_groups=mesh['dp'=4,'row'=4,'col'=2] {'dp','row'}, use_global_device_ids=true, to_apply=%region_56.57 | all-reduce | flops 2048 | bytes 16384 | tf_op jit(solution)/shard_map/psum | solution.py:308
  1319.2 248.0 %all-reduce.14.cloned.1.call-done = (bf16[1024,1024]{1,0:T(8,128)(2,1)}, bf16[512,1024]{1,0:T(8,128)(2,1)}, bf16[1024,4096]{1,0:T(8,128)(2,1)}, bf16[2048,1024]{1,0:T(8,128)(2,1)}) async-done(((bf16[1024,1024]{1,0:T(8,128)(2,1)}, bf16[512,1024]{1,0:T(8,128)(2,1)}, bf16[1024,4096]{1,0:T(8,128)(2,1)}, bf16[2048,1024]{1,0:T(8,128)(2,1)}), (bf16[1024,1024]{1,0:T(8,128)(2,1)}, bf16[512,1024]{1,0:T(8,128)(2,1)}, ...) | async-done | bytes 15728656 | tf_op jit(solution)/shard_map/psum | solution.py:303
  (499 shorter events, 657.4 us)
Async XLA Ops:
  15.2 95.5 %all-gather.17.cloned.1.call-start = ((), (), s32[]{:S(2)}) async-start(), calls=%async_computation.12 | async-start | bytes 2621440 | tf_op jit(solution)/shard_map/all_gather | solution.py:51
  15.9 139.1 %all-reduce.12.cloned.1.call-start = ((), (), s32[]{:S(2)}) async-start(), calls=%async_computation.38 | async-start | bytes 16777216 | tf_op jit(solution)/shard_map/psum | solution.py:192
  117.3 117.3 %all-gather.19.cloned.1.call-start = ((), (), s32[]{:S(2)}) async-start(), calls=%async_computation.13 | async-start | bytes 1572864 | tf_op jit(solution)/shard_map/all_gather | solution.py:215
  238.4 100.4 %reduce-scatter.17.cloned.1.call-start = ((), (), s32[]{:S(2)}) async-start(), calls=%async_computation.19 | async-start | bytes 2621440 | tf_op jit(solution)/shard_map/reduce_scatter | solution.py:62
  248.6 143.4 %all-gather.27.cloned.1.call-start = ((), (), s32[]{:S(2)}) async-start(), calls=%async_computation.20 | async-start | bytes 2621440 | tf_op jit(solution)/shard_map/all_gather | solution.py:51
  346.7 92.2 %all-gather.21.cloned.1.call-start = ((), (), s32[]{:S(2)}) async-start(), calls=%async_computation.15 | async-start | bytes 2621440 | tf_op jit(solution)/shard_map/all_gather | solution.py:51
  347.4 138.2 %all-gather.41.cloned.1.call-start = ((), (), s32[]{:S(2)}) async-start(), calls=%async_computation.36 | async-start | bytes 2621440 | tf_op jit(solution)/shard_map/all_gather | solution.py:51
  348.5 183.9 %all-gather.43.cloned.1.call-start = ((), (), s32[]{:S(2)}) async-start(), calls=%async_computation.37 | async-start | bytes 2621440 | tf_op jit(solution)/shard_map/all_gather | solution.py:51
  349.3 244.9 %all-reduce.16.cloned.1.call-start = ((), (), s32[]{:S(2)}) async-start(), calls=%async_computation.40 | async-start | bytes 33554432 | tf_op jit(solution)/shard_map/psum | solution.py:229
  468.1 158.1 %reduce-scatter.21.cloned.1.call-start = ((), (), s32[]{:S(2)}) async-start(), calls=%async_computation.22 | async-start | bytes 6291456 | tf_op jit(solution)/shard_map/reduce_scatter | solution.py:241
  495.0 152.7 %reduce-scatter.29.cloned.1.call-start = ((), (), s32[]{:S(2)}) async-start(), calls=%async_computation.29 | async-start | bytes 6291456 | tf_op jit(solution)/shard_map/reduce_scatter | solution.py:241
  541.8 114.7 %all-gather.29.cloned.1.call-start = ((), (), s32[]{:S(2)}) async-start(), calls=%async_computation.23 | async-start | bytes 12582912 | tf_op jit(solution)/shard_map/all_gather | solution.py:247
  656.5 103.9 %reduce-scatter.23.cloned.1.call-start = ((), (), s32[]{:S(2)}) async-start(), calls=%async_computation.24 | async-start | bytes 2621440 | tf_op jit(solution)/shard_map/reduce_scatter | solution.py:62
  685.4 91.2 %reduce-scatter.31.cloned.1.call-start = ((), (), s32[]{:S(2)}) async-start(), calls=%async_computation.31 | async-start | bytes 2621440 | tf_op jit(solution)/shard_map/reduce_scatter | solution.py:62
  712.7 109.4 %reduce-scatter.19.cloned.1.call-start = ((), (), s32[]{:S(2)}) async-start(), calls=%async_computation.21 | async-start | bytes 2621440 | tf_op jit(solution)/shard_map/reduce_scatter | solution.py:62
  739.3 128.8 %reduce-scatter.15.cloned.1.call-start = ((), (), s32[]{:S(2)}) async-start(), calls=%async_computation.16 | async-start | bytes 2621440 | tf_op jit(solution)/shard_map/reduce_scatter | solution.py:62
  760.3 158.0 %all-gather.31.cloned.1.call-start = ((), (), s32[]{:S(2)}) async-start(), calls=%async_computation.25 | async-start | bytes 2621440 | tf_op jit(solution)/shard_map/all_gather | solution.py:51
  872.9 91.8 %all-gather.37.cloned.1.call-start = ((), (), s32[]{:S(2)}) async-start(), calls=%async_computation.32 | async-start | bytes 2621440 | tf_op jit(solution)/shard_map/all_gather | solution.py:51
  873.6 101.2 %reduce-scatter.25.cloned.1.call-start = ((), (), s32[]{:S(2)}) async-start(), calls=%async_computation.26 | async-start | bytes 1572864 | tf_op jit(solution)/shard_map/reduce_scatter | solution.py:266
  922.2 148.2 %reduce-scatter.33.cloned.1.call-start = ((), (), s32[]{:S(2)}) async-start(), calls=%async_computation.33 | async-start | bytes 1572864 | tf_op jit(solution)/shard_map/reduce_scatter | solution.py:266
  968.5 191.0 %all-gather.33.cloned.1.call-start = ((), (), s32[]{:S(2)}) async-start(), calls=%async_computation.27 | async-start | bytes 4718592 | tf_op jit(solution)/shard_map/all_gather | solution.py:278
  1149.5 104.2 %reduce-scatter.27.cloned.1.call-start = ((), (), s32[]{:S(2)}) async-start(), calls=%async_computation.28 | async-start | bytes 2621440 | tf_op jit(solution)/shard_map/reduce_scatter | solution.py:62
  1175.4 92.8 %reduce-scatter.35.cloned.1.call-start = ((), (), s32[]{:S(2)}) async-start(), calls=%async_computation.35 | async-start | bytes 2621440 | tf_op jit(solution)/shard_map/reduce_scatter | solution.py:62
  1205.1 362.0 %all-reduce.14.cloned.1.call-start = ((), (), s32[]{:S(2)}) async-start(), calls=%async_computation.39 | async-start | bytes 31457280 | tf_op jit(solution)/shard_map/psum | solution.py:303
  (104 other events, 1873.5 us)
Sparse Core Ops, SparseCore 0:
  15.3 48.5 all-gather.22
  66.0 44.6 all-gather.16
  117.4 37.6 all-reduce.11
  247.5 45.0 reduce-scatter.12
  295.6 43.1 reduce-scatter.16
  346.8 45.2 all-gather.26
  394.2 44.5 all-gather.20
  440.9 44.6 all-gather.40
  487.7 44.6 all-gather.42
  535.4 58.7 all-reduce.15
  596.6 13.2 reduce-scatter.20
  612.0 13.3 reduce-scatter.28
  633.8 21.0 all-gather.28
  656.6 21.0 all-gather.34
  685.6 45.0 reduce-scatter.22
  733.4 43.1 reduce-scatter.30
  779.0 43.1 reduce-scatter.18
  824.9 43.1 reduce-scatter.14
  873.0 45.2 all-gather.30
  919.9 44.6 all-gather.36
  1161.0 13.2 all-gather.38
  1177.1 45.0 reduce-scatter.26
  1225.0 43.1 reduce-scatter.34
  1273.8 293.2 all-reduce.13
  (5 shorter events, 50.3 us)
where the time goes:
time: 1600 us
  waiting for transfers between devices  853 us (53%)
  matrix products  307 us (19%)
  local copies, waits for them, and re-layouts  225 us (14%)
  other arithmetic  123 us (8%)
  blocking collectives  52.3 us (3%)
  loops' own time  16.4 us (1%)
    all_gather x8, waiting for transfers between devices, gather_tokens(): return lax.all_gather(shard_rows, 'row', axis=0, tiled=True)  286 us
    psum x1, waiting for transfers between devices, body(): lax.psum(qkv_acc.astype(jnp.bfloat16), 'dp').astype(jnp.float32)  248 us
    reduce_scatter x8, waiting for transfers between devices, scatter_tokens(): lax.psum_scatter(lax.dot_general(left_side, right_side, (contracted, ((),...  207 us
    dot_general x8, matrix products, scatter_tokens(): lax.dot_general(left_side, right_side, (contracted, ((), ())), preferred_...  61.9 us
    dot_general x8, matrix products, contract_rows(): lax.dot_general(left_side, right_side, (((0,), (0,)), ((), ())), preferre...  58 us
    psum x1, waiting for transfers between devices, body(): lax.psum(partial_units.astype(jnp.bfloat16), 'col').astype(jnp.float32)  52.1 us
    psum x1, blocking collectives, body(): gain_one, gain_two = lax.psum((attn_gain_acc, ffn_gain_acc), ('dp', 'row'))  42.3 us
    psum x1, waiting for transfers between devices, body(): lax.psum(jnp.dot(normed_one, qkv_weight, preferred_element_type=jnp.float...  34.4 us
  transfers between devices with their start and end apart: 29, of which 20 were waited for; matrix products, arithmetic and copies ran while one was open for 30% of the time, Pallas kernels for 0%

commit v1 on v0

v1 whole, which is shorter than its diff:
```python
import functools
import math

import jax
import jax.numpy as jnp
from jax import lax
from jax.experimental import pallas as pl
from jax.experimental.pallas import tpu as pltpu
from jax.sharding import PartitionSpec as P

WIDTH = 2048
HEADS = 16
KV_HEADS = 8
HEAD_DIM = 128
PREFIX_TOP = 512

epsilon = 1e-05
rope_base = 1000000.0
scale = 1.0 / math.sqrt(HEAD_DIM)
MIB = 1 << 20
F32 = jnp.float32
BF16 = jnp.bfloat16

NT = (((1,), (1,)), ((), ()))
NN = (((1,), (0,)), ((), ()))
TN = (((0,), (0,)), ((), ()))


def dot(left_side, right_side, dims):
    return lax.dot_general(left_side, right_side, dims, preferred_element_type=F32)


def params(mib, grid_rank):
    return pltpu.CompilerParams(
        dimension_semantics=("arbitrary",) * grid_rank, vmem_limit_bytes=mib * MIB
    )


def cost(flops, nbytes, exps=0):
    return pl.CostEstimate(flops=int(flops), bytes_accessed=int(nbytes), transcendentals=int(exps))


def whole(shape):
    return pl.BlockSpec(shape, lambda *_: (0,) * len(shape))


def rope_tables(length):
    half_size = HEAD_DIM // 2
    inverse = rope_base ** (-(jnp.arange(half_size, dtype=F32) * 2.0 / HEAD_DIM))
    angle = jnp.arange(length, dtype=F32)[:, None] * inverse[None, :]
    cosine = jnp.concatenate([jnp.cos(angle), jnp.cos(angle)], axis=1)
    signed = jnp.concatenate([-jnp.sin(angle), jnp.sin(angle)], axis=1)
    return cosine, signed


def rope(values, cosine, signed):
    return values * cosine + pltpu.roll(values, HEAD_DIM // 2, 1) * signed


def rope_back(values, cosine, signed):
    return values * cosine - pltpu.roll(values, HEAD_DIM // 2, 1) * signed


def attend_back_kernel(
    heads, block, prefix_ref, dz_own_ref, dz_oth_ref, wo_own_ref, wo_oth_ref, qkv_ref, log_ref,
    cos_ref, sin_ref, grad_ref, dk_ref, dv_ref, kt_ref,
):
    step = pl.program_id(0)
    length = qkv_ref.shape[0]
    count = length // block
    k_col, v_col = heads * HEAD_DIM, (heads + 1) * HEAD_DIM

    @pl.when(step == 0)
    def _():
        dk_ref[...] = jnp.zeros_like(dk_ref)
        dv_ref[...] = jnp.zeros_like(dv_ref)
        kt_ref[...] = qkv_ref[:, pl.ds(k_col, HEAD_DIM)].T

    for index in range(count):

        @pl.when(step == index)
        def _(index=index):
            first = index * block
            rows = pl.ds(first, block)
            extent = min(length, max(first + block, PREFIX_TOP))
            upto = pl.ds(0, extent)
            grads = dot(dz_own_ref[...], wo_own_ref[...], NT)
            grads = (grads + dot(dz_oth_ref[...], wo_oth_ref[...], NT)).astype(BF16)
            keys = qkv_ref[upto, pl.ds(k_col, HEAD_DIM)]
            values = qkv_ref[upto, pl.ds(v_col, HEAD_DIM)]
            key_at = lax.broadcasted_iota(jnp.int32, (extent, block), 0)
            query_at = lax.broadcasted_iota(jnp.int32, (extent, block), 1) + first
            allowed = (key_at <= query_at) | (key_at < prefix_ref[0])
            cosine, signed = cos_ref[rows, :], sin_ref[rows, :]
            for head in range(heads):
                cols = pl.ds(head * HEAD_DIM, HEAD_DIM)
                query = qkv_ref[rows, cols]
                grad = grads[:, head * HEAD_DIM : (head + 1) * HEAD_DIM]
                raw = dot(keys, query, NT) * scale - log_ref[pl.ds(head, 1), rows]
                probs = jnp.exp(jnp.where(allowed, raw, -1e30))
                dv_ref[upto, :] += dot(probs.astype(BF16), grad, NN)
                prob_grad = dot(values, grad, NT)
                inner = jnp.sum(probs * prob_grad, axis=0, keepdims=True)
                rounded = (probs * (prob_grad - inner) * scale).astype(BF16)
                dk_ref[upto, :] += dot(rounded, query, NN)
                dq = dot(kt_ref[:, upto], rounded, NN).T
                grad_ref[rows, cols] = rope_back(dq, cosine, signed).astype(BF16)

    @pl.when(step == count - 1)
    def _():
        dk = rope_back(dk_ref[...], cos_ref[...], sin_ref[...])
        grad_ref[:, pl.ds(k_col, HEAD_DIM)] = dk.astype(BF16)
        grad_ref[:, pl.ds(v_col, HEAD_DIM)] = dv_ref[...].astype(BF16)


def attend_back(prefix, dz_own, dz_oth, wo_own, wo_oth, qkv, logs, tables, heads):
    length, depth = dz_own.shape
    block = min(256, length)
    count = length // block
    rows_spec = pl.BlockSpec((block, depth), lambda i, p: (i, 0))
    return pl.pallas_call(
        functools.partial(attend_back_kernel, heads, block),
        grid_spec=pltpu.PrefetchScalarGridSpec(
            num_scalar_prefetch=1,
            grid=(count,),
            in_specs=[
                rows_spec, rows_spec, whole(wo_own.shape), whole(wo_oth.shape), whole(qkv.shape),
                whole(logs.shape), whole(tables[0].shape), whole(tables[1].shape),
            ],
            out_specs=whole(qkv.shape),
            scratch_shapes=[
                pltpu.VMEM((length, HEAD_DIM), F32),
                pltpu.VMEM((length, HEAD_DIM), F32),
                pltpu.VMEM((HEAD_DIM, length), BF16),
            ],
        ),
        out_shape=jax.ShapeDtypeStruct(qkv.shape, BF16),
        compiler_params=params(40, 1),
        cost_estimate=cost(
            4 * length * depth * wo_own.shape[0] + 20 * heads * length * length * HEAD_DIM,
            4 * length * depth,
            heads * length * length,
        ),
    )(prefix, dz_own, dz_oth, wo_own, wo_oth, qkv, logs, *tables)


def units_kernel(
    chunk, n_own, n_oth, g_own, g_oth, wg_own, wg_oth, wu_own, wu_oth, wd_own, wd_oth,
    act_ref, gate_ref, up_ref,
):
    @pl.loop(0, n_own.shape[0] // chunk)
    def _(index):
        rows = pl.ds(pl.multiple_of(index * chunk, chunk), chunk)
        gate = dot(n_own[rows, :], wg_own[...], NN) + dot(n_oth[rows, :], wg_oth[...], NN)
        up = dot(n_own[rows, :], wu_own[...], NN) + dot(n_oth[rows, :], wu_oth[...], NN)
        da = dot(g_own[rows, :], wd_own[...], NT) + dot(g_oth[rows, :], wd_oth[...], NT)
        sigmoid = 1.0 / (1.0 + jnp.exp(-gate))
        silu = gate * sigmoid
        act_ref[rows, :] = (silu * up).astype(BF16)
        gate_ref[rows, :] = (da * up * sigmoid * (1.0 + gate * (1.0 - sigmoid))).astype(BF16)
        up_ref[rows, :] = (da * silu).astype(BF16)


def units(n_own, n_oth, g_own, g_oth, wg_own, wg_oth, wu_own, wu_oth, wd_own, wd_oth):
    length, depth = n_own.shape
    share = wg_own.shape[1]
    block = min(256, share)
    chunk = min(256, length)
    col_spec = pl.BlockSpec((depth, block), lambda i: (0, i))
    row_spec = pl.BlockSpec((block, depth), lambda i: (i, 0))
    out_spec = pl.BlockSpec((length, block), lambda i: (0, i))
    return pl.pallas_call(
        functools.partial(units_kernel, chunk),
        grid=(share // block,),
        in_specs=[whole(n_own.shape)] * 4 + [col_spec] * 4 + [row_spec] * 2,
        out_specs=[out_spec] * 3,
        out_shape=[jax.ShapeDtypeStruct((length, share), BF16)] * 3,
        compiler_params=params(48, 1),
        cost_estimate=cost(
            12 * length * depth * share,
            8 * length * depth + 12 * depth * share + 6 * length * share,
            length * share,
        ),
    )(n_own, n_oth, g_own, g_oth, wg_own, wg_oth, wu_own, wu_oth, wd_own, wd_oth)


def sum_products_kernel(count, dims, *refs):
    total = dot(refs[0][...], refs[count][...], dims)
    for index in range(1, count):
        total = total + dot(refs[index][...], refs[count + index][...], dims)
    refs[-1][...] = total.astype(BF16)


def sum_products(lefts, rights, dims):
    rows = lefts[0].shape[0]
    columns = rights[0].shape[0 if dims is NT else 1]
    block = min(256, columns)
    if dims is NT:
        specs = [pl.BlockSpec((block, r.shape[1]), lambda i: (i, 0)) for r in rights]
    else:
        specs = [pl.BlockSpec((r.shape[0], block), lambda i: (0, i)) for r in rights]
    depth = sum(left.shape[1] for left in lefts)
    return pl.pallas_call(
        functools.partial(sum_products_kernel, len(lefts), dims),
        grid=(columns // block,),
        in_specs=[whole(left.shape) for left in lefts] + specs,
        out_specs=pl.BlockSpec((rows, block), lambda i: (0, i)),
        out_shape=jax.ShapeDtypeStruct((rows, columns), BF16),
        compiler_params=params(48, 1),
        cost_estimate=cost(
            2 * rows * depth * columns, 2 * (rows * depth + depth * columns + rows * columns)
        ),
    )(*lefts, *rights)


def grads_kernel(groups, batches, nb, shared_left, c_ref, *refs):
    shared = refs[:batches]
    outs = refs[batches + 2 * groups * batches :]
    part = pl.program_id(0) // nb
    for group in range(groups):
        for half in range(2):
            at = group * 2 + half

            @pl.when(part == at)
            def _(group=group, at=at):
                total = None
                for m in range(batches):
                    moving = refs[batches + at * batches + m][...]
                    pair = (shared[m][...], moving) if shared_left else (moving, shared[m][...])
                    term = dot(pair[0], pair[1], TN)
                    total = term if total is None else total + term
                outs[group][...] = total.astype(BF16)


def weight_grads(col_index, shared, groups, shared_left):
    batches = len(shared)
    tokens, shared_width = shared[0].shape
    half_width = groups[0][0][0].shape[1]
    block = min(256, half_width)
    nb = half_width // block
    steps = len(groups) * 2 * nb

    def moving_spec(at):
        return pl.BlockSpec((tokens, block), lambda i, c: (0, jnp.clip(i - at * nb, 0, nb - 1)))

    def out_spec(group):
        def place(i, c):
            inner = jnp.clip(i - group * 2 * nb, 0, 2 * nb - 1)
            half = inner // nb
            at = jnp.where(half == 0, c[0], 1 - c[0]) * nb + inner % nb
            return (0, at) if shared_left else (at, 0)

        shape = (shared_width, block) if shared_left else (block, shared_width)
        return pl.BlockSpec(shape, place)

    if shared_left:
        out_dims = (shared_width, 2 * half_width)
    else:
        out_dims = (2 * half_width, shared_width)
    moving = [x for group in groups for half in group for x in half]
    moving_specs = [moving_spec(at) for at in range(2 * len(groups)) for _ in range(batches)]
    return pl.pallas_call(
        functools.partial(grads_kernel, len(groups), batches, nb, shared_left),
        grid_spec=pltpu.PrefetchScalarGridSpec(
            num_scalar_prefetch=1,
            grid=(steps,),
            in_specs=[whole(s.shape) for s in shared] + moving_specs,
            out_specs=[out_spec(group) for group in range(len(groups))],
        ),
        out_shape=[jax.ShapeDtypeStruct(out_dims, BF16) for _ in groups],
        compiler_params=params(48, 1),
        cost_estimate=cost(
            4 * len(groups) * batches * tokens * shared_width * half_width,
            2 * batches * tokens * (shared_width + 2 * len(groups) * half_width),
        ),
    )(col_index.reshape(1), *shared, *moving)


class Line:
    def __init__(self, n):
        self.n = n
        self.r = lax.axis_index("row")
        self.c = lax.axis_index("col")

    def copy(self, src, dst, send, recv, **where):
        return pltpu.make_async_remote_copy(
            src_ref=src, dst_ref=dst, send_sem=send, recv_sem=recv, device_id=where,
            device_id_type=pl.DeviceIdType.MESH,
        )

    def up(self, src, dst, send, recv):
        return self.copy(src, dst, send, recv, row=self.r + 1)

    def down(self, src, dst, send, recv):
        return self.copy(src, dst, send, recv, row=self.r - 1)

    def across(self, src, dst, send, recv):
        return self.copy(src, dst, send, recv, col=1 - self.c)

    def barrier(self):
        barrier = pltpu.get_barrier_semaphore()

        def signal(**where):
            pl.semaphore_signal(
                barrier, inc=1, device_id=where, device_id_type=pl.DeviceIdType.MESH
            )

        @pl.when(self.r > 0)
        def _():
            signal(row=self.r - 1)

        @pl.when(self.r < self.n - 1)
        def _():
            signal(row=self.r + 1)

        signal(col=1 - self.c)

        at_end = (self.r == 0) | (self.r == self.n - 1)

        @pl.when(at_end)
        def _():
            pl.semaphore_wait(barrier, 2)

        @pl.when(jnp.logical_not(at_end))
        def _():
            pl.semaphore_wait(barrier, 3)

    def nearest(self, k):
        n = self.n
        code = 0
        for r in range(n):
            order = sorted(range(n), key=lambda q: (abs(q - r), q))
            code += order[k] * n**r
        place, result = self.r * 0 + code, 0
        for r in range(n):
            result = result + (place // n**r) % n * (1 - jnp.minimum(jnp.abs(self.r - r), 1))
        return result


class Gather:
    def __init__(self, line, own, oth, sends, recvs):
        self.line, self.own, self.oth, self.sends, self.recvs = line, own, oth, sends, recvs

    def hop(self, kind, q):
        way = (self.line.up, self.line.down)[kind]
        return way(self.own.at[q], self.own.at[q], self.sends.at[q, kind], self.recvs.at[q, 0])

    def cross(self, q):
        return self.line.across(
            self.own.at[q], self.oth.at[q], self.sends.at[q, 2], self.recvs.at[q, 1]
        )

    def start(self):
        line = self.line

        @pl.when(line.r < line.n - 1)
        def _():
            self.hop(0, line.r).start()

        @pl.when(line.r > 0)
        def _():
            self.hop(1, line.r).start()

        self.cross(line.r).start()

    def step(self, s):
        line = self.line
        low, high = line.r - s, line.r + s

        @pl.when(low >= 0)
        def _():
            self.hop(0, low).wait_recv()

            @pl.when(line.r < line.n - 1)
            def _():
                self.hop(0, low).start()

            self.cross(low).start()

        @pl.when(high <= line.n - 1)
        def _():
            self.hop(1, high).wait_recv()

            @pl.when(line.r > 0)
            def _():
                self.hop(1, high).start()

            self.cross(high).start()

    def arrive(self, q):
        self.cross(q).wait_recv()

    def drain(self):
        line = self.line
        for q in range(line.n):

            @pl.when((line.r >= q) & (line.r < line.n - 1))
            def _(q=q):
                self.hop(0, q).wait_send()

            @pl.when((line.r <= q) & (line.r > 0))
            def _(q=q):
                self.hop(1, q).wait_send()

            self.cross(q).wait_send()


class Scatter:
    def __init__(self, line, part, ups, downs, sends, recvs):
        self.line, self.part, self.ups, self.downs = line, part, ups, downs
        self.sends, self.recvs = sends, recvs

    def hop(self, kind, s, target):
        way = (self.line.up, self.line.down)[kind]
        box = (self.ups, self.downs)[kind]
        return way(
            self.part.at[target], box.at[s - 1], self.sends.at[kind, s - 1], self.recvs.at[kind, s - 1]
        )

    def step(self, s):
        line = self.line
        for kind in range(2):
            behind = line.r if kind == 0 else line.n - 1 - line.r
            target = line.r + line.n - s if kind == 0 else line.r - (line.n - s)
            box = (self.ups, self.downs)[kind]

            @pl.when(behind <= s - 1)
            def _(kind=kind, behind=behind, target=target, box=box):
                if s > 1:

                    @pl.when(behind >= 1)
                    def _():
                        self.hop(kind, s - 1, target).wait_recv()
                        self.part[target] = (
                            self.part[target].astype(F32) + box[s - 2].astype(F32)
                        ).astype(BF16)

                self.hop(kind, s, target).start()

    def total(self, out):
        line = self.line
        last = line.n - 1
        out[...] = self.part[line.r].astype(F32)

        @pl.when(line.r >= 1)
        def _():
            self.hop(0, last, line.r).wait_recv()
            out[...] += self.ups[last - 1].astype(F32)

        @pl.when(line.r <= last - 1)
        def _():
            self.hop(1, last, line.r).wait_recv()
            out[...] += self.downs[last - 1].astype(F32)

    def drain(self):
        line = self.line
        for s in range(1, line.n):

            @pl.when(line.r <= s - 1)
            def _(s=s):
                self.hop(0, s, line.r + line.n - s).wait_send()

            @pl.when(line.n - 1 - line.r <= s - 1)
            def _(s=s):
                self.hop(1, s, line.r - (line.n - s)).wait_send()


def communicate(number, mib):
    return pltpu.CompilerParams(
        collective_id=number, has_side_effects=True, vmem_limit_bytes=mib * MIB
    )


def forward_kernel(
    n, heads, shared_kv,
    prefix_ref, normed_ref, cos_ref, sin_ref, grad_in, wq, wk, wv, wo, wgate, wup, wdown,
    n1_out, g_own_out, g_oth_out, qkv_out, log_out, o_own_out, o_oth_out, sum_out,
    gate_from, up_from, down_from, wo_from,
    n1_own, n1_oth, g_own, g_oth, w_own, w_from, wo_ref, qkv_ref, vt_ref, o_own, o_oth, log_ref,
    part, ups, downs, total,
    gather_sends, gather_recvs, scatter_sends, scatter_recvs, cross_sends, cross_recvs, local_sems,
):
    batches, tokens, depth = normed_ref.shape
    length = n * tokens
    line = Line(n)
    r, c = line.r, line.c
    q_width = heads * HEAD_DIM
    k_col, v_col = q_width, q_width + HEAD_DIM
    share = wgate.shape[1] // 2
    kv_own = 0 if shared_kv else c * HEAD_DIM
    kv_oth = 0 if shared_kv else (1 - c) * HEAD_DIM

    def lanes(at, size):
        return pl.ds(pl.multiple_of(at, 128), size)

    local_count = [0]

    def local(src, dst):
        copy = pltpu.make_async_copy(src, dst, local_sems.at[local_count[0]])
        local_count[0] += 1
        copy.start()
        return copy

    cross_count = [0]

    def cross(src, dst):
        at = cross_count[0]
        cross_count[0] += 1
        return line.across(src, dst, cross_sends.at[at], cross_recvs.at[at])

    loads = [
        local(wq.at[:, lanes(c * q_width, q_width)], w_own.at[:, pl.ds(0, q_width)]),
        local(wk.at[:, lanes(kv_own, HEAD_DIM)], w_own.at[:, pl.ds(k_col, HEAD_DIM)]),
        local(wv.at[:, lanes(kv_own, HEAD_DIM)], w_own.at[:, pl.ds(v_col, HEAD_DIM)]),
    ]
    wo_load = local(wo, wo_ref)
    g_loads = [local(grad_in.at[m], g_own.at[m, r]) for m in range(batches)]
    n1_own[0, r] = normed_ref[0]
    n1_own[1, r] = normed_ref[1]
    line.barrier()

    n1 = [
        Gather(line, n1_own.at[m], n1_oth.at[m], gather_sends.at[m], gather_recvs.at[m])
        for m in range(batches)
    ]
    g = [
        Gather(
            line, g_own.at[m], g_oth.at[m], gather_sends.at[batches + m], gather_recvs.at[batches + m]
        )
        for m in range(batches)
    ]
    rs = [
        Scatter(line, part.at[m], ups.at[m], downs.at[m], scatter_sends.at[m], scatter_recvs.at[m])
        for m in range(batches)
    ]
    n1[0].start()
    w_cross = [
        cross(wq.at[:, lanes((1 - c) * q_width, q_width)], w_from.at[:, pl.ds(0, q_width)]),
        cross(wk.at[:, lanes(kv_oth, HEAD_DIM)], w_from.at[:, pl.ds(k_col, HEAD_DIM)]),
        cross(wv.at[:, lanes(kv_oth, HEAD_DIM)], w_from.at[:, pl.ds(v_col, HEAD_DIM)]),
    ]
    for copy in w_cross:
        copy.start()
    for copy in loads:
        copy.wait()
    for copy in w_cross:
        copy.wait_recv()

    def project(m, q):
        n1[m].arrive(q)
        rows = pl.ds(pl.multiple_of(q * tokens, tokens), tokens)
        pre = dot(n1_own[m, q], w_own[...], NN) + dot(n1_oth[m, q], w_from[...], NN)
        cosine, signed = cos_ref[rows, :], sin_ref[rows, :]
        for head in range(heads + 1):
            piece = pre[:, head * HEAD_DIM : (head + 1) * HEAD_DIM]
            qkv_ref[m, rows, pl.ds(head * HEAD_DIM, HEAD_DIM)] = rope(piece, cosine, signed).astype(BF16)
        values = pre[:, v_col : v_col + HEAD_DIM].astype(BF16)
        qkv_ref[m, rows, pl.ds(v_col, HEAD_DIM)] = values
        vt_ref[m, :, rows] = values.T

    block = min(256, length)
    count = length // block

    def attend_block(m, index):
        first = index * block
        extent = min(length, max(first + block, PREFIX_TOP))
        keys = qkv_ref[m, pl.ds(0, extent), pl.ds(k_col, HEAD_DIM)]
        key_at = lax.broadcasted_iota(jnp.int32, (extent, block), 0)
        query_at = lax.broadcasted_iota(jnp.int32, (extent, block), 1) + first
        allowed = (key_at <= query_at) | (key_at < prefix_ref[m, 0])
        for head in range(heads):
            cols = pl.ds(head * HEAD_DIM, HEAD_DIM)
            query = qkv_ref[m, pl.ds(first, block), cols]
            scores = jnp.where(allowed, dot(keys, query, NT) * scale, -1e30)
            topmost = jnp.max(scores, axis=0, keepdims=True)
            exponent = jnp.exp(scores - topmost)
            summed = jnp.sum(exponent, axis=0, keepdims=True)
            weights = (exponent * (1.0 / summed)).astype(BF16)
            result = dot(vt_ref[m, :, pl.ds(0, extent)], weights, NN)
            o_own[m, pl.ds(first, block), cols] = result.T.astype(BF16)
            log_ref[m, pl.ds(head, 1), pl.ds(first, block)] = topmost + jnp.log(summed)

    def project_out(m):
        @pl.loop(0, n)
        def _(p):
            rows = pl.ds(pl.multiple_of(p * tokens, tokens), tokens)
            own_rows = pl.ds(pl.multiple_of(c * q_width, q_width), q_width)
            oth_rows = pl.ds(pl.multiple_of((1 - c) * q_width, q_width), q_width)
            value = dot(o_own[m, rows, :], wo_ref[own_rows, :], NN)
            value = value + dot(o_oth[m, rows, :], wo_ref[oth_rows, :], NN)
            part[m, p] = value.astype(BF16)

    def walk(item, m, first, last):
        for k in range(first, last):
            item.step(k)
            project(m, line.nearest(k))

    project(0, r)
    walk(n1[0], 0, 1, n - 1)
    n1[1].start()
    walk(n1[0], 0, n - 1, n)
    project(1, r)
    half = (n + 1) // 2
    for index in range(count // 2):
        attend_block(0, index)
    walk(n1[1], 1, 1, half)
    for index in range(count // 2, count):
        attend_block(0, index)
    o_cross = [cross(o_own.at[m], o_oth.at[m]) for m in range(batches)]
    o_cross[0].start()
    walk(n1[1], 1, half, n - 1)
    o_cross[0].wait_recv()
    wo_load.wait()
    project_out(0)
    rs[0].step(1)
    g_loads[0].wait()
    g[0].start()
    walk(n1[1], 1, n - 1, n)
    for s in range(2, half + 1):
        rs[0].step(s)
    for index in range(count // 2):
        attend_block(1, index)
    for s in range(half + 1, n):
        rs[0].step(s)
    for k in range(1, half):
        g[0].step(k)
    for index in range(count // 2, count):
        attend_block(1, index)
    o_cross[1].start()
    for k in range(half, n - 1):
        g[0].step(k)
    o_cross[1].wait_recv()
    project_out(1)
    rs[1].step(1)
    g_loads[1].wait()
    g[1].start()
    rs[0].total(total.at[0])
    big_cross = [
        cross(wgate.at[:, lanes((1 - c) * share, share)], gate_from),
        cross(wup.at[:, lanes((1 - c) * share, share)], up_from),
        cross(wdown.at[pl.ds(pl.multiple_of((1 - c) * share, share), share), :], down_from),
        cross(wo.at[pl.ds(pl.multiple_of((1 - c) * q_width, q_width), q_width), :], wo_from),
    ]
    for copy in big_cross:
        copy.start()
    stores = [
        local(n1_own, n1_out), local(qkv_ref, qkv_out), local(log_ref, log_out),
        local(o_own, o_own_out), local(o_oth, o_oth_out), local(total.at[0], sum_out.at[0]),
    ]
    g[0].step(n - 1)
    for s in range(2, n):
        g[1].step(s - 1)
        rs[1].step(s)
    rs[1].total(total.at[1])
    stores.append(local(total.at[1], sum_out.at[1]))
    g[1].step(n - 1)
    for m in range(batches):
        for q in range(n):
            g[m].arrive(q)
    stores += [local(g_own, g_own_out), local(g_oth, g_oth_out)]
    for copy in big_cross:
        copy.wait_recv()
    for copy in big_cross + w_cross + o_cross:
        copy.wait_send()
    for item in n1 + g + rs:
        item.drain()
    for copy in stores:
        copy.wait()


def forward(prefix, normed, tables, grad_in, wq, wk, wv, wo, wgate, wup, wdown, n, heads, shared_kv):
    batches, tokens, depth = normed.shape
    length = n * tokens
    width = (heads + 2) * HEAD_DIM
    q_width = heads * HEAD_DIM
    share = wgate.shape[1] // 2
    vmem = pl.BlockSpec(memory_space=pltpu.VMEM)
    anywhere = pl.BlockSpec(memory_space=pl.ANY)
    gathered = (batches, n, tokens, depth)
    shapes = [
        (gathered, BF16), (gathered, BF16), (gathered, BF16),
        ((batches, length, width), BF16), ((batches, 8, length), F32),
        ((batches, length, q_width), BF16), ((batches, length, q_width), BF16),
        ((batches, tokens, depth), F32),
        ((depth, share), BF16), ((depth, share), BF16), ((share, depth), BF16), ((q_width, depth), BF16),
    ]
    boxes = (batches, n - 1, tokens, depth)
    return pl.pallas_call(
        functools.partial(forward_kernel, n, heads, shared_kv),
        in_specs=[pl.BlockSpec(memory_space=pltpu.SMEM), vmem, vmem, vmem] + [anywhere] * 8,
        out_specs=[anywhere] * len(shapes),
        out_shape=[jax.ShapeDtypeStruct(*item) for item in shapes],
        scratch_shapes=[
            pltpu.VMEM(gathered, BF16), pltpu.VMEM(gathered, BF16),
            pltpu.VMEM(gathered, BF16), pltpu.VMEM(gathered, BF16),
            pltpu.VMEM((depth, width), BF16), pltpu.VMEM((depth, width), BF16),
            pltpu.VMEM(wo.shape, BF16), pltpu.VMEM((batches, length, width), BF16),
            pltpu.VMEM((batches, HEAD_DIM, length), BF16),
            pltpu.VMEM((batches, length, q_width), BF16), pltpu.VMEM((batches, length, q_width), BF16),
            pltpu.VMEM((batches, 8, length), F32),
            pltpu.VMEM(gathered, BF16), pltpu.VMEM(boxes, BF16), pltpu.VMEM(boxes, BF16),
            pltpu.VMEM((batches, tokens, depth), F32),
            pltpu.SemaphoreType.DMA((2 * batches, n, 3)), pltpu.SemaphoreType.DMA((2 * batches, n, 2)),
            pltpu.SemaphoreType.DMA((batches, 2, n - 1)), pltpu.SemaphoreType.DMA((batches, 2, n - 1)),
            pltpu.SemaphoreType.DMA((9,)), pltpu.SemaphoreType.DMA((9,)),
            pltpu.SemaphoreType.DMA((16,)),
        ],
        compiler_params=communicate(1, 56),
        cost_estimate=cost(
            batches * (4 * length * depth * width + 8 * heads * length * length * HEAD_DIM),
            40 * MIB,
        ),
    )(prefix, normed, *tables, grad_in, wq, wk, wv, wo, wgate, wup, wdown)


def other_core(values):
    count = lax.axis_size("col")
    return lax.ppermute(values, "col", [(i, (i + 1) % count) for i in range(count)])


def place_kernel(n, row_ref, *refs):
    pieces, out, sems = refs[: 2 * n - 1], refs[2 * n - 1], refs[2 * n]
    size = pieces[0].shape[0]
    for row in range(n):

        @pl.when(row_ref[0] == row)
        def _(row=row):
            copies = [
                pltpu.make_async_copy(
                    pieces[at - row + n - 1], out.at[pl.ds(at * size, size)], sems.at[at]
                )
                for at in range(n)
            ]
            for copy in copies:
                copy.start()
            for copy in copies:
                copy.wait()


def place(row_index, pieces):
    n = (len(pieces) + 1) // 2
    size, width = pieces[0].shape
    return pl.pallas_call(
        functools.partial(place_kernel, n),
        in_specs=[pl.BlockSpec(memory_space=pltpu.SMEM)]
        + [pl.BlockSpec(memory_space=pl.ANY)] * len(pieces),
        out_specs=pl.BlockSpec(memory_space=pltpu.VMEM),
        out_shape=jax.ShapeDtypeStruct((n * size, width), pieces[0].dtype),
        scratch_shapes=[pltpu.SemaphoreType.DMA((n,))],
        cost_estimate=cost(0, 4 * n * size * width),
    )(row_index.reshape(1), *pieces)


def row_gather(row_index, shard):
    n = lax.axis_size("row")
    below, above = [shard], [shard]
    for step in range(1, n):
        below.append(lax.ppermute(below[-1], "row", [(i, i + 1) for i in range(step - 1, n - 1)]))
        above.append(lax.ppermute(above[-1], "row", [(i, i - 1) for i in range(1, n - step + 1)]))
    return place(row_index, below[:0:-1] + above)


def row_scatter(row_index, partial_sums):
    n = lax.axis_size("row")
    width = partial_sums.shape[1]
    pieces = partial_sums.reshape(n, -1, width)

    def piece(at):
        return lax.dynamic_index_in_dim(pieces, jnp.clip(at, 0, n - 1), 0, keepdims=False).astype(F32)

    up = down = None
    for step in range(1, n):
        far = n - step
        send_up, send_down = piece(row_index + far), piece(row_index - far)
        if up is not None:
            send_up, send_down = send_up + up.astype(F32), send_down + down.astype(F32)
        up = lax.ppermute(send_up.astype(BF16), "row", [(i, i + 1) for i in range(step)])
        down = lax.ppermute(send_down.astype(BF16), "row", [(i, i - 1) for i in range(n - step, n)])
    total = piece(row_index)
    if up is not None:
        total = total + up.astype(F32) + down.astype(F32)
    return total


def butterfly(values, axes):
    for axis in axes:
        n = lax.axis_size(axis)
        reach = 1
        while reach < n:
            values = values + lax.ppermute(values, axis, [(i, i ^ reach) for i in range(n)])
            reach *= 2
    return values


def after(values, *earlier):
    return lax.optimization_barrier((values, *earlier))[0]


def body(
    hidden_in,
    attn_gain,
    ffn_gain,
    query_weight,
    key_weight,
    value_weight,
    output_weight,
    gate_weight,
    up_weight,
    down_weight,
    prefix_len,
    out_grad,
):
    col_count, row_count = lax.axis_size("col"), lax.axis_size("row")
    col_index = lax.axis_index("col").astype(jnp.int32)
    row_index = lax.axis_index("row").astype(jnp.int32)
    batches, tokens, _ = hidden_in.shape
    length = tokens * row_count
    heads = query_weight.shape[1] // HEAD_DIM // col_count
    row_kv = key_weight.shape[1] // HEAD_DIM
    shared_kv = row_kv < col_count
    q_width = heads * HEAD_DIM
    share = gate_weight.shape[1] // col_count
    tables = rope_tables(length)

    def parts(weight, axis, size, fixed=False):
        if fixed:
            return weight, weight
        own = lax.dynamic_slice_in_dim(weight, col_index * size, size, axis)
        oth = lax.dynamic_slice_in_dim(weight, (1 - col_index) * size, size, axis)
        return own, oth

    q_own, q_oth = parts(query_weight, 1, q_width)
    k_own, k_oth = parts(key_weight, 1, HEAD_DIM, shared_kv)
    v_own, v_oth = parts(value_weight, 1, HEAD_DIM, shared_kv)
    qkv_own = jnp.concatenate([q_own, k_own, v_own], axis=1)
    qkv_oth = jnp.concatenate([q_oth, k_oth, v_oth], axis=1)
    out_own, out_oth = parts(output_weight, 0, q_width)
    gate_own, gate_oth = parts(gate_weight, 1, share)
    up_own, up_oth = parts(up_weight, 1, share)
    down_own, down_oth = parts(down_weight, 0, share)

    resid = hidden_in.astype(F32)
    squares = jnp.sum(resid * resid, axis=2)
    scale_one = lax.rsqrt((squares + other_core(squares)) / WIDTH + epsilon)[..., None]
    normed = (resid * scale_one * attn_gain).astype(BF16)
    (
        n1_all, g_own, g_oth, qkv, logs, o_own, o_oth, attn_sum, gate_from, up_from, down_from, out_from,
    ) = forward(
        prefix_len, normed, tables, out_grad, query_weight, key_weight, value_weight, output_weight,
        gate_weight, up_weight, down_weight, row_count, heads, shared_kv,
    )
    flat = (batches, length, -1)
    n1_all, g_own, g_oth = (item.reshape(flat) for item in (n1_all, g_own, g_oth))
    n1 = [(n1_all[m], None) for m in range(batches)]
    g = [(g_own[m], g_oth[m]) for m in range(batches)]
    heads_out = [(o_own[m], o_oth[m]) for m in range(batches)]
    kept = [(qkv[m], logs[m]) for m in range(batches)]

    mids, scales, n2 = [], [], []
    for m in range(batches):
        middle = resid[m] + attn_sum[m]
        squares = jnp.sum(middle * middle, axis=1)
        scale_two = lax.rsqrt((squares + other_core(squares)) / WIDTH + epsilon)[:, None]
        gathered = row_gather(row_index, (middle * scale_two * ffn_gain).astype(BF16))
        mids.append(middle)
        scales.append(scale_two)
        n2.append((gathered, other_core(gathered)))

    acts, dgates, dups = [], [], []
    for m in range(batches):
        act, dgate, dup = units(
            *n2[m], *g[m], gate_own, gate_from, up_own, up_from, down_own, down_from
        )
        acts.append((act, other_core(act)))
        dgates.append((dgate, other_core(dgate)))
        dups.append((dup, other_core(dup)))

    def halves(pairs):
        return [[pair[side] for pair in pairs] for side in range(2)]

    (down_grad,) = weight_grads(col_index, [pair[0] for pair in g], [halves(acts)], False)
    gate_grad, up_grad = weight_grads(
        col_index, [pair[0] for pair in n2], [halves(dgates), halves(dups)], True
    )
    down_sum = lax.psum(down_grad, "dp")
    gate_grad, up_grad = lax.optimization_barrier((gate_grad, up_grad, down_sum))[:2]
    gate_sum, up_sum = lax.psum((gate_grad, up_grad), "dp")

    results, middle_grads, dz = [], [], []
    ffn_gain_acc = jnp.zeros(ffn_gain.shape, F32)
    for m in range(batches):
        normed_grad = row_scatter(
            row_index,
            sum_products(
                [dgates[m][0], dgates[m][1], dups[m][0], dups[m][1]],
                [gate_own, gate_oth, up_own, up_oth],
                NT,
            ),
        )
        ffn_gain_acc = ffn_gain_acc + jnp.sum(normed_grad * mids[m] * scales[m], axis=0)
        weighted = normed_grad * ffn_gain
        inner = jnp.sum(weighted * mids[m], axis=1)
        inner = (inner + other_core(inner))[:, None]
        middle_grad = (
            out_grad[m].astype(F32)
            + weighted * scales[m]
            - mids[m] * (scales[m] * scales[m] * scales[m]) * inner / WIDTH
        )
        middle_grads.append(middle_grad)
        gathered = row_gather(row_index, middle_grad.astype(BF16))
        dz.append((gathered, other_core(gathered)))
        result = mids[m] + row_scatter(row_index, sum_products(list(acts[m]), [down_own, down_oth], NN))
        results.append(result.astype(BF16))

    in_grads, dqkv = [], []
    attn_gain_acc = jnp.zeros(attn_gain.shape, F32)
    for m in range(batches):
        grad = attend_back(
            prefix_len[m], *dz[m], out_own, out_from, *kept[m], tables, heads
        )
        dqkv.append((grad, other_core(grad)))
        first_grad = row_scatter(
            row_index, sum_products(list(dqkv[m]), [qkv_own, qkv_oth], NT)
        )
        attn_gain_acc = attn_gain_acc + jnp.sum(first_grad * resid[m] * scale_one[m], axis=0)
        weighted = first_grad * attn_gain
        inner = jnp.sum(weighted * resid[m], axis=1)
        inner = (inner + other_core(inner))[:, None]
        s = scale_one[m]
        in_grads.append(middle_grads[m] + weighted * s - resid[m] * (s * s * s) * inner / WIDTH)

    (output_grad,) = weight_grads(col_index, [pair[0] for pair in dz], [halves(heads_out)], False)
    (qkv_grad,) = weight_grads(col_index, [pair[0] for pair in n1], [halves(dqkv)], True)
    output_grad, qkv_grad = lax.optimization_barrier((output_grad, qkv_grad, gate_sum, up_sum))[:2]
    output_sum, qkv_sum = lax.psum((output_grad, qkv_grad), "dp")
    both = qkv_sum.astype(F32).reshape(-1, col_count, q_width + 2 * HEAD_DIM)

    def columns(first, size, shared):
        piece = both[:, :, first : first + size]
        return piece.sum(axis=1) if shared else piece.reshape(-1, col_count * size)

    gain_one, gain_two = butterfly(jnp.stack([attn_gain_acc, ffn_gain_acc]), ("dp", "row"))
    return (
        jnp.stack(results),
        jnp.stack(in_grads),
        gain_one,
        gain_two,
        columns(0, q_width, False),
        columns(q_width, HEAD_DIM, shared_kv),
        columns(q_width + HEAD_DIM, HEAD_DIM, shared_kv),
        output_sum.astype(F32),
        gate_sum.astype(F32),
        up_sum.astype(F32),
        down_sum.astype(F32),
    )


def solution(mesh):
    return jax.shard_map(
        body,
        mesh=mesh,
        in_specs=(
            P(None, ("dp", "row"), "col"),
            P("col"),
            P("col"),
            P("col", "row"),
            P("col", "row"),
            P("col", "row"),
            P("row", "col"),
            P("col", "row"),
            P("col", "row"),
            P("row", "col"),
            P(None, "dp"),
            P(None, ("dp", "row"), "col"),
        ),
        out_specs=(
            P(None, ("dp", "row"), "col"),
            P(None, ("dp", "row"), "col"),
            P("col"),
            P("col"),
            P("col", "row"),
            P("col", "row"),
            P("col", "row"),
            P("row", "col"),
            P("col", "row"),
            P("col", "row"),
            P("row", "col"),
        ),
        check_vma=False,
    )
```

time: 1600 us -> 962 us (0.60)
  waiting for transfers between devices: 853 us -> 292 us
  Pallas kernels: 0 us -> 384 us
  matrix products: 307 us -> 0 us
  local copies, waits for them, and re-layouts: 225 us -> 56.8 us
  starting transfers between devices: 3.61 us -> 142 us
  other arithmetic: 123 us -> 65.7 us
  blocking collectives: 52.3 us -> 0 us
  loops' own time: 16.4 us -> 0 us
    pallas_call x0 -> x19, Pallas kernels: none -> 384 us  [the longest x1 196 us: forward(): pl.pallas_call(functools.partial(forward_kernel, n, heads, shared_kv), in...]
    dot_general x52 -> x0, matrix products: 307 us -> none  [the longest x8 61.9 us: scatter_tokens(): lax.dot_general(left_side, right_side, (contracted, ((), ())), preferred_...]
    all_gather x14 -> x0, waiting for transfers between devices: 302 us -> none  [the longest x8 286 us: gather_tokens(): return lax.all_gather(shard_rows, 'row', axis=0, tiled=True)]
    psum x3, waiting for transfers between devices: 335 us -> 46.3 us  [the longest x1 22 us: body(): output_sum, qkv_sum = lax.psum((output_grad, qkv_grad), 'dp')]
    ppermute x0 -> x83, waiting for transfers between devices: none -> 246 us  [the longest x12 99.8 us: row_gather(): lax.ppermute(above[-1], 'row', [(i, i - 1) for i in range(1, n - step + 1)])]
    reduce_scatter x12 -> x0, waiting for transfers between devices: 213 us -> none  [the longest x8 207 us: scatter_tokens(): lax.psum_scatter(lax.dot_general(left_side, right_side, (contracted, ((),...]
    ppermute x0 -> x83, starting transfers between devices: none -> 142 us  [the longest x18 62.3 us: row_scatter(): lax.ppermute(send_up.astype(BF16), 'row', [(i, i + 1) for i in range(step)])]
    psum x5 -> x0, blocking collectives: 52.3 us -> none  [the longest x1 42.3 us: body(): gain_one, gain_two = lax.psum((attn_gain_acc, ffn_gain_acc), ('dp', 'row'))]
  transfers between devices with their start and end apart: 29 -> 86, of which waited for: 20 -> 43; matrix products, arithmetic and copies ran while one was open for 30% -> 9% of each run, Pallas kernels for 0% -> 14%
where the time goes in v1:
time: 962 us; the launch traced here: 957 us
  Pallas kernels  384 us (40%)
  waiting for transfers between devices  292 us (30%)
  starting transfers between devices  142 us (15%)
  other arithmetic  65.7 us (7%)
  local copies, waits for them, and re-layouts  56.8 us (6%)
  between operations  15.8 us (2%)
    pallas_call x1, Pallas kernels, forward(): pl.pallas_call(functools.partial(forward_kernel, n, heads, shared_kv), in...  196 us
    ppermute x12, waiting for transfers between devices, row_gather(): lax.ppermute(above[-1], 'row', [(i, i - 1) for i in range(1, n - step + 1)])  99.8 us
    ppermute x18, waiting for transfers between devices, row_scatter(): lax.ppermute(send_up.astype(BF16), 'row', [(i, i + 1) for i in range(step)])  72.4 us
    ppermute x18, starting transfers between devices, row_scatter(): lax.ppermute(send_up.astype(BF16), 'row', [(i, i + 1) for i in range(step)])  62.3 us
    pallas_call x4, Pallas kernels, weight_grads(): pl.pallas_call(functools.partial(grads_kernel, len(groups), batches, nb,...  55.6 us
    pallas_call x6, Pallas kernels, sum_products(): pl.pallas_call(functools.partial(sum_products_kernel, len(lefts), dims),...  52.6 us
    pallas_call x2, Pallas kernels, units(): pl.pallas_call(functools.partial(units_kernel, chunk), grid=(share // blo...  44.4 us
    ppermute x12, starting transfers between devices, row_gather(): lax.ppermute(below[-1], 'row', [(i, i + 1) for i in range(step - 1, n - 1)])  31.4 us
  transfers between devices with their start and end apart: 86, of which 43 were waited for; matrix products, arithmetic and copies ran while one was open for 9% of the time, Pallas kernels for 14%

profile of v1, /device:TPU:0, one launch (start us, length us, event | category | flops | bytes accessed | tf_op | source)
XLA Modules:
  0.0 957.0 jit_solution(12674709752056813827)
XLA Ops:
  15.3 196.0 %shard_map.203 = (bf16[2,4,256,1024]{3,2,1,0:T(8,128)(2,1)}, bf16[2,4,256,1024]{3,2,1,0:T(8,128)(2,1)}, bf16[2,4,256,1024]{3,2,1,0:T(8,128)(2,1)}, bf16[2,1024,5...) custom-call(s32[2,1]{1,0:T(2,128)} %copy.23.prefix_ref, ...), custom_call_target="tpu_custom_call" | custom-call | flops 8589934592 | bytes 41943040 | tf_op jit(solution)/shard_map/pallas_call | solution.py:688
  219.3 10.3 %collective-permute-done.2.refs_2_ = bf16[256,1024]{1,0:T(8,128)(2,1)S(1)} collective-permute-done((bf16[256,1024]{1,0:T(8,128)(2,1)S(1)}, bf16[256,1024]{1,0:T(8,128)(2,1)S(1)}, u32[]{:S(2)}, u32[]{:S(2)}) %collective-permute-start.2) | collective-permute-done | bytes 524320 | tf_op jit(solution)/shard_map/ppermute | solution.py:758
  236.6 12.2 %collective-permute-done.6.refs_5_ = bf16[256,1024]{1,0:T(8,128)(2,1)} collective-permute-done((bf16[256,1024]{1,0:T(8,128)(2,1)S(1)}, bf16[256,1024]{1,0:T(8,128)(2,1)}, u32[]{:S(2)}, u32[]{:S(2)}) %collective-permute-start.6) | collective-permute-done | bytes 524320 | tf_op jit(solution)/shard_map/ppermute | solution.py:759
  250.1 13.0 %collective-permute-done.7.refs_6_ = bf16[256,1024]{1,0:T(8,128)(2,1)} collective-permute-done((bf16[256,1024]{1,0:T(8,128)(2,1)}, bf16[256,1024]{1,0:T(8,128)(2,1)}, u32[]{:S(2)}, u32[]{:S(2)}) %collective-permute-start.7) | collective-permute-done | bytes 524320 | tf_op jit(solution)/shard_map/ppermute | solution.py:759
  284.6 22.1 %shard_map.205 = (bf16[1024,1024]{1,0:T(8,128)(2,1)}, bf16[1024,1024]{1,0:T(8,128)(2,1)S(1)}, bf16[1024,1024]{1,0:T(8,128)(2,1)}) custom-call(bf16[1024,1024]{1,0:T(8,128)(2,1)} %shard_map.204.n_own.refs_0_, bf16[1024,1024]{1,0:T(8,128)(2,1)} %copy-done.78, bf16[1024,1024]{1,0:T(8,128)(2,1)} %bitcast.254, bf16[1024,1024]{1,0:T(8,128)(2,1)} %bitcast.277, ...), custom_call_target="tpu_custom_call" | custom-call | flops 12884901888 | bytes 27262976 | tf_op jit(solution)/shard_map/pallas_call | solution.py:172
  315.9 13.4 %shard_map.210 = bf16[1024,1024]{1,0:T(8,128)(2,1)S(1)} custom-call(bf16[1024,1024]{1,0:T(8,128)(2,1)S(1)} %copy-done.15, bf16[1024,1024]{1,0:T(8,128)(2,1)} %collective-permute-done.31.refs_1_.refs_4_, bf16[1024,1024]{1,0:T(8,128)(2,1)} %get-tuple-element.44.refs_2_.refs_6_, bf16[1024,1024]{1,0:T(8,128)(2,1)} %collective-permute-done.32.refs_3_.refs_8_, ...), custom_call_target="tpu_custom_call" | custom-call | flops 8589934592 | bytes 18874368 | tf_op jit(solution)/shard_map/pallas_call | solution.py:203
  400.7 9.1 collective-permute-done.12
  443.9 11.3 %collective-permute-done.21.refs_5_ = bf16[256,1024]{1,0:T(8,128)(2,1)S(1)} collective-permute-done((bf16[256,1024]{1,0:T(8,128)(2,1)S(1)}, bf16[256,1024]{1,0:T(8,128)(2,1)S(1)}, u32[]{:S(2)}, u32[]{:S(2)}) %collective-permute-start.21) | collective-permute-done | bytes 524320 | tf_op jit(solution)/shard_map/ppermute | solution.py:759
  457.3 10.4 %collective-permute-done.22.refs_6_ = bf16[256,1024]{1,0:T(8,128)(2,1)} collective-permute-done((bf16[256,1024]{1,0:T(8,128)(2,1)S(1)}, bf16[256,1024]{1,0:T(8,128)(2,1)}, u32[]{:S(2)}, u32[]{:S(2)}) %collective-permute-start.22) | collective-permute-done | bytes 524320 | tf_op jit(solution)/shard_map/ppermute | solution.py:759
  476.4 22.3 %shard_map.208 = (bf16[1024,1024]{1,0:T(8,128)(2,1)S(1)}, bf16[1024,1024]{1,0:T(8,128)(2,1)S(1)}, bf16[1024,1024]{1,0:T(8,128)(2,1)}) custom-call(bf16[1024,1024]{1,0:T(8,128)(2,1)} %shard_map.207.n_own.refs_1_, bf16[1024,1024]{1,0:T(8,128)(2,1)} %copy-done.79, bf16[1024,1024]{1,0:T(8,128)(2,1)} %bitcast.256, bf16[1024,1024]{1,0:T(8,128)(2,1)} %bitcast.274, ...), custom_call_target="tpu_custom_call" | custom-call | flops 12884901888 | bytes 27262976 | tf_op jit(solution)/shard_map/pallas_call | solution.py:172
  510.2 13.4 %shard_map.214 = bf16[1024,1024]{1,0:T(8,128)(2,1)S(1)} custom-call(bf16[1024,1024]{1,0:T(8,128)(2,1)S(1)} %get-tuple-element.48.refs_0_.refs_3_, bf16[1024,1024]{1,0:T(8,128)(2,1)} %copy-done.76, bf16[1024,1024]{1,0:T(8,128)(2,1)} %get-tuple-element.49.refs_2_.refs_7_, bf16[1024,1024]{1,0:T(8,128)(2,1)} %copy-done.77, ...), custom_call_target="tpu_custom_call" | custom-call | flops 8589934592 | bytes 18874368 | tf_op jit(solution)/shard_map/pallas_call | solution.py:203
  556.0 13.3 %shard_map.221 = bf16[2048,1024]{1,0:T(8,128)(2,1)} custom-call(s32[1]{0:T(128)} %bitcast.75.c_ref, bf16[1024,1024]{1,0:T(8,128)(2,1)S(1)} %bitcast.255, bf16[1024,1024]{1,0:T(8,128)(2,1)S(1)} %bitcast.257, bf16[1024,1024]{1,0:T(8,128)(2,1)} %get-tuple-element.41.refs_0_.refs_2_, bf16[1024,1024]{1,0:T(8,128)(2,1)} %copy-done.17, ...), custom_call_target="tpu_custom_call" | custom-call | flops 8589934592 | bytes 12582912 | tf_op jit(solution)/shard_map/pallas_call | solution.py:262
  591.8 9.8 %collective-permute-done.27 = bf16[256,1024]{1,0:T(8,128)(2,1)S(1)} collective-permute-done((bf16[256,1024]{1,0:T(8,128)(2,1)S(1)}, bf16[256,1024]{1,0:T(8,128)(2,1)S(1)}, u32[]{:S(2)}, u32[]{:S(2)}) %collective-permute-start.27) | collective-permute-done | bytes 524320 | tf_op jit(solution)/shard_map/ppermute | solution.py:777
  616.7 11.5 %collective-permute-start.40 = (bf16[256,1024]{1,0:T(8,128)(2,1)}, bf16[256,1024]{1,0:T(8,128)(2,1)S(1)}, u32[]{:S(2)}, u32[]{:S(2)}) collective-permute-start(bf16[256,1024]{1,0:T(8,128)(2,1)} %get-tuple-element.75.refs_3_), channel_id=1, source_target_pairs={{0,2},{2,4},{4,6},{1,3},{3,5},{5,7},{8,10},{10,12},{12,14},{9,11},... | collective-permute-start | bytes 1572872 | tf_op jit(solution)/shard_map/ppermute | solution.py:758
  629.5 27.5 %shard_map.220 = (bf16[1024,2048]{1,0:T(8,128)(2,1)}, bf16[1024,2048]{1,0:T(8,128)(2,1)}) custom-call(s32[1]{0:T(128)} %bitcast.75.c_ref, bf16[1024,1024]{1,0:T(8,128)(2,1)S(1)} %copy-done.6, bf16[1024,1024]{1,0:T(8,128)(2,1)S(1)} %copy-done.7, bf16[1024,1024]{1,0:T(8,128)(2,1)} %copy-done.14, bf16[1024,1024]{1,0:T(8,128)(2,1)} %copy-done.16, ...), custom_call_target="tpu_custom_call" | custom-call | flops 17179869184 | bytes 20971520 | tf_op jit(solution)/shard_map/pallas_call | solution.py:262
  657.0 14.6 %all-reduce.6.cloned.1.call-done = bf16[2048,1024]{1,0:T(8,128)(2,1)} async-done(((bf16[2048,1024]{1,0:T(8,128)(2,1)}), bf16[2048,1024]{1,0:T(8,128)(2,1)}) %all-reduce.6.cloned.1.call-update) | async-done | bytes 4194320 | tf_op jit(solution)/shard_map/psum | solution.py:885
  704.8 9.2 collective-permute-done.45.refs_6_
  725.5 13.5 %collective-permute-done.69.refs_6_ = bf16[256,1024]{1,0:T(8,128)(2,1)S(1)} collective-permute-done((bf16[256,1024]{1,0:T(8,128)(2,1)S(1)}, bf16[256,1024]{1,0:T(8,128)(2,1)S(1)}, u32[]{:S(2)}, u32[]{:S(2)}) %collective-permute-start.69) | collective-permute-done | bytes 524320 | tf_op jit(solution)/shard_map/ppermute | solution.py:759
  746.1 11.4 %shard_map.212.refs_0_.refs_2_ = bf16[1024,512]{1,0:T(8,128)(2,1)S(1)} custom-call(s32[1]{0:T(128)} %bitcast.36.prefix_ref, bf16[1024,1024]{1,0:T(8,128)(2,1)S(1)} %copy-done.8, bf16[1024,1024]{1,0:T(8,128)(2,1)} %collective-permute-done.46.dz_oth_ref, bf16[256,1024]{1,0:T(8,128)(2,1)S(1)} %constant_dynamic-slice_fusion.6.wo_own_ref, ...), custom_call_target="tpu_custom_call" | custom-call | flops 6442450944 | bytes 4194304 | tf_op jit(solution)/shard_map/pallas_call | solution.py:121
  758.3 12.5 %shard_map.216.refs_0_.refs_3_ = bf16[1024,512]{1,0:T(8,128)(2,1)} custom-call(s32[1]{0:T(128)} %bitcast.58.prefix_ref, bf16[1024,1024]{1,0:T(8,128)(2,1)S(1)} %copy-done.9, bf16[1024,1024]{1,0:T(8,128)(2,1)} %collective-permute-done.70.dz_oth_ref, bf16[256,1024]{1,0:T(8,128)(2,1)S(1)} %constant_dynamic-slice_fusion.6.wo_own_ref, ...), custom_call_target="tpu_custom_call" | custom-call | flops 6442450944 | bytes 4194304 | tf_op jit(solution)/shard_map/pallas_call | solution.py:121
  830.0 9.5 shard_map.219
  839.5 9.6 %all-reduce.10.cloned.1.call-done = (bf16[1024,2048]{1,0:T(8,128)(2,1)}, bf16[1024,2048]{1,0:T(8,128)(2,1)}) async-done(((bf16[1024,2048]{1,0:T(8,128)(2,1)}, bf16[1024,2048]{1,0:T(8,128)(2,1)}), (bf16[1024,2048]{1,0:T(8,128)(2,1)}, bf16[1024,2048]{1,0:T(8,128)(2,1)})) %all-reduce.10.cloned.1.call-update) | async-done | bytes 8388624 | tf_op jit(solution)/shard_map/psum | solution.py:887
  870.5 10.1 %collective-permute-done.74 = bf16[256,1024]{1,0:T(8,128)(2,1)S(1)} collective-permute-done((bf16[256,1024]{1,0:T(8,128)(2,1)S(1)}, bf16[256,1024]{1,0:T(8,128)(2,1)S(1)}, u32[]{:S(2)}, u32[]{:S(2)}) %collective-permute-start.74) | collective-permute-done | bytes 524320 | tf_op jit(solution)/shard_map/ppermute | solution.py:777
  920.0 22.0 %all-reduce.8.cloned.1.call-done = (bf16[1024,2,512]{2,1,0:T(2,128)(2,1)}, bf16[512,1024]{1,0:T(8,128)(2,1)}) async-done(((bf16[1024,2,512]{2,1,0:T(2,128)(2,1)}, bf16[512,1024]{1,0:T(8,128)(2,1)}), (bf16[1024,2,512]{2,1,0:T(2,128)(2,1)}, bf16[512,1024]{1,0:T(8,128)(2,1)})) %all-reduce.8.cloned.1.call-update) | async-done | bytes 3145744 | tf_op jit(solution)/shard_map/psum | solution.py:935
  (412 shorter events, 433.3 us)
Async XLA Ops:
  7.2 664.5 %all-reduce.6.cloned.1.call-start = ((), (), s32[]{:S(2)}) async-start(), calls=%async_computation | async-start | bytes 8388608 | tf_op jit(solution)/shard_map/psum | solution.py:885
  308.5 24.3 %collective-permute-start.9 = (bf16[1024,1024]{1,0:T(8,128)(2,1)}, bf16[1024,1024]{1,0:T(8,128)(2,1)}, u32[]{:S(2)}, u32[]{:S(2)}) collective-permute-start(bf16[1024,1024]{1,0:T(8,128)(2,1)} %get-tuple-element.41.refs_0_.refs_2_), channel_id=1, source_target_pairs={{0,1},{1,0},{2,3},{3,2},{4,5},{5,4},{6,7},{7,6},{8,9},{9,8},{10,11... | collective-permute-start | bytes 6291464 | tf_op jit(solution)/shard_map/ppermute | solution.py:718
  398.2 22.6 %collective-permute-start.15 = (bf16[256,1024]{1,0:T(8,128)(2,1)}, bf16[256,1024]{1,0:T(8,128)(2,1)}, u32[]{:S(2)}, u32[]{:S(2)}) collective-permute-start(bf16[256,1024]{1,0:T(8,128)(2,1)} %fusion.30), channel_id=1, source_target_pairs={{2,0},{4,2},{6,4},{3,1},{5,3},{7,5},{10,8},{12,10},{14,12},{11,9},... | collective-permute-start | bytes 1572872 | tf_op jit(solution)/shard_map/ppermute | solution.py:778
  499.3 26.7 %collective-permute-start.24 = (bf16[1024,1024]{1,0:T(8,128)(2,1)S(1)}, bf16[1024,1024]{1,0:T(8,128)(2,1)}, u32[]{:S(2)}, u32[]{:S(2)}) collective-permute-start(bf16[1024,1024]{1,0:T(8,128)(2,1)S(1)} %get-tuple-element.42.refs_0_.refs_3_), channel_id=1, source_target_pairs={{0,1},{1,0},{2,3},{3,2},{4,5},{5,4},{6,7},{7,6},{8,9},{9,8},{10,11... | collective-permute-start | bytes 6291464 | tf_op jit(solution)/shard_map/ppermute | solution.py:718
  535.9 33.5 %collective-permute-start.60 = (bf16[256,1024]{1,0:T(8,128)(2,1)}, bf16[256,1024]{1,0:T(8,128)(2,1)}, u32[]{:S(2)}, u32[]{:S(2)}) collective-permute-start(bf16[256,1024]{1,0:T(8,128)(2,1)} %get-tuple-element.120), channel_id=1, source_target_pairs={{6,4},{7,5},{14,12},{15,13},{22,20},{23,21},{30,28},{31,29}} | collective-permute-start | bytes 1572872 | tf_op jit(solution)/shard_map/ppermute | solution.py:778
  537.3 35.0 %collective-permute-start.28 = (bf16[256,1024]{1,0:T(8,128)(2,1)}, bf16[256,1024]{1,0:T(8,128)(2,1)}, u32[]{:S(2)}, u32[]{:S(2)}) collective-permute-start(bf16[256,1024]{1,0:T(8,128)(2,1)} %get-tuple-element.128), channel_id=1, source_target_pairs={{6,4},{7,5},{14,12},{15,13},{22,20},{23,21},{30,28},{31,29}} | collective-permute-start | bytes 1572872 | tf_op jit(solution)/shard_map/ppermute | solution.py:778
  539.8 29.6 %collective-permute-start.58 = (bf16[256,1024]{1,0:T(8,128)(2,1)}, bf16[256,1024]{1,0:T(8,128)(2,1)}, u32[]{:S(2)}, u32[]{:S(2)}) collective-permute-start(bf16[256,1024]{1,0:T(8,128)(2,1)} %fusion.7), channel_id=1, source_target_pairs={{0,2},{2,4},{1,3},{3,5},{8,10},{10,12},{9,11},{11,13},{16,18},{18,... | collective-permute-start | bytes 1572872 | tf_op jit(solution)/shard_map/ppermute | solution.py:777
  569.3 279.8 %all-reduce.10.cloned.1.call-start = ((), (), s32[]{:S(2)}) async-start(), calls=%async_computation.2 | async-start | bytes 16777216 | tf_op jit(solution)/shard_map/psum | solution.py:887
  579.5 22.1 %collective-permute-start.27 = (bf16[256,1024]{1,0:T(8,128)(2,1)S(1)}, bf16[256,1024]{1,0:T(8,128)(2,1)S(1)}, u32[]{:S(2)}, u32[]{:S(2)}) collective-permute-start(bf16[256,1024]{1,0:T(8,128)(2,1)S(1)} %get-tuple-element.125), channel_id=1, source_target_pairs={{0,2},{2,4},{4,6},{1,3},{3,5},{5,7},{8,10},{10,12},{12,14},{9,11},... | collective-permute-start | bytes 1572872 | tf_op jit(solution)/shard_map/ppermute | solution.py:777
  585.8 24.4 %collective-permute-start.30 = (bf16[256,1024]{1,0:T(8,128)(2,1)S(1)}, bf16[256,1024]{1,0:T(8,128)(2,1)S(1)}, u32[]{:S(2)}, u32[]{:S(2)}) collective-permute-start(bf16[256,1024]{1,0:T(8,128)(2,1)S(1)} %fusion.23), channel_id=1, source_target_pairs={{2,0},{4,2},{6,4},{3,1},{5,3},{7,5},{10,8},{12,10},{14,12},{11,9},... | collective-permute-start | bytes 1572872 | tf_op jit(solution)/shard_map/ppermute | solution.py:778
  587.1 24.5 %collective-permute-start.39 = (f32[256]{0:T(256)S(1)}, f32[256]{0:T(256)S(1)}, u32[]{:S(2)}, u32[]{:S(2)}) collective-permute-start(f32[256]{0:T(256)S(1)} %get-tuple-element.66), channel_id=1, source_target_pairs={{0,1},{1,0},{2,3},{3,2},{4,5},{5,4},{6,7},{7,6},{8,9},{9,8},{10,11... | collective-permute-start | bytes 3080 | tf_op jit(solution)/shard_map/ppermute | solution.py:718
  616.7 55.0 %collective-permute-start.40 = (bf16[256,1024]{1,0:T(8,128)(2,1)}, bf16[256,1024]{1,0:T(8,128)(2,1)S(1)}, u32[]{:S(2)}, u32[]{:S(2)}) collective-permute-start(bf16[256,1024]{1,0:T(8,128)(2,1)} %get-tuple-element.75.refs_3_), channel_id=1, source_target_pairs={{0,2},{2,4},{4,6},{1,3},{3,5},{5,7},{8,10},{10,12},{12,14},{9,11},... | collective-permute-start | bytes 1572872 | tf_op jit(solution)/shard_map/ppermute | solution.py:758
  628.2 44.3 %collective-permute-start.43 = (bf16[256,1024]{1,0:T(8,128)(2,1)}, bf16[256,1024]{1,0:T(8,128)(2,1)S(1)}, u32[]{:S(2)}, u32[]{:S(2)}) collective-permute-start(bf16[256,1024]{1,0:T(8,128)(2,1)} %get-tuple-element.75.refs_3_), channel_id=1, source_target_pairs={{2,0},{4,2},{6,4},{3,1},{5,3},{7,5},{10,8},{12,10},{14,12},{11,9},... | collective-permute-start | bytes 1572872 | tf_op jit(solution)/shard_map/ppermute | solution.py:759
  671.7 270.3 %all-reduce.8.cloned.1.call-start = ((), (), s32[]{:S(2)}) async-start(), calls=%async_computation.1 | async-start | bytes 6291456 | tf_op jit(solution)/shard_map/psum | solution.py:935
  680.7 22.0 %collective-permute-start.67 = (bf16[256,1024]{1,0:T(8,128)(2,1)S(1)}, bf16[256,1024]{1,0:T(8,128)(2,1)S(1)}, u32[]{:S(2)}, u32[]{:S(2)}) collective-permute-start(bf16[256,1024]{1,0:T(8,128)(2,1)S(1)} %copy-done.37), channel_id=1, source_target_pairs={{2,0},{4,2},{6,4},{3,1},{5,3},{7,5},{10,8},{12,10},{14,12},{11,9},... | collective-permute-start | bytes 1572872 | tf_op jit(solution)/shard_map/ppermute | solution.py:759
  691.5 22.6 %collective-permute-start.45 = (bf16[256,1024]{1,0:T(8,128)(2,1)S(1)}, bf16[256,1024]{1,0:T(8,128)(2,1)}, u32[]{:S(2)}, u32[]{:S(2)}) collective-permute-start(bf16[256,1024]{1,0:T(8,128)(2,1)S(1)} %collective-permute-done.44.refs_5_), channel_id=1, source_target_pairs={{2,0},{3,1},{10,8},{11,9},{18,16},{19,17},{26,24},{27,25}} | collective-permute-start | bytes 1572872 | tf_op jit(solution)/shard_map/ppermute | solution.py:759
  692.8 24.3 %collective-permute-start.65 = (bf16[256,1024]{1,0:T(8,128)(2,1)S(1)}, bf16[256,1024]{1,0:T(8,128)(2,1)}, u32[]{:S(2)}, u32[]{:S(2)}) collective-permute-start(bf16[256,1024]{1,0:T(8,128)(2,1)S(1)} %collective-permute-done.64.refs_2_), channel_id=1, source_target_pairs={{2,4},{4,6},{3,5},{5,7},{10,12},{12,14},{11,13},{13,15},{18,20},{2... | collective-permute-start | bytes 1572872 | tf_op jit(solution)/shard_map/ppermute | solution.py:758
  717.0 28.3 %collective-permute-start.46 = (bf16[1024,1024]{1,0:T(8,128)(2,1)}, bf16[1024,1024]{1,0:T(8,128)(2,1)}, u32[]{:S(2)}, u32[]{:S(2)}) collective-permute-start(bf16[1024,1024]{1,0:T(8,128)(2,1)} %shard_map.211.dz_own_ref.refs_0_), channel_id=1, source_target_pairs={{0,1},{1,0},{2,3},{3,2},{4,5},{5,4},{6,7},{7,6},{8,9},{9,8},{10,11... | collective-permute-start | bytes 6291464 | tf_op jit(solution)/shard_map/ppermute | solution.py:718
  792.6 22.7 %collective-permute-start.51 = (bf16[256,1024]{1,0:T(8,128)(2,1)}, bf16[256,1024]{1,0:T(8,128)(2,1)S(1)}, u32[]{:S(2)}, u32[]{:S(2)}) collective-permute-start(bf16[256,1024]{1,0:T(8,128)(2,1)} %get-tuple-element.112), channel_id=1, source_target_pairs={{6,4},{7,5},{14,12},{15,13},{22,20},{23,21},{30,28},{31,29}} | collective-permute-start | bytes 1572872 | tf_op jit(solution)/shard_map/ppermute | solution.py:778
  793.4 25.9 %collective-permute-start.75 = (bf16[256,1024]{1,0:T(8,128)(2,1)S(1)}, bf16[256,1024]{1,0:T(8,128)(2,1)S(1)}, u32[]{:S(2)}, u32[]{:S(2)}) collective-permute-start(bf16[256,1024]{1,0:T(8,128)(2,1)S(1)} %get-tuple-element.106), channel_id=1, source_target_pairs={{6,4},{7,5},{14,12},{15,13},{22,20},{23,21},{30,28},{31,29}} | collective-permute-start | bytes 1572872 | tf_op jit(solution)/shard_map/ppermute | solution.py:778
  817.8 43.8 %collective-permute-start.52 = (bf16[256,1024]{1,0:T(8,128)(2,1)}, bf16[256,1024]{1,0:T(8,128)(2,1)}, u32[]{:S(2)}, u32[]{:S(2)}) collective-permute-start(bf16[256,1024]{1,0:T(8,128)(2,1)} %get-tuple-element.110), channel_id=1, source_target_pairs={{4,2},{6,4},{5,3},{7,5},{12,10},{14,12},{13,11},{15,13},{20,18},{2... | collective-permute-start | bytes 1572872 | tf_op jit(solution)/shard_map/ppermute | solution.py:778
  828.5 35.6 %collective-permute-start.76 = (bf16[256,1024]{1,0:T(8,128)(2,1)}, bf16[256,1024]{1,0:T(8,128)(2,1)}, u32[]{:S(2)}, u32[]{:S(2)}) collective-permute-start(bf16[256,1024]{1,0:T(8,128)(2,1)} %get-tuple-element.104), channel_id=1, source_target_pairs={{4,2},{6,4},{5,3},{7,5},{12,10},{14,12},{13,11},{15,13},{20,18},{2... | collective-permute-start | bytes 1572872 | tf_op jit(solution)/shard_map/ppermute | solution.py:778
  858.2 22.4 %collective-permute-start.74 = (bf16[256,1024]{1,0:T(8,128)(2,1)S(1)}, bf16[256,1024]{1,0:T(8,128)(2,1)S(1)}, u32[]{:S(2)}, u32[]{:S(2)}) collective-permute-start(bf16[256,1024]{1,0:T(8,128)(2,1)S(1)} %copy-done.67), channel_id=1, source_target_pairs={{0,2},{2,4},{4,6},{1,3},{3,5},{5,7},{8,10},{10,12},{12,14},{9,11},... | collective-permute-start | bytes 1572872 | tf_op jit(solution)/shard_map/ppermute | solution.py:777
  865.6 23.5 %collective-permute-start.77 = (bf16[256,1024]{1,0:T(8,128)(2,1)S(1)}, bf16[256,1024]{1,0:T(8,128)(2,1)S(1)}, u32[]{:S(2)}, u32[]{:S(2)}) collective-permute-start(bf16[256,1024]{1,0:T(8,128)(2,1)S(1)} %fusion.1), channel_id=1, source_target_pairs={{2,0},{4,2},{6,4},{3,1},{5,3},{7,5},{10,8},{12,10},{14,12},{11,9},... | collective-permute-start | bytes 1572872 | tf_op jit(solution)/shard_map/ppermute | solution.py:778
  (142 other events, 1939.8 us)
Sparse Core Ops, SparseCore 0:
  569.4 102.1 all-reduce.5
  676.4 172.6 all-reduce.9
  853.8 88.1 all-reduce.7

commit v2 on v1

v2 whole, which is shorter than its diff:
```python
import functools
import math

import jax
import jax.numpy as jnp
from jax import lax
from jax.experimental import pallas as pl
from jax.experimental.pallas import tpu as pltpu
from jax.sharding import PartitionSpec as P

WIDTH = 2048
HEADS = 16
KV_HEADS = 8
HEAD_DIM = 128
PREFIX_TOP = 512

epsilon = 1e-05
rope_base = 1000000.0
scale = 1.0 / math.sqrt(HEAD_DIM)
MIB = 1 << 20
F32 = jnp.float32
BF16 = jnp.bfloat16

NT = (((1,), (1,)), ((), ()))
NN = (((1,), (0,)), ((), ()))
TN = (((0,), (0,)), ((), ()))


def dot(left_side, right_side, dims):
    return lax.dot_general(left_side, right_side, dims, preferred_element_type=F32)


def params(mib, grid_rank):
    return pltpu.CompilerParams(
        dimension_semantics=("arbitrary",) * grid_rank, vmem_limit_bytes=mib * MIB
    )


def cost(flops, nbytes, exps=0):
    return pl.CostEstimate(flops=int(flops), bytes_accessed=int(nbytes), transcendentals=int(exps))


def whole(shape):
    return pl.BlockSpec(shape, lambda *_: (0,) * len(shape))


def rope_tables(length):
    half_size = HEAD_DIM // 2
    inverse = rope_base ** (-(jnp.arange(half_size, dtype=F32) * 2.0 / HEAD_DIM))
    angle = jnp.arange(length, dtype=F32)[:, None] * inverse[None, :]
    cosine = jnp.concatenate([jnp.cos(angle), jnp.cos(angle)], axis=1)
    signed = jnp.concatenate([-jnp.sin(angle), jnp.sin(angle)], axis=1)
    return cosine, signed


def rope(values, cosine, signed):
    return values * cosine + pltpu.roll(values, HEAD_DIM // 2, 1) * signed


def rope_back(values, cosine, signed):
    return values * cosine - pltpu.roll(values, HEAD_DIM // 2, 1) * signed


def grads_kernel(groups, nb, shared_left, c_ref, shared_ref, *refs):
    part = pl.program_id(0) // nb
    for at in range(2 * groups):

        @pl.when(part == at)
        def _(at=at):
            pair = (shared_ref[...], refs[at][...])
            left, right = pair if shared_left else pair[::-1]
            refs[2 * groups + at // 2][...] = dot(left, right, TN).astype(BF16)


def weight_grads(col_index, shared, groups, shared_left):
    tokens, shared_width = shared.shape
    half_width = groups[0][0].shape[1]
    block = min(256, half_width)
    nb = half_width // block
    steps = len(groups) * 2 * nb

    def moving_spec(at):
        return pl.BlockSpec((tokens, block), lambda i, c: (0, jnp.clip(i - at * nb, 0, nb - 1)))

    def out_spec(group):
        def place(i, c):
            inner = jnp.clip(i - group * 2 * nb, 0, 2 * nb - 1)
            at = jnp.where(inner // nb == 0, c[0], 1 - c[0]) * nb + inner % nb
            return (0, at) if shared_left else (at, 0)

        return pl.BlockSpec((shared_width, block) if shared_left else (block, shared_width), place)

    dims = (shared_width, 2 * half_width) if shared_left else (2 * half_width, shared_width)
    return pl.pallas_call(
        functools.partial(grads_kernel, len(groups), nb, shared_left),
        grid_spec=pltpu.PrefetchScalarGridSpec(
            num_scalar_prefetch=1,
            grid=(steps,),
            in_specs=[whole(shared.shape)] + [moving_spec(at) for at in range(2 * len(groups))],
            out_specs=[out_spec(group) for group in range(len(groups))],
        ),
        out_shape=[jax.ShapeDtypeStruct(dims, BF16) for _ in groups],
        compiler_params=params(48, 1),
        cost_estimate=cost(1, 1),
    )(col_index.reshape(1), shared, *[half for group in groups for half in group])


class Line:
    def __init__(self, n):
        self.n = n
        self.r = lax.axis_index("row")
        self.c = lax.axis_index("col")
        self.d = lax.axis_index("dp")

    def copy(self, src, dst, send, recv, **where):
        return pltpu.make_async_remote_copy(
            src_ref=src, dst_ref=dst, send_sem=send, recv_sem=recv, device_id=where,
            device_id_type=pl.DeviceIdType.MESH,
        )

    def up(self, src, dst, send, recv):
        return self.copy(src, dst, send, recv, row=self.r + 1)

    def down(self, src, dst, send, recv):
        return self.copy(src, dst, send, recv, row=self.r - 1)

    def across(self, src, dst, send, recv):
        return self.copy(src, dst, send, recv, col=1 - self.c)

    def barrier(self, core=True, bits=()):
        barrier = pltpu.get_barrier_semaphore()

        def signal(**where):
            pl.semaphore_signal(
                barrier, inc=1, device_id=where, device_id_type=pl.DeviceIdType.MESH
            )

        @pl.when(self.r > 0)
        def _():
            signal(row=self.r - 1)

        @pl.when(self.r < self.n - 1)
        def _():
            signal(row=self.r + 1)

        if core:
            signal(col=1 - self.c)
        for bit in bits:
            signal(dp=self.partner(bit))
        at_end = (self.r == 0) | (self.r == self.n - 1)
        others = int(core) + len(bits)

        @pl.when(at_end)
        def _():
            pl.semaphore_wait(barrier, 1 + others)

        @pl.when(jnp.logical_not(at_end))
        def _():
            pl.semaphore_wait(barrier, 2 + others)

    def side(self, bit):
        return (self.d // 2**bit) % 2

    def partner(self, bit):
        return self.d + (1 - 2 * self.side(bit)) * 2**bit

    def nearest(self, k):
        n = self.n
        code = 0
        for r in range(n):
            order = sorted(range(n), key=lambda q: (abs(q - r), q))
            code += order[k] * n**r
        place, result = self.r * 0 + code, 0
        for r in range(n):
            result = result + (place // n**r) % n * (1 - jnp.minimum(jnp.abs(self.r - r), 1))
        return result


class Gather:
    def __init__(self, line, own, oth, sends, recvs):
        self.line, self.own, self.oth, self.sends, self.recvs = line, own, oth, sends, recvs

    def hop(self, kind, q):
        way = (self.line.up, self.line.down)[kind]
        return way(self.own.at[q], self.own.at[q], self.sends.at[q, kind], self.recvs.at[q, 0])

    def cross(self, q):
        return self.line.across(
            self.own.at[q], self.oth.at[q], self.sends.at[q, 2], self.recvs.at[q, 1]
        )

    def start(self):
        line = self.line

        @pl.when(line.r < line.n - 1)
        def _():
            self.hop(0, line.r).start()

        @pl.when(line.r > 0)
        def _():
            self.hop(1, line.r).start()

        self.cross(line.r).start()

    def step(self, s):
        line = self.line
        low, high = line.r - s, line.r + s

        @pl.when(low >= 0)
        def _():
            self.hop(0, low).wait_recv()

            @pl.when(line.r < line.n - 1)
            def _():
                self.hop(0, low).start()

            self.cross(low).start()

        @pl.when(high <= line.n - 1)
        def _():
            self.hop(1, high).wait_recv()

            @pl.when(line.r > 0)
            def _():
                self.hop(1, high).start()

            self.cross(high).start()

    def arrive(self, q):
        self.cross(q).wait_recv()

    def drain(self):
        line = self.line
        for q in range(line.n):

            @pl.when((line.r >= q) & (line.r < line.n - 1))
            def _(q=q):
                self.hop(0, q).wait_send()

            @pl.when((line.r <= q) & (line.r > 0))
            def _(q=q):
                self.hop(1, q).wait_send()

            self.cross(q).wait_send()


class Scatter:
    def __init__(self, line, part, ups, downs, sends, recvs):
        self.line, self.part, self.ups, self.downs = line, part, ups, downs
        self.sends, self.recvs = sends, recvs

    def hop(self, kind, s, target):
        way = (self.line.up, self.line.down)[kind]
        box = (self.ups, self.downs)[kind]
        return way(
            self.part.at[target], box.at[s - 1], self.sends.at[kind, s - 1], self.recvs.at[kind, s - 1]
        )

    def step(self, s):
        line = self.line
        for kind in range(2):
            behind = line.r if kind == 0 else line.n - 1 - line.r
            target = line.r + line.n - s if kind == 0 else line.r - (line.n - s)
            box = (self.ups, self.downs)[kind]

            @pl.when(behind <= s - 1)
            def _(kind=kind, behind=behind, target=target, box=box):
                if s > 1:

                    @pl.when(behind >= 1)
                    def _():
                        self.hop(kind, s - 1, target).wait_recv()
                        self.part[target] = (
                            self.part[target].astype(F32) + box[s - 2].astype(F32)
                        ).astype(BF16)

                self.hop(kind, s, target).start()

    def total(self, out):
        line = self.line
        last = line.n - 1
        out[...] = self.part[line.r].astype(F32)

        @pl.when(line.r >= 1)
        def _():
            self.hop(0, last, line.r).wait_recv()
            out[...] += self.ups[last - 1].astype(F32)

        @pl.when(line.r <= last - 1)
        def _():
            self.hop(1, last, line.r).wait_recv()
            out[...] += self.downs[last - 1].astype(F32)

    def drain(self):
        line = self.line
        for s in range(1, line.n):

            @pl.when(line.r <= s - 1)
            def _(s=s):
                self.hop(0, s, line.r + line.n - s).wait_send()

            @pl.when(line.n - 1 - line.r <= s - 1)
            def _(s=s):
                self.hop(1, s, line.r - (line.n - s)).wait_send()


class Total:
    def __init__(self, line, ref, result, boxes, bits, sends, recvs):
        self.line, self.ref, self.result, self.boxes, self.bits = line, ref, result, boxes, bits
        self.sends, self.recvs = sends, recvs
        low, size, self.levels = 0, ref.shape[0], []
        for bit in bits:
            size //= 2
            keep = low + line.side(bit) * size
            self.levels.append((size, keep, low + (1 - line.side(bit)) * size))
            low = keep

    def rows(self, at, size):
        return pl.ds(pl.multiple_of(at, 16), size)

    def copy(self, step):
        count = len(self.bits)
        level = step if step < count else 2 * count - 1 - step
        size, keep, give = self.levels[level]
        if step < count:
            src, dst = self.ref.at[self.rows(give, size), :], self.boxes[level]
        else:
            src = dst = self.result.at[self.rows(keep, size), :]
        return self.line.copy(
            src, dst, self.sends.at[step], self.recvs.at[step], dp=self.line.partner(self.bits[level])
        )

    def step(self, step):
        count = len(self.bits)
        if step > 0:
            self.copy(step - 1).wait_recv()
            if step <= count:
                size, keep, _ = self.levels[step - 1]
                rows = self.rows(keep, size)
                kept = self.ref[rows, :].astype(F32) + self.boxes[step - 1][...].astype(F32)
                (self.result if step == count else self.ref)[rows, :] = kept.astype(BF16)
        if step < 2 * count:
            self.copy(step).start()

    def drain(self):
        for step in range(2 * len(self.bits)):
            self.copy(step).wait_send()


def communicate(number, mib):
    return pltpu.CompilerParams(
        collective_id=number, has_side_effects=True, vmem_limit_bytes=mib * MIB
    )


def forward_kernel(
    n, heads, shared_kv,
    prefix_ref, x_ref, gain_one, gain_two, cos_ref, sin_ref,
    grad_in, wq, wk, wv, wo, wgate, wup, wdown,
    n1_out, n2_out, g_out, qkv_out, log_out, o_own_out, o_oth_out, mid_out, scale_out, wo_from,
    a_own_out, a_oth_out, dg_own_out, dg_oth_out, du_own_out, du_oth_out,
    n_own, n_oth, g_own, g_oth, w_own, w_from, wo_ref, wg_ref, wu_ref, wd_ref,
    qkv_ref, vt_ref, o_own, o_oth, log_ref, part, ups, downs, total, scales, row_out, row_in, stage,
    gather_sends, gather_recvs, scatter_sends, scatter_recvs, cross_sends, cross_recvs, local_sems,
    unit_sends, unit_recvs, unit_stores,
):
    batches, tokens, depth = x_ref.shape
    length = n * tokens
    line = Line(n)
    r, c = line.r, line.c
    q_width = heads * HEAD_DIM
    k_col, v_col = q_width, q_width + HEAD_DIM
    share = wgate.shape[1] // 2
    kv_own = 0 if shared_kv else c * HEAD_DIM
    kv_oth = 0 if shared_kv else (1 - c) * HEAD_DIM

    def lanes(at, size):
        return pl.ds(pl.multiple_of(at, 128), size)

    def rows_at(at, size):
        return pl.ds(pl.multiple_of(at, size), size)

    local_count, cross_count = [0], [0]

    def local(src, dst):
        copy = pltpu.make_async_copy(src, dst, local_sems.at[local_count[0]])
        local_count[0] += 1
        copy.start()
        return copy

    def cross(src, dst):
        at = cross_count[0]
        cross_count[0] += 1
        return line.across(src, dst, cross_sends.at[at], cross_recvs.at[at])

    loads = [
        local(wq.at[:, lanes(c * q_width, q_width)], w_own.at[:, pl.ds(0, q_width)]),
        local(wk.at[:, lanes(kv_own, HEAD_DIM)], w_own.at[:, pl.ds(k_col, HEAD_DIM)]),
        local(wv.at[:, lanes(kv_own, HEAD_DIM)], w_own.at[:, pl.ds(v_col, HEAD_DIM)]),
    ]
    wo_load = local(wo, wo_ref)
    g_loads = [local(grad_in.at[m], g_own.at[m, r]) for m in range(batches)]
    unit_loads = [
        local(wgate.at[:, lanes(c * share, share)], wg_ref.at[0]),
        local(wup.at[:, lanes(c * share, share)], wu_ref.at[0]),
        local(wdown.at[rows_at(c * share, share), :], wd_ref.at[0]),
    ]
    for m in range(batches):
        x = x_ref[m].astype(F32)
        squares = jnp.sum(x * x, axis=1, keepdims=True)
        row_out[0, m] = jnp.broadcast_to(squares, (tokens, 128))
    line.barrier()

    def row_cross(which, m):
        return cross(row_out.at[which, m], row_in.at[which, m])

    def norm_scale(which, m, copy):
        copy.wait_recv()
        squares = row_out[which, m] + row_in[which, m]
        value = lax.rsqrt(squares * (1.0 / WIDTH) + epsilon)
        scales[which, m] = value
        return value[:, :1]

    crosses = [row_cross(0, m) for m in range(batches)]
    for copy in crosses:
        copy.start()
    w_cross = [
        cross(wq.at[:, lanes((1 - c) * q_width, q_width)], w_from.at[:, pl.ds(0, q_width)]),
        cross(wk.at[:, lanes(kv_oth, HEAD_DIM)], w_from.at[:, pl.ds(k_col, HEAD_DIM)]),
        cross(wv.at[:, lanes(kv_oth, HEAD_DIM)], w_from.at[:, pl.ds(v_col, HEAD_DIM)]),
    ]
    gathers = [
        [
            Gather(line, own.at[m], oth.at[m], gather_sends.at[at, m], gather_recvs.at[at, m])
            for m in range(batches)
        ]
        for at, (own, oth) in enumerate(((n_own, n_oth), (g_own, g_oth), (n_own, n_oth)))
    ]
    n1, g, n2 = gathers
    rs = [
        Scatter(line, part.at[m], ups.at[m], downs.at[m], scatter_sends.at[m], scatter_recvs.at[m])
        for m in range(batches)
    ]
    for m in range(batches):
        scale_one = norm_scale(0, m, crosses[m])
        n_own[m, r] = (x_ref[m].astype(F32) * scale_one * gain_one[...]).astype(BF16)
        if m == 0:
            n1[0].start()
            for copy in w_cross:
                copy.start()
    for copy in loads:
        copy.wait()
    for copy in w_cross:
        copy.wait_recv()

    def project(m, q):
        n1[m].arrive(q)
        rows = rows_at(q * tokens, tokens)
        pre = dot(n_own[m, q], w_own[...], NN) + dot(n_oth[m, q], w_from[...], NN)
        cosine, signed = cos_ref[rows, :], sin_ref[rows, :]
        for head in range(heads + 1):
            piece = pre[:, head * HEAD_DIM : (head + 1) * HEAD_DIM]
            qkv_ref[m, rows, pl.ds(head * HEAD_DIM, HEAD_DIM)] = rope(piece, cosine, signed).astype(BF16)
        values = pre[:, v_col : v_col + HEAD_DIM].astype(BF16)
        qkv_ref[m, rows, pl.ds(v_col, HEAD_DIM)] = values
        vt_ref[m, :, rows] = values.T

    block = min(256, length)
    count = length // block

    def attend_block(m, index):
        first = index * block
        extent = min(length, max(first + block, PREFIX_TOP))
        keys = qkv_ref[m, pl.ds(0, extent), pl.ds(k_col, HEAD_DIM)]
        key_at = lax.broadcasted_iota(jnp.int32, (extent, block), 0)
        query_at = lax.broadcasted_iota(jnp.int32, (extent, block), 1) + first
        allowed = (key_at <= query_at) | (key_at < prefix_ref[m, 0])
        for head in range(heads):
            cols = pl.ds(head * HEAD_DIM, HEAD_DIM)
            query = qkv_ref[m, pl.ds(first, block), cols]
            scores = jnp.where(allowed, dot(keys, query, NT) * scale, -1e30)
            topmost = jnp.max(scores, axis=0, keepdims=True)
            exponent = jnp.exp(scores - topmost)
            summed = jnp.sum(exponent, axis=0, keepdims=True)
            weights = (exponent * (1.0 / summed)).astype(BF16)
            result = dot(vt_ref[m, :, pl.ds(0, extent)], weights, NN)
            o_own[m, pl.ds(first, block), cols] = result.T.astype(BF16)
            log_ref[m, pl.ds(head, 1), pl.ds(first, block)] = topmost + jnp.log(summed)

    def project_out(m):
        own_rows, oth_rows = rows_at(c * q_width, q_width), rows_at((1 - c) * q_width, q_width)

        @pl.loop(0, n)
        def _(p):
            rows = rows_at(p * tokens, tokens)
            value = dot(o_own[m, rows, :], wo_ref[own_rows, :], NN)
            value = value + dot(o_oth[m, rows, :], wo_ref[oth_rows, :], NN)
            part[m, p] = value.astype(BF16)

    def walk(m, first, last):
        for k in range(first, last):
            n1[m].step(k)
            project(m, line.nearest(k))

    def release(m, store):
        store.wait()
        n1[m].drain()

    def middle(m):
        rs[m].total(total.at[m])
        total[m] = total[m] + x_ref[m].astype(F32)
        mid = total[m]
        squares = jnp.sum(mid * mid, axis=1, keepdims=True)
        row_out[1, m] = jnp.broadcast_to(squares, (tokens, 128))
        copy = row_cross(1, m)
        copy.start()
        scale_two = norm_scale(1, m, copy)
        n_own[m, r] = (total[m] * scale_two * gain_two[...]).astype(BF16)
        crosses.append(copy)
        n2[m].start()

    outs = ((a_own_out, a_oth_out), (dg_own_out, dg_oth_out), (du_own_out, du_oth_out))
    order = [(m, k) for m in range(batches) for k in range(n)]

    def unit_away(at, kind):
        m, k = order[at]
        return line.across(
            stage.at[at % 2, kind], outs[kind][1].at[m, line.nearest(k)],
            unit_sends.at[at, kind], unit_recvs.at[at, kind],
        )

    def unit_kept(at, kind):
        m, k = order[at]
        return pltpu.make_async_copy(
            stage.at[at % 2, kind], outs[kind][0].at[m, line.nearest(k)], unit_stores.at[at, kind]
        )

    def unit_wait(at):
        for kind in range(3):
            unit_away(at, kind).wait_send()
            unit_kept(at, kind).wait()

    def units(at):
        m, k = order[at]
        q = line.nearest(k)
        n2[m].arrive(q)
        g[m].arrive(q)
        if at >= 2:
            unit_wait(at - 2)
        slot = at % 2
        size = min(256, share)

        @pl.loop(0, share // size)
        def _(b):
            cols = rows_at(b * size, size)
            gate = dot(n_own[m, q], wg_ref[0, :, cols], NN) + dot(n_oth[m, q], wg_ref[1, :, cols], NN)
            up = dot(n_own[m, q], wu_ref[0, :, cols], NN) + dot(n_oth[m, q], wu_ref[1, :, cols], NN)
            da = dot(g_own[m, q], wd_ref[0, cols, :], NT) + dot(g_oth[m, q], wd_ref[1, cols, :], NT)
            sigmoid = 1.0 / (1.0 + jnp.exp(-gate))
            silu = gate * sigmoid
            stage[slot, 0, :, cols] = (silu * up).astype(BF16)
            stage[slot, 1, :, cols] = (da * up * sigmoid * (1.0 + gate * (1.0 - sigmoid))).astype(BF16)
            stage[slot, 2, :, cols] = (da * silu).astype(BF16)

        for kind in range(3):
            unit_away(at, kind).start()
            unit_kept(at, kind).start()

    half = (n + 1) // 2
    o_cross = [cross(o_own.at[m], o_oth.at[m]) for m in range(batches)]
    stores = []

    project(0, r)
    walk(0, 1, n - 1)
    n1[1].start()
    walk(0, n - 1, n)
    n1_stores = [local(n_own.at[0], n1_out.at[0])]
    project(1, r)
    for index in range(count // 2):
        attend_block(0, index)
    walk(1, 1, half)
    for index in range(count // 2, count):
        attend_block(0, index)
    o_cross[0].start()
    big_cross = [
        cross(wgate.at[:, lanes((1 - c) * share, share)], wg_ref.at[1]),
        cross(wup.at[:, lanes((1 - c) * share, share)], wu_ref.at[1]),
        cross(wdown.at[rows_at((1 - c) * share, share), :], wd_ref.at[1]),
        cross(wo.at[rows_at((1 - c) * q_width, q_width), :], wo_from),
    ]
    walk(1, half, n - 1)
    o_cross[0].wait_recv()
    wo_load.wait()
    project_out(0)
    rs[0].step(1)
    g_loads[0].wait()
    g[0].start()
    walk(1, n - 1, n)
    n1_stores.append(local(n_own.at[1], n1_out.at[1]))
    for copy in big_cross:
        copy.start()
    for index in range(count // 2):
        attend_block(1, index)
    for s in range(2, half + 1):
        rs[0].step(s)
    for index in range(count // 2, count):
        attend_block(1, index)
    o_cross[1].start()
    for k in range(1, half):
        g[0].step(k)
    release(0, n1_stores[0])
    for s in range(half + 1, n):
        rs[0].step(s)
    o_cross[1].wait_recv()
    project_out(1)
    rs[1].step(1)
    for k in range(half, n - 1):
        g[0].step(k)
    middle(0)
    release(1, n1_stores[1])
    for s in range(2, half + 1):
        rs[1].step(s)
    g[0].step(n - 1)
    for copy in unit_loads:
        copy.wait()
    for copy in big_cross:
        copy.wait_recv()
    g_loads[1].wait()
    stores += [local(g_own.at[0], g_out.at[0])]
    stores += [local(qkv_ref, qkv_out), local(log_ref, log_out)]
    stores += [local(o_own, o_own_out), local(o_oth, o_oth_out), local(total.at[0], mid_out.at[0])]
    units(0)
    for k in range(1, half):
        n2[0].step(k)
        units(k)
    for s in range(half + 1, n):
        rs[1].step(s)
    for k in range(half, n - 1):
        n2[0].step(k)
    g[1].start()
    for k in range(half, n - 1):
        units(k)
    middle(1)
    stores.append(local(total.at[1], mid_out.at[1]))
    stores.append(local(scales, scale_out))
    n2[0].step(n - 1)
    units(n - 1)
    units(n)
    for k in range(1, n):
        g[1].step(k)
        n2[1].step(k)
        units(n + k)
    stores += [local(g_own.at[1], g_out.at[1]), local(n_own, n2_out)]
    for at in range(2 * n - 2, 2 * n):
        unit_wait(at)
    for at in range(2 * n):
        for kind in range(3):
            unit_away(at, kind).wait_recv()
    for copy in crosses + w_cross + o_cross + big_cross:
        copy.wait_send()
    for item in g + n2 + rs:
        item.drain()
    for copy in stores:
        copy.wait()


def forward(
    prefix, x, gain_one, gain_two, tables, grad_in, wq, wk, wv, wo, wgate, wup, wdown, n, heads, shared_kv
):
    batches, tokens, depth = x.shape
    length = n * tokens
    width = (heads + 2) * HEAD_DIM
    q_width = heads * HEAD_DIM
    share = wgate.shape[1] // 2
    vmem = pl.BlockSpec(memory_space=pltpu.VMEM)
    anywhere = pl.BlockSpec(memory_space=pl.ANY)
    gathered, units = (batches, n, tokens, depth), (batches, n, tokens, share)
    rows = (2, batches, tokens, 128)
    shapes = [
        (gathered, BF16), (gathered, BF16), (gathered, BF16),
        ((batches, length, width), BF16), ((batches, 8, length), F32),
        ((batches, length, q_width), BF16), ((batches, length, q_width), BF16),
        ((batches, tokens, depth), F32), (rows, F32), ((q_width, depth), BF16),
    ] + [(units, BF16)] * 6
    boxes = (batches, n - 1, tokens, depth)
    dma = pltpu.SemaphoreType.DMA
    return pl.pallas_call(
        functools.partial(forward_kernel, n, heads, shared_kv),
        in_specs=[pl.BlockSpec(memory_space=pltpu.SMEM)] + [vmem] * 5 + [anywhere] * 8,
        out_specs=[anywhere] * len(shapes),
        out_shape=[jax.ShapeDtypeStruct(*item) for item in shapes],
        scratch_shapes=[
            pltpu.VMEM(gathered, BF16), pltpu.VMEM(gathered, BF16),
            pltpu.VMEM(gathered, BF16), pltpu.VMEM(gathered, BF16),
            pltpu.VMEM((depth, width), BF16), pltpu.VMEM((depth, width), BF16),
            pltpu.VMEM(wo.shape, BF16),
            pltpu.VMEM((2, depth, share), BF16), pltpu.VMEM((2, depth, share), BF16),
            pltpu.VMEM((2, share, depth), BF16),
            pltpu.VMEM((batches, length, width), BF16),
            pltpu.VMEM((batches, HEAD_DIM, length), BF16),
            pltpu.VMEM((batches, length, q_width), BF16), pltpu.VMEM((batches, length, q_width), BF16),
            pltpu.VMEM((batches, 8, length), F32),
            pltpu.VMEM(gathered, BF16), pltpu.VMEM(boxes, BF16), pltpu.VMEM(boxes, BF16),
            pltpu.VMEM((batches, tokens, depth), F32),
            pltpu.VMEM(rows, F32), pltpu.VMEM(rows, F32), pltpu.VMEM(rows, F32),
            pltpu.VMEM((2, 3, tokens, share), BF16),
            dma((3, batches, n, 3)), dma((3, batches, n, 2)),
            dma((batches, 2, n - 1)), dma((batches, 2, n - 1)), dma((13,)), dma((13,)), dma((24,)),
            dma((batches * n, 3)), dma((batches * n, 3)), dma((batches * n, 3)),
        ],
        compiler_params=communicate(1, 62),
        cost_estimate=cost(2e11, 100 * MIB),
    )(prefix, x, gain_one, gain_two, *tables, grad_in, wq, wk, wv, wo, wgate, wup, wdown)


def tail_kernel(
    n, bits, a_own_in, a_oth_in, wdown, n1_in, dqkv_own_in, dqkv_oth_in, dz_in, o_own_in, o_oth_in,
    sum_out, qkv_out, o_out,
    a_ref, wd_ref, part, ups, downs, total, n1_ref, dqkv_ref, dz_ref, o_ref, qkv_ref, o_part, qkv_sum, o_sum, boxes,
    load_sems, a_sems, sends, recvs, total_sends, total_recvs,
):
    batches, _, tokens, share = a_own_in.shape
    depth = wdown.shape[1]
    width, q_width = dqkv_own_in.shape[1], o_own_in.shape[1]
    line = Line(n)
    c = line.c
    pairs = [(n1_in, n1_ref), (dqkv_own_in, dqkv_ref.at[0]), (dqkv_oth_in, dqkv_ref.at[1])]
    pairs += [(dz_in, dz_ref), (o_own_in, o_ref.at[0]), (o_oth_in, o_ref.at[1]), (wdown, wd_ref)]
    loads = [pltpu.make_async_copy(a, b, load_sems.at[i]) for i, (a, b) in enumerate(pairs)]
    order = [(m, p) for m in range(batches) for p in range(n)]

    def a_loads(at):
        m, p = order[at]
        return [
            pltpu.make_async_copy(src.at[m, p], a_ref.at[at % 2, side], a_sems.at[at % 2, side])
            for side, src in enumerate((a_own_in, a_oth_in))
        ]

    for copy in loads + a_loads(0):
        copy.start()
    line.barrier(core=False, bits=bits)
    scatters = [
        Scatter(line, part.at[m], ups.at[m], downs.at[m], sends.at[m], recvs.at[m])
        for m in range(batches)
    ]
    sums = []
    for ref, result, refs in ((qkv_ref, qkv_sum, boxes[0]), (o_part, o_sum, boxes[1])):
        half = ref.shape[0] // 2
        for part_at in range(2):
            at = len(sums)
            rows = pl.ds(part_at * half, half)
            sums.append(
                Total(
                    line, ref.at[rows, :], result.at[rows, :], [box.at[part_at] for box in refs],
                    bits if part_at == 0 else bits[::-1], total_sends.at[at], total_recvs.at[at],
                )
            )
    for copy in loads[:3]:
        copy.wait()
    for side in range(2):
        place = c if side == 0 else 1 - c
        value = dot(n1_ref[...], dqkv_ref[side], TN)
        qkv_ref[:, pl.ds(pl.multiple_of(place * width, 128), width)] = value.astype(BF16)
    for item in sums[:2]:
        item.step(0)
    for copy in loads[3:6]:
        copy.wait()
    for side in range(2):
        place = c if side == 0 else 1 - c
        value = dot(o_ref[side], dz_ref[...], TN)
        o_part[pl.ds(pl.multiple_of(place * q_width, q_width), q_width), :] = value.astype(BF16)
    for item in sums[2:]:
        item.step(0)
    loads[6].wait()
    own_rows = pl.ds(pl.multiple_of(c * share, share), share)
    oth_rows = pl.ds(pl.multiple_of((1 - c) * share, share), share)

    def product(at):
        m, p = order[at]
        for copy in a_loads(at):
            copy.wait()
        if at + 1 < len(order):
            for copy in a_loads(at + 1):
                copy.start()
        value = dot(a_ref[at % 2, 0], wd_ref[own_rows, :], NN)
        part[m, p] = (value + dot(a_ref[at % 2, 1], wd_ref[oth_rows, :], NN)).astype(BF16)

    for at in range(n):
        product(at)
    scatters[0].step(1)
    for item in sums[:2]:
        item.step(1)
    for at in range(n, 2 * n):
        product(at)
    for item in sums[2:]:
        item.step(1)
    turn = 2
    last_turn = 2 * len(bits)
    for s in range(2, n):
        scatters[0].step(s)
        if turn <= last_turn:
            for item in sums:
                item.step(turn)
        turn += 1
    scatters[1].step(1)
    scatters[0].total(total.at[0])
    for s in range(2, n):
        if turn <= last_turn:
            for item in sums:
                item.step(turn)
        turn += 1
        scatters[1].step(s)
    while turn <= last_turn:
        for item in sums:
            item.step(turn)
        turn += 1
    stores = [
        pltpu.make_async_copy(qkv_sum, qkv_out, load_sems.at[0]),
        pltpu.make_async_copy(o_sum, o_out, load_sems.at[1]),
    ]
    for copy in stores:
        copy.start()
    scatters[1].total(total.at[1])
    stores.append(pltpu.make_async_copy(total, sum_out, load_sems.at[2]))
    stores[-1].start()
    for item in scatters + sums:
        item.drain()
    for copy in stores:
        copy.wait()


def tail(a_own, a_oth, wdown, n1, dqkv_own, dqkv_oth, dz, o_own, o_oth, dp_count):
    batches, n, tokens, share = a_own.shape
    rows, depth = n1.shape
    width, q_width = dqkv_own.shape[1], o_own.shape[1]
    bits = list(range(dp_count.bit_length() - 1))
    anywhere = pl.BlockSpec(memory_space=pl.ANY)
    boxes = (batches, n - 1, tokens, depth)
    shapes = [((batches, tokens, depth), F32), ((depth, 2 * width), BF16), ((2 * q_width, depth), BF16)]
    sums = [shape for shape, _ in shapes[1:]]
    return pl.pallas_call(
        functools.partial(tail_kernel, n, bits),
        in_specs=[anywhere] * 9,
        out_specs=[anywhere] * 3,
        out_shape=[jax.ShapeDtypeStruct(*item) for item in shapes],
        scratch_shapes=[
            pltpu.VMEM((2, 2, tokens, share), BF16), pltpu.VMEM(wdown.shape, BF16),
            pltpu.VMEM((batches, n, tokens, depth), BF16), pltpu.VMEM(boxes, BF16),
            pltpu.VMEM(boxes, BF16), pltpu.VMEM((batches, tokens, depth), F32),
            pltpu.VMEM((rows, depth), BF16), pltpu.VMEM((2, rows, width), BF16),
            pltpu.VMEM((rows, depth), BF16), pltpu.VMEM((2, rows, q_width), BF16),
            pltpu.VMEM(sums[0], BF16), pltpu.VMEM(sums[1], BF16),
            pltpu.VMEM(sums[0], BF16), pltpu.VMEM(sums[1], BF16),
            [
                [pltpu.VMEM((2, shape[0] // 2 ** (level + 2), shape[1]), BF16) for level in range(len(bits))]
                for shape in sums
            ],
            pltpu.SemaphoreType.DMA((7,)), pltpu.SemaphoreType.DMA((2, 2)),
            pltpu.SemaphoreType.DMA((batches, 2, n - 1)), pltpu.SemaphoreType.DMA((batches, 2, n - 1)),
            pltpu.SemaphoreType.DMA((4, 2 * len(bits))), pltpu.SemaphoreType.DMA((4, 2 * len(bits))),
        ],
        compiler_params=communicate(4, 56),
        cost_estimate=cost(1e11, 100 * MIB),
    )(a_own, a_oth, wdown, n1, dqkv_own, dqkv_oth, dz, o_own, o_oth)


def backward_kernel(
    n, heads, shared_kv,
    prefix_ref, mid_ref, s2_ref, top_ref, gain_ref, cos_ref, sin_ref, log_ref,
    dg_own_in, dg_oth_in, du_own_in, du_oth_in, wgate, wup, wo, wo_from, wq, wk, wv, qkv_in,
    dz_out, dqkv_own_out, dqkv_oth_out, mgrad_out, fsum_out, gain_out,
    wg_ref, wu_ref, unit_ref, wo_ref, w_own, w_oth, qkv_ref, part, ups, downs, total,
    dz_own, dz_oth, dk_ref, dv_ref, kt_ref, dqkv_own, dqkv_oth, row_out, row_in,
    load_sems, unit_sems, scatter_sends, scatter_recvs, gather_sends, gather_recvs,
    cross_sends, cross_recvs, store_sems,
):
    batches, tokens, depth = mid_ref.shape
    length = n * tokens
    share = wgate.shape[1] // 2
    line = Line(n)
    r, c = line.r, line.c
    q_width = heads * HEAD_DIM
    k_col, v_col = q_width, q_width + HEAD_DIM

    def lanes(at, size):
        return pl.ds(pl.multiple_of(at, 128), size)

    def qkv_columns(side, dst):
        kv = 0 if shared_kv else side * HEAD_DIM
        return [
            (wq.at[:, lanes(side * q_width, q_width)], dst.at[:, pl.ds(0, q_width)]),
            (wk.at[:, lanes(kv, HEAD_DIM)], dst.at[:, pl.ds(k_col, HEAD_DIM)]),
            (wv.at[:, lanes(kv, HEAD_DIM)], dst.at[:, pl.ds(v_col, HEAD_DIM)]),
        ]

    own_rows = pl.ds(pl.multiple_of(c * q_width, q_width), q_width)
    pairs = [(wgate, wg_ref), (wup, wu_ref)]
    pairs += [(wo.at[own_rows, :], wo_ref.at[0]), (wo_from, wo_ref.at[1]), (qkv_in, qkv_ref)]
    pairs += qkv_columns(c, w_own) + qkv_columns(1 - c, w_oth)
    loads = [pltpu.make_async_copy(a, b, load_sems.at[i]) for i, (a, b) in enumerate(pairs)]
    order = [(m, p) for m in range(batches) for p in range(n)]

    def unit_loads(at):
        m, p = order[at]
        return [
            pltpu.make_async_copy(src.at[m, p], unit_ref.at[at % 2, i], unit_sems.at[at % 2, i])
            for i, src in enumerate((dg_own_in, dg_oth_in, du_own_in, du_oth_in))
        ]

    for copy in loads[:2] + unit_loads(0) + loads[2:]:
        copy.start()
    line.barrier()
    units_rs, heads_rs = (
        [
            Scatter(
                line, part.at[m], ups.at[which, m], downs.at[which, m],
                scatter_sends.at[which, m], scatter_recvs.at[which, m],
            )
            for m in range(batches)
        ]
        for which in range(2)
    )
    gathers = [
        Gather(line, dz_own.at[m], dz_oth.at[m], gather_sends.at[m], gather_recvs.at[m])
        for m in range(batches)
    ]
    cols_own = lanes(c * share, share)
    cols_oth = lanes((1 - c) * share, share)

    def unit_part(at):
        m, p = order[at]
        for copy in unit_loads(at):
            copy.wait()
        if at + 1 < len(order):
            for copy in unit_loads(at + 1):
                copy.start()
        slot = at % 2
        block = min(256, depth)

        @pl.loop(0, depth // block)
        def _(b):
            rows = pl.ds(pl.multiple_of(b * block, block), block)
            value = dot(unit_ref[slot, 0], wg_ref[rows, cols_own], NT)
            value = value + dot(unit_ref[slot, 1], wg_ref[rows, cols_oth], NT)
            value = value + dot(unit_ref[slot, 2], wu_ref[rows, cols_own], NT)
            value = value + dot(unit_ref[slot, 3], wu_ref[rows, cols_oth], NT)
            part[m, p, :, rows] = value.astype(BF16)

    def row_cross(m):
        return line.across(row_out.at[m], row_in.at[m], cross_sends.at[m], cross_recvs.at[m])

    def grad_cross(m):
        at = batches + m
        return line.across(dqkv_own.at[m], dqkv_oth.at[m], cross_sends.at[at], cross_recvs.at[at])

    def middle(m):
        units_rs[m].total(total.at[m])
        normed_grad, mid, s = total[m], mid_ref[m], s2_ref[m]
        gain_out_part = jnp.sum(normed_grad * mid * s, axis=0, keepdims=True)
        gain_out[pl.ds(m, 1), :] = gain_out_part
        weighted = normed_grad * gain_ref[...]
        inner = jnp.sum(weighted * mid, axis=1, keepdims=True)
        row_out[m] = jnp.broadcast_to(inner, (tokens, 128))
        row_cross(m).start()
        row_cross(m).wait_recv()
        inner = row_out[m, :, pl.ds(0, 1)] + row_in[m, :, pl.ds(0, 1)]
        result = (
            top_ref[m].astype(F32)
            + total[m] * gain_ref[...] * s
            - mid_ref[m] * ((s * s * s) * inner * (1.0 / WIDTH))
        )
        total[m] = result
        dz_own[m, r] = result.astype(BF16)
        gathers[m].start()

    def store(which, m, src, dst):
        return pltpu.make_async_copy(src, dst, store_sems.at[which, m])

    def attend_back(m, q):
        gathers[m].arrive(q)
        rows = pl.ds(pl.multiple_of(q * tokens, tokens), tokens)
        grads = dot(dz_own[m, q], wo_ref[0], NT)
        grads = (grads + dot(dz_oth[m, q], wo_ref[1], NT)).astype(BF16)
        cosine, signed = cos_ref[rows, :], sin_ref[rows, :]

        def with_keys(extent):
            upto = pl.ds(0, extent)
            keys = qkv_ref[m, upto, pl.ds(k_col, HEAD_DIM)]
            values = qkv_ref[m, upto, pl.ds(v_col, HEAD_DIM)]
            key_at = lax.broadcasted_iota(jnp.int32, (extent, tokens), 0)
            query_at = lax.broadcasted_iota(jnp.int32, (extent, tokens), 1) + q * tokens
            allowed = (key_at <= query_at) | (key_at < prefix_ref[m, 0])
            for head in range(heads):
                cols = pl.ds(head * HEAD_DIM, HEAD_DIM)
                query = qkv_ref[m, rows, cols]
                grad = grads[:, head * HEAD_DIM : (head + 1) * HEAD_DIM]
                raw = dot(keys, query, NT) * scale - log_ref[m, pl.ds(head, 1), rows]
                probs = jnp.exp(jnp.where(allowed, raw, -1e30))
                dv_ref[upto, :] += dot(probs.astype(BF16), grad, NN)
                prob_grad = dot(values, grad, NT)
                inner = jnp.sum(probs * prob_grad, axis=0, keepdims=True)
                rounded = (probs * (prob_grad - inner) * scale).astype(BF16)
                dk_ref[upto, :] += dot(rounded, query, NN)
                dq = dot(kt_ref[:, upto], rounded, NN).T
                dqkv_own[m, rows, cols] = rope_back(dq, cosine, signed).astype(BF16)

        lower = max(length // 2, min(PREFIX_TOP, length))
        split = lower // tokens if lower == length // 2 else 0

        @pl.when(q < split)
        def _():
            with_keys(lower)

        @pl.when(q >= split)
        def _():
            with_keys(length)

    def attention(m, hook):
        dk_ref[...] = jnp.zeros_like(dk_ref)
        dv_ref[...] = jnp.zeros_like(dv_ref)
        kt_ref[...] = qkv_ref[m, :, pl.ds(k_col, HEAD_DIM)].T

        @pl.loop(0, n)
        def _(k):
            @pl.when(k > 0)
            def _():
                gathers[m].step(k)

            hook(k)
            q = 0
            for j in range(n):
                q = q + line.nearest(j) * (1 - jnp.minimum(jnp.abs(k - j), 1))
            attend_back(m, q)

        dk = rope_back(dk_ref[...], cos_ref[...], sin_ref[...])
        dqkv_own[m, :, pl.ds(k_col, HEAD_DIM)] = dk.astype(BF16)
        dqkv_own[m, :, pl.ds(v_col, HEAD_DIM)] = dv_ref[...].astype(BF16)
        grad_cross(m).start()
        store(0, m, dqkv_own.at[m], dqkv_own_out.at[m]).start()
        grad_cross(m).wait_recv()
        store(1, m, dqkv_oth.at[m], dqkv_oth_out.at[m]).start()
        units_rs[m].drain()

        @pl.loop(0, n)
        def _(p):
            rows = pl.ds(pl.multiple_of(p * tokens, tokens), tokens)
            value = dot(dqkv_own[m, rows, :], w_own[...], NT)
            part[m, p] = (value + dot(dqkv_oth[m, rows, :], w_oth[...], NT)).astype(BF16)

    for copy in loads[:2]:
        copy.wait()
    for at in range(n):
        unit_part(at)
    units_rs[0].step(1)
    for at in range(n, 2 * n):
        unit_part(at)
    for copy in loads[2:]:
        copy.wait()
    for s in range(2, n):
        units_rs[0].step(s)
    units_rs[1].step(1)
    middle(0)
    if n > 2:
        units_rs[1].step(2)

    def hook_first(k):
        for s in range(3, n):

            @pl.when(k == s - 2)
            def _(s=s):
                units_rs[1].step(s)

        @pl.when(k == max(n - 2, 0))
        def _():
            middle(1)

    attention(0, hook_first)
    heads_rs[0].step(1)

    def hook_second(k):
        for s in range(2, n):

            @pl.when(k == s - 1)
            def _(s=s):
                heads_rs[0].step(s)

    attention(1, hook_second)
    heads_rs[1].step(1)
    final_stores = [
        store(2, m, total.at[m], mgrad_out.at[m]) for m in range(batches)
    ] + [store(3, m, dz_own.at[m], dz_out.at[m]) for m in range(batches)]
    for copy in final_stores:
        copy.start()
    for copy in final_stores[:batches]:
        copy.wait()
    heads_rs[0].total(total.at[0])
    for s in range(2, n):
        heads_rs[1].step(s)
    heads_rs[1].total(total.at[1])
    sums = [store(4, m, total.at[m], fsum_out.at[m]) for m in range(batches)]
    for copy in sums:
        copy.start()
    for m in range(batches):
        row_cross(m).wait_send()
        grad_cross(m).wait_send()
        heads_rs[m].drain()
        gathers[m].drain()
        store(0, m, dqkv_own.at[m], dqkv_own_out.at[m]).wait()
        store(1, m, dqkv_oth.at[m], dqkv_oth_out.at[m]).wait()
    for copy in final_stores[batches:] + sums:
        copy.wait()


def backward(
    prefix, mid, s2, top, gain, tables, logs, dg_own, dg_oth, du_own, du_oth,
    wgate, wup, wo, wo_from, wq, wk, wv, qkv, n, heads, shared_kv,
):
    batches, tokens, depth = mid.shape
    length, width = qkv.shape[1:]
    share = wgate.shape[1] // 2
    vmem = pl.BlockSpec(memory_space=pltpu.VMEM)
    anywhere = pl.BlockSpec(memory_space=pl.ANY)
    gathered = (batches, n, tokens, depth)
    boxes = (2, batches, n - 1, tokens, depth)
    shapes = [
        (gathered, BF16), (qkv.shape, BF16), (qkv.shape, BF16), (mid.shape, F32), (mid.shape, F32),
        ((8, depth), F32),
    ]
    return pl.pallas_call(
        functools.partial(backward_kernel, n, heads, shared_kv),
        in_specs=[pl.BlockSpec(memory_space=pltpu.SMEM)] + [vmem] * 7 + [anywhere] * 12,
        out_specs=[anywhere] * 5 + [vmem],
        out_shape=[jax.ShapeDtypeStruct(*item) for item in shapes],
        scratch_shapes=[
            pltpu.VMEM(wgate.shape, BF16), pltpu.VMEM(wup.shape, BF16),
            pltpu.VMEM((2, 4, tokens, share), BF16), pltpu.VMEM((2, heads * HEAD_DIM, depth), BF16),
            pltpu.VMEM((depth, width), BF16), pltpu.VMEM((depth, width), BF16),
            pltpu.VMEM(qkv.shape, BF16), pltpu.VMEM(gathered, BF16),
            pltpu.VMEM(boxes, BF16), pltpu.VMEM(boxes, BF16), pltpu.VMEM(mid.shape, F32),
            pltpu.VMEM(gathered, BF16), pltpu.VMEM(gathered, BF16),
            pltpu.VMEM((length, HEAD_DIM), F32), pltpu.VMEM((length, HEAD_DIM), F32),
            pltpu.VMEM((HEAD_DIM, length), BF16), pltpu.VMEM(qkv.shape, BF16), pltpu.VMEM(qkv.shape, BF16),
            pltpu.VMEM((batches, tokens, 128), F32), pltpu.VMEM((batches, tokens, 128), F32),
            pltpu.SemaphoreType.DMA((11,)), pltpu.SemaphoreType.DMA((2, 4)),
            pltpu.SemaphoreType.DMA((2, batches, 2, n - 1)), pltpu.SemaphoreType.DMA((2, batches, 2, n - 1)),
            pltpu.SemaphoreType.DMA((batches, n, 3)), pltpu.SemaphoreType.DMA((batches, n, 2)),
            pltpu.SemaphoreType.DMA((2 * batches,)), pltpu.SemaphoreType.DMA((2 * batches,)),
            pltpu.SemaphoreType.DMA((5, batches)),
        ],
        compiler_params=communicate(3, 60),
        cost_estimate=cost(2e11, 300 * MIB),
    )(
        prefix, mid, s2, top, gain, *tables, logs, dg_own, dg_oth, du_own, du_oth,
        wgate, wup, wo, wo_from, wq, wk, wv, qkv,
    )


def other_core(values):
    count = lax.axis_size("col")
    return lax.ppermute(values, "col", [(i, (i + 1) % count) for i in range(count)])


def butterfly(values, axes):
    for axis in axes:
        n = lax.axis_size(axis)
        reach = 1
        while reach < n:
            values = values + lax.ppermute(values, axis, [(i, i ^ reach) for i in range(n)])
            reach *= 2
    return values


def body(
    hidden_in,
    attn_gain,
    ffn_gain,
    query_weight,
    key_weight,
    value_weight,
    output_weight,
    gate_weight,
    up_weight,
    down_weight,
    prefix_len,
    out_grad,
):
    col_count, row_count = lax.axis_size("col"), lax.axis_size("row")
    col_index = lax.axis_index("col").astype(jnp.int32)
    batches, tokens, _ = hidden_in.shape
    length = tokens * row_count
    heads = query_weight.shape[1] // HEAD_DIM // col_count
    row_kv = key_weight.shape[1] // HEAD_DIM
    shared_kv = row_kv < col_count
    q_width = heads * HEAD_DIM
    tables = rope_tables(length)
    resid = hidden_in.astype(F32)
    (
        n1, n2, g_own, qkv, logs, o_own, o_oth, middle, scales, out_from,
        a_own, a_oth, dg_own, dg_oth, du_own, du_oth,
    ) = forward(
        prefix_len, hidden_in, attn_gain.reshape(1, -1), ffn_gain.reshape(1, -1), tables, out_grad,
        query_weight, key_weight, value_weight, output_weight, gate_weight, up_weight, down_weight,
        row_count, heads, shared_kv,
    )
    scale_one, scale_two = scales[0, :, :, :1], scales[1, :, :, :1]

    def flat(*items):
        return tuple(item.reshape(batches * length, item.shape[-1]) for item in items)

    (down_grad,) = weight_grads(col_index, *flat(g_own), [flat(a_own, a_oth)], False)
    gate_grad, up_grad = weight_grads(
        col_index, *flat(n2), [flat(dg_own, dg_oth), flat(du_own, du_oth)], True
    )
    dg_own, down_grad, gate_grad, up_grad = lax.optimization_barrier(
        (dg_own, down_grad, gate_grad, up_grad)
    )
    down_sum, gate_sum, up_sum = lax.psum((down_grad, gate_grad, up_grad), "dp")
    dz, dqkv_own, dqkv_oth, middle_grad, first_grad, ffn_gains = backward(
        prefix_len, middle, scale_two, out_grad, ffn_gain.reshape(1, -1), tables, logs,
        dg_own, dg_oth, du_own, du_oth, gate_weight, up_weight, output_weight, out_from,
        query_weight, key_weight, value_weight, qkv, row_count, heads, shared_kv,
    )
    down_part, qkv_sum, output_sum = tail(
        a_own, a_oth, down_weight, *flat(n1, dqkv_own, dqkv_oth, dz, o_own, o_oth), lax.axis_size("dp")
    )
    result = (middle + down_part).astype(BF16)
    attn_gain_acc = jnp.sum(first_grad * resid * scale_one, axis=(0, 1))
    ffn_gain_acc = ffn_gains[:batches].sum(axis=0)
    weighted = first_grad * attn_gain
    inner = jnp.sum(weighted * resid, axis=2)
    inner = (inner + other_core(inner))[..., None]
    cubed = scale_one * scale_one * scale_one
    in_grad = middle_grad + weighted * scale_one - resid * cubed * inner / WIDTH

    width = q_width + 2 * HEAD_DIM

    def columns(first, size, shared):
        pieces = [
            qkv_sum[:, side * width + first : side * width + first + size].astype(F32)
            for side in range(col_count)
        ]
        return sum(pieces) if shared else jnp.concatenate(pieces, axis=1)

    gain_one, gain_two = butterfly(jnp.stack([attn_gain_acc, ffn_gain_acc]), ("dp", "row"))
    return (
        result,
        in_grad,
        gain_one,
        gain_two,
        columns(0, q_width, False),
        columns(q_width, HEAD_DIM, shared_kv),
        columns(q_width + HEAD_DIM, HEAD_DIM, shared_kv),
        output_sum.astype(F32),
        gate_sum.astype(F32),
        up_sum.astype(F32),
        down_sum.astype(F32),
    )


def solution(mesh):
    return jax.shard_map(
        body,
        mesh=mesh,
        in_specs=(
            P(None, ("dp", "row"), "col"),
            P("col"),
            P("col"),
            P("col", "row"),
            P("col", "row"),
            P("col", "row"),
            P("row", "col"),
            P("col", "row"),
            P("col", "row"),
            P("row", "col"),
            P(None, "dp"),
            P(None, ("dp", "row"), "col"),
        ),
        out_specs=(
            P(None, ("dp", "row"), "col"),
            P(None, ("dp", "row"), "col"),
            P("col"),
            P("col"),
            P("col", "row"),
            P("col", "row"),
            P("col", "row"),
            P("row", "col"),
            P("col", "row"),
            P("col", "row"),
            P("row", "col"),
        ),
        check_vma=False,
    )
```

time: 962 us -> 677 us (0.70)
  waiting for transfers between devices: 292 us -> 2.52 us
  Pallas kernels: 384 us -> 609 us
  starting transfers between devices: 142 us -> 5.39 us
  local copies, waits for them, and re-layouts: 56.8 us -> 11.2 us
  other arithmetic: 65.7 us -> 30.6 us
    ppermute x60 -> x0, waiting for transfers between devices: 219 us -> none  [the longest x12 99.8 us: row_gather(): lax.ppermute(above[-1], 'row', [(i, i - 1) for i in range(1, n - step + 1)])]
    pallas_call x18 -> x4, Pallas kernels: 188 us -> 354 us  [the longest x1 201 us: backward(): pl.pallas_call(functools.partial(backward_kernel, n, heads, shared_kv), i...]
    ppermute x60 -> x0, starting transfers between devices: 133 us -> none  [the longest x18 62.3 us: row_scatter(): lax.ppermute(send_up.astype(BF16), 'row', [(i, i + 1) for i in range(step)])]
    pallas_call x1, Pallas kernels: 196 us -> 256 us  [forward(): pl.pallas_call(functools.partial(forward_kernel, n, heads, shared_kv), in...]
    psum x3 -> x1, waiting for transfers between devices: 46.3 us -> 0.01 us  [body(): down_sum, gate_sum, up_sum = lax.psum((down_grad, gate_grad, up_grad), 'dp')]
    convert_element_type x22 -> x1, other arithmetic: 31.5 us -> 1.29 us  [body(): result = (middle + down_part).astype(BF16)]
    ppermute x19 -> x1, waiting for transfers between devices: 22.6 us -> 0.01 us  [other_core(): lax.ppermute(values, 'col', [(i, (i + 1) % count) for i in range(count)])]
    unnamed x164 -> x27, local copies, waits for them, and re-layouts: 20.6 us -> 6.37 us
  transfers between devices with their start and end apart: 86 -> 6, of which waited for: 43 -> 2; matrix products, arithmetic and copies ran while one was open for 9% -> 2% of each run, Pallas kernels for 14% -> 46%
where the time goes in v2:
time: 677 us; the launch traced here: 673 us
  Pallas kernels  609 us (90%)
  other arithmetic  30.6 us (5%)
  between operations  14.4 us (2%)
  local copies, waits for them, and re-layouts  11.2 us (2%)
    pallas_call x1, Pallas kernels, forward(): pl.pallas_call(functools.partial(forward_kernel, n, heads, shared_kv), in...  256 us
    pallas_call x1, Pallas kernels, backward(): pl.pallas_call(functools.partial(backward_kernel, n, heads, shared_kv), i...  201 us
    pallas_call x1, Pallas kernels, tail(): pl.pallas_call(functools.partial(tail_kernel, n, bits), in_specs=[anywher...  110 us
    pallas_call x2, Pallas kernels, weight_grads(): pl.pallas_call(functools.partial(grads_kernel, len(groups), nb, shared_le...  42.3 us
  transfers between devices with their start and end apart: 6, of which 2 were waited for; matrix products, arithmetic and copies ran while one was open for 2% of the time, Pallas kernels for 46%

profile of v2, /device:TPU:0, one launch (start us, length us, event | category | flops | bytes accessed | tf_op | source)
XLA Modules:
  0.0 673.5 jit_solution(13002359834014606915)
XLA Ops:
  7.2 1.3 copy.26.prefix_ref
  8.5 2.0 fusion.8
  10.5 1.3 pad_maximum_fusion
  11.8 255.8 %shard_map.203 = (bf16[2,4,256,1024]{3,2,1,0:T(8,128)(2,1)}, bf16[2,4,256,1024]{3,2,1,0:T(8,128)(2,1)}, bf16[2,4,256,1024]{3,2,1,0:T(8,128)(2,1)}, bf16[2,1024,5...) custom-call(s32[2,1]{1,0:T(2,128)} %copy.26.prefix_ref, ...), custom_call_target="tpu_custom_call" | custom-call | flops 199999995904 | bytes 104857600 | tf_op jit(solution)/shard_map/pallas_call | solution.py:687
  267.6 13.5 %shard_map.204 = bf16[2048,1024]{1,0:T(8,128)(2,1)S(1)} custom-call(s32[1]{0:T(128)} %bitcast.4.c_ref, bf16[2048,1024]{1,0:T(8,128)(2,1)} %bitcast.25, bf16[2048,1024]{1,0:T(8,128)(2,1)} %bitcast.23, bf16[2048,1024]{1,0:T(8,128)(2,1)} %bitcast.24), custom_call_target="tpu_custom_call" | custom-call | flops 1 | bytes 1 | tf_op jit(solution)/shard_map/pallas_call | solution.py:94
  281.1 2.0 copy-done
  283.1 28.8 %shard_map.205 = (bf16[1024,2048]{1,0:T(8,128)(2,1)S(1)}, bf16[1024,2048]{1,0:T(8,128)(2,1)}) custom-call(s32[1]{0:T(128)} %bitcast.4.c_ref, bf16[2048,1024]{1,0:T(8,128)(2,1)} %bitcast.30, bf16[2048,1024]{1,0:T(8,128)(2,1)} %bitcast.26, bf16[2048,1024]{1,0:T(8,128)(2,1)} %bitcast.27, bf16[2048,1024]{1,0:T(8,128)(2,1)} %bitcast.28, bf16[2048,1024]{1,0:T(8,128)(2,1)} %bitcast.29), custom_call_target="tpu_custom_call" | custom-call | flops 1 | bytes 1 | tf_op jit(solution)/shard_map/pallas_call | solution.py:94
  312.0 2.0 copy-done.1
  315.0 1.4 slice_reduce_fusion
  316.4 200.9 %shard_map.206 = (bf16[2,4,256,1024]{3,2,1,0:T(8,128)(2,1)}, bf16[2,1024,512]{2,1,0:T(8,128)(2,1)}, bf16[2,1024,512]{2,1,0:T(8,128)(2,1)}, f32[2,256,1024]{2,1,0...) custom-call(s32[2,1]{1,0:T(2,128)} %copy.26.prefix_ref, f32[2,256,1024]{2,1,0:T(8,128)} %get-tuple-element.42.mid_ref, ...), custom_call_target="tpu_custom_call" | custom-call | flops 199999995904 | bytes 314572800 | tf_op jit(solution)/shard_map/pallas_call | solution.py:1129
  517.3 2.3 fusion.5
  521.7 110.3 %shard_map.207 = (f32[2,256,1024]{2,1,0:T(8,128)}, bf16[1024,1024]{1,0:T(8,128)(2,1)}, bf16[512,1024]{1,0:T(8,128)(2,1)}) custom-call(bf16[2,4,256,1024]{3,2,1,0:T(8,128)(2,1)} %get-tuple-element.43.a_own_in, bf16[2,4,256,1024]{3,2,1,0:T(8,128)(2,1)} %get-tuple-element.44.a_oth_in, bf16[2048,1024]{1,0:T(8,128)(2,1)} %wdown.3, bf16[2048,1024]{1,0:T(8,128)(2,1)} %bitcast.42, ...), custom_call_target="tpu_custom_call" | custom-call | flops 99999997952 | bytes 104857600 | tf_op jit(solution)/shard_map/pallas_call | solution.py:841
  632.0 1.4 fusion.10
  633.5 1.4 fusion.11
  634.9 1.3 add_convert_fusion
  636.2 1.6 maximum_convert_fusion
  637.8 2.0 collective-permute-start.2
  641.6 1.2 collective-permute-start.3
  643.9 1.6 convert_element_type.26
  646.3 2.0 fusion.2
  648.2 1.9 collective-permute-done.4
  650.7 6.8 %convert_element_type.27 = f32[1024,2048]{1,0:T(8,128)} convert(bf16[1024,2048]{1,0:T(8,128)(2,1)} %get-tuple-element.75) | non-fusion elementwise | flops 2097152 | bytes 12582912 | tf_op jit(solution)/shard_map/convert_element_type | solution.py:1254
  657.5 4.4 convert_element_type.28
  662.0 4.4 convert_element_type.29
  (46 shorter events, 7.3 us)
Async XLA Ops:
  7.2 643.5 %all-reduce.3.cloned.1.call-start = ((), (), s32[]{:S(2)}) async-start(), calls=%async_computation | async-start | bytes 25165824 | tf_op jit(solution)/shard_map/psum | solution.py:1217
  281.1 2.0 copy-start
  312.0 2.0 copy-start.1
  314.0 1.0 copy-start.10
  316.4 200.9 %copy-start.5 = (bf16[2,256,1024]{2,1,0:T(8,128)(2,1)S(1)}, bf16[2,256,1024]{2,1,0:T(8,128)(2,1)}, u32[]{:S(2)}) copy-start(bf16[2,256,1024]{2,1,0:T(8,128)(2,1)} %x_ref.1) | copy-start | bytes 3145732
  316.4 201.0 %copy-start.11 = (f32[2,256]{1,0:T(2,128)S(1)}, f32[2,256]{1,0:T(2,128)}, u32[]{:S(2)}) copy-start(f32[2,256]{1,0:T(2,128)} %get-tuple-element.84) | copy-start | bytes 6148
  316.4 201.0 %copy-start.12 = (f32[1024]{0:T(1024)S(1)}, f32[1024]{0:T(1024)}, u32[]{:S(2)}) copy-start(f32[1024]{0:T(1024)} %param.13) | copy-start | bytes 12292
  519.7 125.8 %collective-permute-start = (f32[2,256]{1,0:T(2,128)S(1)}, f32[2,256]{1,0:T(2,128)S(1)}, u32[]{:S(2)}, u32[]{:S(2)}) collective-permute-start(f32[2,256]{1,0:T(2,128)S(1)} %get-tuple-element.74), channel_id=1, source_target_pairs={{0,1},{1,0},{2,3},{3,2},{4,5},{5,4},{6,7},{7,6},{8,9},{9,8},{10,11... | collective-permute-start | bytes 6152 | tf_op jit(solution)/shard_map/ppermute | solution.py:1160
  520.5 117.3 %collective-permute-start.1 = (f32[2,1024]{1,0:T(2,128)S(1)}, f32[2,1024]{1,0:T(2,128)S(1)}, u32[]{:S(2)}, u32[]{:S(2)}) collective-permute-start(f32[2,1024]{1,0:T(2,128)S(1)} %pad_maximum_fusion.2), channel_id=1, source_target_pairs={{0,8},{8,0},{16,24},{24,16},{1,9},{9,1},{17,25},{25,17},{2,10},{10... | collective-permute-start | bytes 24584 | tf_op jit(solution)/shard_map/ppermute | solution.py:1168
  632.0 2.9 copy-start.7
  632.0 2.9 copy-start.8
  637.8 6.1 copy-start.9
  637.8 3.7 collective-permute-start.2
  641.6 3.9 collective-permute-start.3
  642.8 3.4 copy-start.2
  642.8 3.4 copy-start.6
  645.5 4.6 collective-permute-start.4
  650.7 6.8 %copy-start.4 = (bf16[1024,2048]{1,0:T(8,128)(2,1)S(1)}, bf16[1024,2048]{1,0:T(8,128)(2,1)}, u32[]{:S(2)}) copy-start(bf16[1024,2048]{1,0:T(8,128)(2,1)} %get-tuple-element.76) | copy-start | bytes 12582916
  657.5 4.5 copy-start.3
Sparse Core Ops, SparseCore 0:
  314.1 260.1 all-reduce.2

commit v3 on v2

--- a/solution.py
+++ b/solution.py
@@ -59,50 +59,6 @@
 
 def rope_back(values, cosine, signed):
     return values * cosine - pltpu.roll(values, HEAD_DIM // 2, 1) * signed
-
-
-def grads_kernel(groups, nb, shared_left, c_ref, shared_ref, *refs):
-    part = pl.program_id(0) // nb
-    for at in range(2 * groups):
-
-        @pl.when(part == at)
-        def _(at=at):
-            pair = (shared_ref[...], refs[at][...])
-            left, right = pair if shared_left else pair[::-1]
-            refs[2 * groups + at // 2][...] = dot(left, right, TN).astype(BF16)
-
-
-def weight_grads(col_index, shared, groups, shared_left):
-    tokens, shared_width = shared.shape
-    half_width = groups[0][0].shape[1]
-    block = min(256, half_width)
-    nb = half_width // block
-    steps = len(groups) * 2 * nb
-
-    def moving_spec(at):
-        return pl.BlockSpec((tokens, block), lambda i, c: (0, jnp.clip(i - at * nb, 0, nb - 1)))
-
-    def out_spec(group):
-        def place(i, c):
-            inner = jnp.clip(i - group * 2 * nb, 0, 2 * nb - 1)
-            at = jnp.where(inner // nb == 0, c[0], 1 - c[0]) * nb + inner % nb
-            return (0, at) if shared_left else (at, 0)
-
-        return pl.BlockSpec((shared_width, block) if shared_left else (block, shared_width), place)
-
-    dims = (shared_width, 2 * half_width) if shared_left else (2 * half_width, shared_width)
-    return pl.pallas_call(
-        functools.partial(grads_kernel, len(groups), nb, shared_left),
-        grid_spec=pltpu.PrefetchScalarGridSpec(
-            num_scalar_prefetch=1,
-            grid=(steps,),
-            in_specs=[whole(shared.shape)] + [moving_spec(at) for at in range(2 * len(groups))],
-            out_specs=[out_spec(group) for group in range(len(groups))],
-        ),
-        out_shape=[jax.ShapeDtypeStruct(dims, BF16) for _ in groups],
-        compiler_params=params(48, 1),
-        cost_estimate=cost(1, 1),
-    )(col_index.reshape(1), shared, *[half for group in groups for half in group])
 
 
 class Line:
@@ -177,30 +133,31 @@
 
 
 class Gather:
-    def __init__(self, line, own, oth, sends, recvs):
+    def __init__(self, line, own, oth, sends, recvs, first=None):
         self.line, self.own, self.oth, self.sends, self.recvs = line, own, oth, sends, recvs
-
-    def hop(self, kind, q):
+        self.first = own.at[line.r] if first is None else first
+
+    def hop(self, kind, q, src=None):
         way = (self.line.up, self.line.down)[kind]
-        return way(self.own.at[q], self.own.at[q], self.sends.at[q, kind], self.recvs.at[q, 0])
-
-    def cross(self, q):
-        return self.line.across(
-            self.own.at[q], self.oth.at[q], self.sends.at[q, 2], self.recvs.at[q, 1]
-        )
+        src = self.own.at[q] if src is None else src
+        return way(src, self.own.at[q], self.sends.at[q, kind], self.recvs.at[q, 0])
+
+    def cross(self, q, src=None):
+        src = self.own.at[q] if src is None else src
+        return self.line.across(src, self.oth.at[q], self.sends.at[q, 2], self.recvs.at[q, 1])
 
     def start(self):
         line = self.line
 
         @pl.when(line.r < line.n - 1)
         def _():
-            self.hop(0, line.r).start()
+            self.hop(0, line.r, self.first).start()
 
         @pl.when(line.r > 0)
         def _():
-            self.hop(1, line.r).start()
-
-        self.cross(line.r).start()
+            self.hop(1, line.r, self.first).start()
+
+        self.cross(line.r, self.first).start()
 
     def step(self, s):
         line = self.line
@@ -304,47 +261,79 @@
                 self.hop(1, s, line.r - (line.n - s)).wait_send()
 
 
-class Total:
-    def __init__(self, line, ref, result, boxes, bits, sends, recvs):
-        self.line, self.ref, self.result, self.boxes, self.bits = line, ref, result, boxes, bits
+def levels_of(line, rows, bits):
+    low, size, levels = 0, rows, []
+    for bit in bits:
+        size //= 2
+        keep = low + line.side(bit) * size
+        levels.append((size, keep, low + (1 - line.side(bit)) * size))
+        low = keep
+    return levels
+
+
+def rows_of(at, size):
+    return pl.ds(pl.multiple_of(at, 16), size)
+
+
+class Reduce:
+    def __init__(self, line, ref, boxes, bits, sends, recvs):
+        self.line, self.ref, self.boxes, self.bits = line, ref, boxes, bits
         self.sends, self.recvs = sends, recvs
-        low, size, self.levels = 0, ref.shape[0], []
-        for bit in bits:
-            size //= 2
-            keep = low + line.side(bit) * size
-            self.levels.append((size, keep, low + (1 - line.side(bit)) * size))
-            low = keep
-
-    def rows(self, at, size):
-        return pl.ds(pl.multiple_of(at, 16), size)
-
-    def copy(self, step):
-        count = len(self.bits)
-        level = step if step < count else 2 * count - 1 - step
-        size, keep, give = self.levels[level]
-        if step < count:
-            src, dst = self.ref.at[self.rows(give, size), :], self.boxes[level]
-        else:
-            src = dst = self.result.at[self.rows(keep, size), :]
+        self.levels = levels_of(line, ref.shape[0], bits)
+
+    def copy(self, at):
+        size, _, give = self.levels[at]
         return self.line.copy(
-            src, dst, self.sends.at[step], self.recvs.at[step], dp=self.line.partner(self.bits[level])
+            self.ref.at[rows_of(give, size), :], self.boxes[at], self.sends.at[at], self.recvs.at[at],
+            dp=self.line.partner(self.bits[at]),
         )
 
-    def step(self, step):
-        count = len(self.bits)
-        if step > 0:
-            self.copy(step - 1).wait_recv()
-            if step <= count:
-                size, keep, _ = self.levels[step - 1]
-                rows = self.rows(keep, size)
-                kept = self.ref[rows, :].astype(F32) + self.boxes[step - 1][...].astype(F32)
-                (self.result if step == count else self.ref)[rows, :] = kept.astype(BF16)
-        if step < 2 * count:
-            self.copy(step).start()
+    def step(self, at, out=None):
+        if at > 0:
+            self.copy(at - 1).wait_recv()
+            size, keep, _ = self.levels[at - 1]
+            rows = rows_of(keep, size)
+            kept = self.ref[rows, :].astype(F32) + self.boxes[at - 1][...].astype(F32)
+            (self.ref if out is None else out)[rows, :] = kept.astype(BF16)
+        if at < len(self.bits):
+            self.copy(at).start()
+
+    def kept(self):
+        size, keep, _ = self.levels[-1]
+        return rows_of(keep, size)
 
     def drain(self):
-        for step in range(2 * len(self.bits)):
-            self.copy(step).wait_send()
+        for at in range(len(self.bits)):
+            self.copy(at).wait_send()
+
+
+class Spread:
+    def __init__(self, line, ref, bits, sends, recvs):
+        self.line, self.ref, self.bits, self.sends, self.recvs = line, ref, bits, sends, recvs
+        self.levels = levels_of(line, ref.shape[0], bits)
+
+    def copy(self, at):
+        level = len(self.bits) - 1 - at
+        size, keep, _ = self.levels[level]
+        part = self.ref.at[rows_of(keep, size), :]
+        return self.line.copy(
+            part, part, self.sends.at[at], self.recvs.at[at], dp=self.line.partner(self.bits[level])
+        )
+
+    def step(self, at):
+        if at > 0:
+            self.copy(at - 1).wait_recv()
+        if at < len(self.bits):
+            self.copy(at).start()
+
+    def drain(self):
+        for at in range(len(self.bits)):
+            self.copy(at).wait_send()
+
+
+def two_ways(ref, bits):
+    half = ref.shape[0] // 2
+    return [(ref.at[pl.ds(at * half, half), :], bits if at == 0 else bits[::-1]) for at in range(2)]
 
 
 def communicate(number, mib):
@@ -713,177 +702,276 @@
     )(prefix, x, gain_one, gain_two, *tables, grad_in, wq, wk, wv, wo, wgate, wup, wdown)
 
 
-def tail_kernel(
-    n, bits, a_own_in, a_oth_in, wdown, n1_in, dqkv_own_in, dqkv_oth_in, dz_in, o_own_in, o_oth_in,
-    sum_out, qkv_out, o_out,
-    a_ref, wd_ref, part, ups, downs, total, n1_ref, dqkv_ref, dz_ref, o_ref, qkv_ref, o_part, qkv_sum, o_sum, boxes,
-    load_sems, a_sems, sends, recvs, total_sends, total_recvs,
+def unit_grads_kernel(
+    n, bits,
+    mid_ref, scales_ref, top_ref, gain_ref,
+    g_in, n2_in, a_own, a_oth, dg_own, dg_oth, du_own, du_oth, wgate, wup,
+    dz_out, dz_oth_out, mgrad_out, down_out, gate_out, up_out, gain_out,
+    wg_ref, wu_ref, unit_ref, part, ups, downs, total, dz_ref, row_out, row_in,
+    shared_ref, moving_ref, down_ref, gate_ref, up_ref, boxes,
+    load_sems, unit_sems, moving_sems, scatter_sends, scatter_recvs, gather_sends, gather_recvs,
+    cross_sends, cross_recvs, store_sems, reduce_sends, reduce_recvs, part_sems,
 ):
-    batches, _, tokens, share = a_own_in.shape
-    depth = wdown.shape[1]
-    width, q_width = dqkv_own_in.shape[1], o_own_in.shape[1]
+    batches, tokens, depth = mid_ref.shape
+    share = a_own.shape[1]
     line = Line(n)
-    c = line.c
-    pairs = [(n1_in, n1_ref), (dqkv_own_in, dqkv_ref.at[0]), (dqkv_oth_in, dqkv_ref.at[1])]
-    pairs += [(dz_in, dz_ref), (o_own_in, o_ref.at[0]), (o_oth_in, o_ref.at[1]), (wdown, wd_ref)]
-    loads = [pltpu.make_async_copy(a, b, load_sems.at[i]) for i, (a, b) in enumerate(pairs)]
+    r, c = line.r, line.c
+    loads = [
+        pltpu.make_async_copy(a, b, load_sems.at[i])
+        for i, (a, b) in enumerate(((wgate, wg_ref), (wup, wu_ref), (g_in, shared_ref)))
+    ]
     order = [(m, p) for m in range(batches) for p in range(n)]
 
-    def a_loads(at):
-        m, p = order[at]
+    def unit_loads(at):
         return [
-            pltpu.make_async_copy(src.at[m, p], a_ref.at[at % 2, side], a_sems.at[at % 2, side])
-            for side, src in enumerate((a_own_in, a_oth_in))
+            pltpu.make_async_copy(
+                src.at[pl.ds(at * tokens, tokens), :], unit_ref.at[at % 2, i], unit_sems.at[at % 2, i]
+            )
+            for i, src in enumerate((dg_own, dg_oth, du_own, du_oth))
         ]
 
-    for copy in loads + a_loads(0):
+    width = min(256, share)
+    nb = share // width
+    kinds = ((a_own, a_oth), (dg_own, dg_oth), (du_own, du_oth))
+
+    def moving(kind, index, go):
+        for side in range(2):
+
+            @pl.when(index // nb == side)
+            def _(side=side):
+                cols = pl.ds(pl.multiple_of((index - side * nb) * width, width), width)
+                copy = pltpu.make_async_copy(
+                    kinds[kind][side].at[:, cols], moving_ref.at[index % 2], moving_sems.at[index % 2]
+                )
+                copy.start() if go else copy.wait()
+
+    for copy in loads[:2] + unit_loads(0) + loads[2:]:
         copy.start()
-    line.barrier(core=False, bits=bits)
+    line.barrier(bits=bits)
     scatters = [
-        Scatter(line, part.at[m], ups.at[m], downs.at[m], sends.at[m], recvs.at[m])
+        Scatter(line, part.at[m], ups.at[m], downs.at[m], scatter_sends.at[m], scatter_recvs.at[m])
         for m in range(batches)
     ]
-    sums = []
-    for ref, result, refs in ((qkv_ref, qkv_sum, boxes[0]), (o_part, o_sum, boxes[1])):
-        half = ref.shape[0] // 2
-        for part_at in range(2):
-            at = len(sums)
-            rows = pl.ds(part_at * half, half)
-            sums.append(
-                Total(
-                    line, ref.at[rows, :], result.at[rows, :], [box.at[part_at] for box in refs],
-                    bits if part_at == 0 else bits[::-1], total_sends.at[at], total_recvs.at[at],
-                )
+    gathers = [
+        Gather(
+            line, dz_out.at[m], dz_oth_out.at[m], gather_sends.at[m], gather_recvs.at[m], dz_ref.at[m]
+        )
+        for m in range(batches)
+    ]
+    reduces = []
+    for kind, ref in enumerate((down_ref, gate_ref, up_ref)):
+        pair = [
+            Reduce(
+                line, view, [box.at[way] for box in boxes[kind]], way_bits,
+                reduce_sends.at[kind, way], reduce_recvs.at[kind, way],
             )
-    for copy in loads[:3]:
-        copy.wait()
-    for side in range(2):
-        place = c if side == 0 else 1 - c
-        value = dot(n1_ref[...], dqkv_ref[side], TN)
-        qkv_ref[:, pl.ds(pl.multiple_of(place * width, 128), width)] = value.astype(BF16)
-    for item in sums[:2]:
-        item.step(0)
-    for copy in loads[3:6]:
-        copy.wait()
-    for side in range(2):
-        place = c if side == 0 else 1 - c
-        value = dot(o_ref[side], dz_ref[...], TN)
-        o_part[pl.ds(pl.multiple_of(place * q_width, q_width), q_width), :] = value.astype(BF16)
-    for item in sums[2:]:
-        item.step(0)
-    loads[6].wait()
-    own_rows = pl.ds(pl.multiple_of(c * share, share), share)
-    oth_rows = pl.ds(pl.multiple_of((1 - c) * share, share), share)
-
-    def product(at):
+            for way, (view, way_bits) in enumerate(two_ways(ref, bits))
+        ]
+        reduces.append(pair)
+    cols_own = pl.ds(pl.multiple_of(c * share, share), share)
+    cols_oth = pl.ds(pl.multiple_of((1 - c) * share, share), share)
+
+    def unit_part(at):
         m, p = order[at]
-        for copy in a_loads(at):
+        for copy in unit_loads(at):
             copy.wait()
         if at + 1 < len(order):
-            for copy in a_loads(at + 1):
+            for copy in unit_loads(at + 1):
                 copy.start()
-        value = dot(a_ref[at % 2, 0], wd_ref[own_rows, :], NN)
-        part[m, p] = (value + dot(a_ref[at % 2, 1], wd_ref[oth_rows, :], NN)).astype(BF16)
-
+        slot = at % 2
+        block = min(256, depth)
+
+        @pl.loop(0, depth // block)
+        def _(b):
+            rows = pl.ds(pl.multiple_of(b * block, block), block)
+            value = dot(unit_ref[slot, 0], wg_ref[rows, cols_own], NT)
+            value = value + dot(unit_ref[slot, 1], wg_ref[rows, cols_oth], NT)
+            value = value + dot(unit_ref[slot, 2], wu_ref[rows, cols_own], NT)
+            value = value + dot(unit_ref[slot, 3], wu_ref[rows, cols_oth], NT)
+            part[m, p, :, rows] = value.astype(BF16)
+
+    def weight_grad(kind):
+        @pl.loop(0, 2 * nb)
+        def _(index):
+            moving(kind, index, False)
+
+            @pl.when(index + 1 < 2 * nb)
+            def _():
+                moving(kind, index + 1, True)
+
+            side = index // nb
+            place = (c + side * (1 - 2 * c)) * nb + index - side * nb
+            cols = pl.ds(pl.multiple_of(place * width, width), width)
+            if kind == 0:
+                down_ref[cols, :] = dot(moving_ref[index % 2], shared_ref[...], TN).astype(BF16)
+            else:
+                ref = gate_ref if kind == 1 else up_ref
+                ref[:, cols] = dot(shared_ref[...], moving_ref[index % 2], TN).astype(BF16)
+
+        if kind + 1 < len(kinds):
+            moving(kind + 1, 0, True)
+
+    def row_cross(m):
+        return line.across(row_out.at[m], row_in.at[m], cross_sends.at[m], cross_recvs.at[m])
+
+    def store(which, m, src, dst):
+        return pltpu.make_async_copy(src, dst, store_sems.at[which, m])
+
+    def middle(m):
+        scatters[m].total(total.at[m])
+        s = scales_ref[1, m][:, :1]
+        gain_out[pl.ds(m, 1), :] = jnp.sum(total[m] * mid_ref[m] * s, axis=0, keepdims=True)
+        total[m] = total[m] * gain_ref[...]
+        inner = jnp.sum(total[m] * mid_ref[m], axis=1, keepdims=True)
+        row_out[m] = jnp.broadcast_to(inner, (tokens, 128))
+        row_cross(m).start()
+        row_cross(m).wait_recv()
+        inner = row_out[m, :, pl.ds(0, 1)] + row_in[m, :, pl.ds(0, 1)]
+        result = (
+            top_ref[m].astype(F32) + total[m] * s - mid_ref[m] * ((s * s * s) * inner * (1.0 / WIDTH))
+        )
+        total[m] = result
+        dz_ref[m] = result.astype(BF16)
+        gathers[m].start()
+        store(0, m, total.at[m], mgrad_out.at[m]).start()
+        store(1, m, dz_ref.at[m], dz_out.at[m, r]).start()
+
+    def steps(item, first, last):
+        for s in range(first, last):
+            item.step(s)
+
+    def reduce_step(kind, at):
+        for item in reduces[kind]:
+            item.step(at)
+
+    half = (n + 1) // 2
+    for copy in loads[:2]:
+        copy.wait()
     for at in range(n):
-        product(at)
+        unit_part(at)
+    moving(0, 0, True)
     scatters[0].step(1)
-    for item in sums[:2]:
-        item.step(1)
+    loads[2].wait()
+    weight_grad(0)
+    reduce_step(0, 0)
+    n2_load = pltpu.make_async_copy(n2_in, shared_ref, load_sems.at[3])
+    n2_load.start()
+    steps(scatters[0], 2, half + 1)
     for at in range(n, 2 * n):
-        product(at)
-    for item in sums[2:]:
-        item.step(1)
-    turn = 2
-    last_turn = 2 * len(bits)
-    for s in range(2, n):
-        scatters[0].step(s)
-        if turn <= last_turn:
-            for item in sums:
-                item.step(turn)
-        turn += 1
+        unit_part(at)
+    steps(scatters[0], half + 1, n)
     scatters[1].step(1)
-    scatters[0].total(total.at[0])
-    for s in range(2, n):
-        if turn <= last_turn:
-            for item in sums:
-                item.step(turn)
-        turn += 1
-        scatters[1].step(s)
-    while turn <= last_turn:
-        for item in sums:
-            item.step(turn)
-        turn += 1
-    stores = [
-        pltpu.make_async_copy(qkv_sum, qkv_out, load_sems.at[0]),
-        pltpu.make_async_copy(o_sum, o_out, load_sems.at[1]),
-    ]
-    for copy in stores:
-        copy.start()
-    scatters[1].total(total.at[1])
-    stores.append(pltpu.make_async_copy(total, sum_out, load_sems.at[2]))
-    stores[-1].start()
-    for item in scatters + sums:
-        item.drain()
-    for copy in stores:
+    n2_load.wait()
+    weight_grad(1)
+    reduce_step(1, 0)
+    middle(0)
+    steps(scatters[1], 2, half + 1)
+    weight_grad(2)
+    reduce_step(2, 0)
+    steps(scatters[1], half + 1, n)
+    steps(gathers[0], 1, half)
+    reduce_step(0, 1)
+    middle(1)
+    steps(gathers[0], half, n)
+    reduce_step(1, 1)
+    steps(gathers[1], 1, half)
+    for kind in range(3):
+        for at in range(2 if kind < 2 else 1, len(bits)):
+            reduce_step(kind, at)
+    steps(gathers[1], half, n)
+    outs = (down_out, gate_out, up_out)
+    kept_stores = []
+    for kind in range(3):
+        reduce_step(kind, len(bits))
+        for way, item in enumerate(reduces[kind]):
+            out_view = two_ways(outs[kind], bits)[way][0]
+            rows = item.kept()
+            copy = pltpu.make_async_copy(
+                item.ref.at[rows, :], out_view.at[rows, :], part_sems.at[kind, way]
+            )
+            copy.start()
+            kept_stores.append(copy)
+    for m in range(batches):
+        for q in range(n):
+            gathers[m].arrive(q)
+        gathers[m].drain()
+        scatters[m].drain()
+        row_cross(m).wait_send()
+        store(0, m, total.at[m], mgrad_out.at[m]).wait()
+        store(1, m, dz_ref.at[m], dz_out.at[m, r]).wait()
+    for pair in reduces:
+        for item in pair:
+            item.drain()
+    for copy in kept_stores:
         copy.wait()
 
 
-def tail(a_own, a_oth, wdown, n1, dqkv_own, dqkv_oth, dz, o_own, o_oth, dp_count):
-    batches, n, tokens, share = a_own.shape
-    rows, depth = n1.shape
-    width, q_width = dqkv_own.shape[1], o_own.shape[1]
+def unit_grads(mid, scales, top, gain, g, n2, halves, wgate, wup, n, dp_count):
+    batches, tokens, depth = mid.shape
+    rows, share = halves[0].shape
     bits = list(range(dp_count.bit_length() - 1))
+    vmem = pl.BlockSpec(memory_space=pltpu.VMEM)
     anywhere = pl.BlockSpec(memory_space=pl.ANY)
+    gathered = (batches, n, tokens, depth)
+    down_dims, gate_dims = (2 * share, depth), (depth, 2 * share)
+    dims = (down_dims, gate_dims, gate_dims)
+    shapes = [(gathered, BF16), (gathered, BF16), (mid.shape, F32)]
+    shapes += [(item, BF16) for item in dims] + [((8, depth), F32)]
     boxes = (batches, n - 1, tokens, depth)
-    shapes = [((batches, tokens, depth), F32), ((depth, 2 * width), BF16), ((2 * q_width, depth), BF16)]
-    sums = [shape for shape, _ in shapes[1:]]
+    width = min(256, share)
+    dma = pltpu.SemaphoreType.DMA
     return pl.pallas_call(
-        functools.partial(tail_kernel, n, bits),
-        in_specs=[anywhere] * 9,
-        out_specs=[anywhere] * 3,
+        functools.partial(unit_grads_kernel, n, bits),
+        in_specs=[vmem] * 4 + [anywhere] * 10,
+        out_specs=[anywhere] * 6 + [vmem],
         out_shape=[jax.ShapeDtypeStruct(*item) for item in shapes],
         scratch_shapes=[
-            pltpu.VMEM((2, 2, tokens, share), BF16), pltpu.VMEM(wdown.shape, BF16),
-            pltpu.VMEM((batches, n, tokens, depth), BF16), pltpu.VMEM(boxes, BF16),
-            pltpu.VMEM(boxes, BF16), pltpu.VMEM((batches, tokens, depth), F32),
+            pltpu.VMEM(wgate.shape, BF16), pltpu.VMEM(wup.shape, BF16),
+            pltpu.VMEM((2, 4, tokens, share), BF16), pltpu.VMEM(gathered, BF16),
+            pltpu.VMEM(boxes, BF16), pltpu.VMEM(boxes, BF16), pltpu.VMEM(mid.shape, F32),
+            pltpu.VMEM(mid.shape, BF16),
+            pltpu.VMEM((batches, tokens, 128), F32), pltpu.VMEM((batches, tokens, 128), F32),
             pltpu.VMEM((rows, depth), BF16), pltpu.VMEM((2, rows, width), BF16),
-            pltpu.VMEM((rows, depth), BF16), pltpu.VMEM((2, rows, q_width), BF16),
-            pltpu.VMEM(sums[0], BF16), pltpu.VMEM(sums[1], BF16),
-            pltpu.VMEM(sums[0], BF16), pltpu.VMEM(sums[1], BF16),
+            pltpu.VMEM(down_dims, BF16), pltpu.VMEM(gate_dims, BF16), pltpu.VMEM(gate_dims, BF16),
             [
-                [pltpu.VMEM((2, shape[0] // 2 ** (level + 2), shape[1]), BF16) for level in range(len(bits))]
-                for shape in sums
+                [pltpu.VMEM((2, item[0] // 2 ** (level + 2), item[1]), BF16) for level in range(len(bits))]
+                for item in dims
             ],
-            pltpu.SemaphoreType.DMA((7,)), pltpu.SemaphoreType.DMA((2, 2)),
-            pltpu.SemaphoreType.DMA((batches, 2, n - 1)), pltpu.SemaphoreType.DMA((batches, 2, n - 1)),
-            pltpu.SemaphoreType.DMA((4, 2 * len(bits))), pltpu.SemaphoreType.DMA((4, 2 * len(bits))),
+            dma((4,)), dma((2, 4)), dma((2,)), dma((batches, 2, n - 1)), dma((batches, 2, n - 1)),
+            dma((batches, n, 3)), dma((batches, n, 2)), dma((batches,)), dma((batches,)),
+            dma((2, batches)), dma((3, 2, len(bits))), dma((3, 2, len(bits))), dma((3, 2)),
         ],
-        compiler_params=communicate(4, 56),
-        cost_estimate=cost(1e11, 100 * MIB),
-    )(a_own, a_oth, wdown, n1, dqkv_own, dqkv_oth, dz, o_own, o_oth)
+        compiler_params=communicate(2, 62),
+        cost_estimate=cost(2e11, 100 * MIB),
+    )(mid, scales, top, gain, g, n2, *halves, wgate, wup)
 
 
 def backward_kernel(
-    n, heads, shared_kv,
-    prefix_ref, mid_ref, s2_ref, top_ref, gain_ref, cos_ref, sin_ref, log_ref,
-    dg_own_in, dg_oth_in, du_own_in, du_oth_in, wgate, wup, wo, wo_from, wq, wk, wv, qkv_in,
-    dz_out, dqkv_own_out, dqkv_oth_out, mgrad_out, fsum_out, gain_out,
-    wg_ref, wu_ref, unit_ref, wo_ref, w_own, w_oth, qkv_ref, part, ups, downs, total,
-    dz_own, dz_oth, dk_ref, dv_ref, kt_ref, dqkv_own, dqkv_oth, row_out, row_in,
-    load_sems, unit_sems, scatter_sends, scatter_recvs, gather_sends, gather_recvs,
-    cross_sends, cross_recvs, store_sems,
+    n, heads, shared_kv, bits,
+    prefix_ref, x_ref, scales_ref, gain_ref, cos_ref, sin_ref, log_ref,
+    mgrad_in, dz_own_in, dz_oth_in, wo, wo_from, wq, wk, wv, qkv_in, a_own_in, a_oth_in, wdown, n1_in,
+    o_own_in, o_oth_in, down_in, gate_in, up_in,
+    grad_out, sum_out, qkv_out, o_out, down_out, gate_out, up_out, gain_out,
+    dz_ref, dz_oth, wo_ref, w_own, w_oth, qkv_ref, dk_ref, dv_ref, kt_ref, dqkv_own, dqkv_oth,
+    part, ups, downs, total, mgrad_ref, a_ref, wide_ref, o_ref, qkv_grad, o_grad, qkv_sum, o_sum, boxes,
+    row_out, row_in,
+    load_sems, dz_sems, a_sems, scatter_sends, scatter_recvs, cross_sends, cross_recvs, store_sems,
+    reduce_sends, reduce_recvs, spread_sends, spread_recvs, unit_sends, unit_recvs,
 ):
-    batches, tokens, depth = mid_ref.shape
+    batches, tokens, depth = x_ref.shape
     length = n * tokens
-    share = wgate.shape[1] // 2
+    share = a_own_in.shape[1]
     line = Line(n)
     r, c = line.r, line.c
     q_width = heads * HEAD_DIM
     k_col, v_col = q_width, q_width + HEAD_DIM
+    width = v_col + HEAD_DIM
 
     def lanes(at, size):
         return pl.ds(pl.multiple_of(at, 128), size)
+
+    def rows_at(at, size):
+        return pl.ds(pl.multiple_of(at, size), size)
 
     def qkv_columns(side, dst):
         kv = 0 if shared_kv else side * HEAD_DIM
@@ -893,24 +981,36 @@
             (wv.at[:, lanes(kv, HEAD_DIM)], dst.at[:, pl.ds(v_col, HEAD_DIM)]),
         ]
 
-    own_rows = pl.ds(pl.multiple_of(c * q_width, q_width), q_width)
-    pairs = [(wgate, wg_ref), (wup, wu_ref)]
-    pairs += [(wo.at[own_rows, :], wo_ref.at[0]), (wo_from, wo_ref.at[1]), (qkv_in, qkv_ref)]
+    pairs = [(wdown, wide_ref.at[pl.ds(0, 2 * share), :]), (qkv_in, qkv_ref)]
+    pairs += [(wo.at[rows_at(c * q_width, q_width), :], wo_ref.at[0]), (wo_from, wo_ref.at[1])]
+    pairs += [(dz_own_in, dz_ref)]
+    first = len(pairs)
     pairs += qkv_columns(c, w_own) + qkv_columns(1 - c, w_oth)
+    pairs += [(o_own_in, o_ref.at[0]), (o_oth_in, o_ref.at[1]), (mgrad_in, mgrad_ref)]
     loads = [pltpu.make_async_copy(a, b, load_sems.at[i]) for i, (a, b) in enumerate(pairs)]
+    n1_load = pltpu.make_async_copy(n1_in, wide_ref.at[pl.ds(0, batches * length), :], load_sems.at[len(pairs)])
     order = [(m, p) for m in range(batches) for p in range(n)]
 
-    def unit_loads(at):
+    def a_loads(at):
+        rows = pl.ds(at * tokens, tokens)
+        return [
+            pltpu.make_async_copy(src.at[rows, :], a_ref.at[at % 2, side], a_sems.at[at % 2, side])
+            for side, src in enumerate((a_own_in, a_oth_in))
+        ]
+
+    def dz_load(at):
         m, p = order[at]
-        return [
-            pltpu.make_async_copy(src.at[m, p], unit_ref.at[at % 2, i], unit_sems.at[at % 2, i])
-            for i, src in enumerate((dg_own_in, dg_oth_in, du_own_in, du_oth_in))
-        ]
-
-    for copy in loads[:2] + unit_loads(0) + loads[2:]:
+        return pltpu.make_async_copy(dz_oth_in.at[m, p], dz_oth.at[at % 2], dz_sems.at[at % 2])
+
+    for copy in loads[:1] + a_loads(0) + loads[1:first] + [dz_load(0)] + loads[first:]:
         copy.start()
-    line.barrier()
-    units_rs, heads_rs = (
+    line.barrier(bits=bits)
+    spreads = [
+        Spread(line, view, way_bits, unit_sends.at[kind, way], unit_recvs.at[kind, way])
+        for kind, ref in enumerate((down_out, gate_out, up_out))
+        for way, (view, way_bits) in enumerate(two_ways(ref, bits))
+    ]
+    out_rs, head_rs = (
         [
             Scatter(
                 line, part.at[m], ups.at[which, m], downs.at[which, m],
@@ -920,244 +1020,273 @@
         ]
         for which in range(2)
     )
-    gathers = [
-        Gather(line, dz_own.at[m], dz_oth.at[m], gather_sends.at[m], gather_recvs.at[m])
-        for m in range(batches)
-    ]
-    cols_own = lanes(c * share, share)
-    cols_oth = lanes((1 - c) * share, share)
-
-    def unit_part(at):
+    reduces, gatherers = [], []
+    for kind, (ref, result) in enumerate(((qkv_grad, qkv_sum), (o_grad, o_sum))):
+        results = two_ways(result, bits)
+        for way, (view, way_bits) in enumerate(two_ways(ref, bits)):
+            reduces.append(
+                Reduce(
+                    line, view, [box.at[way] for box in boxes[kind]], way_bits,
+                    reduce_sends.at[kind, way], reduce_recvs.at[kind, way],
+                )
+            )
+            gatherers.append(
+                Spread(
+                    line, results[way][0], way_bits, spread_sends.at[kind, way], spread_recvs.at[kind, way]
+                )
+            )
+    count = len(bits)
+
+    def total_step(items, at):
+        for item in items:
+            if at <= count:
+                reduces[item].step(at, gatherers[item].ref if at == count else None)
+            if at >= count:
+                gatherers[item].step(at - count)
+
+    def spread_step(at):
+        for item in spreads:
+            item.step(at)
+
+    own_rows, oth_rows = rows_at(c * share, share), rows_at((1 - c) * share, share)
+
+    def down_part(at):
         m, p = order[at]
-        for copy in unit_loads(at):
+        for copy in a_loads(at):
             copy.wait()
         if at + 1 < len(order):
-            for copy in unit_loads(at + 1):
+            for copy in a_loads(at + 1):
                 copy.start()
-        slot = at % 2
-        block = min(256, depth)
-
-        @pl.loop(0, depth // block)
-        def _(b):
-            rows = pl.ds(pl.multiple_of(b * block, block), block)
-            value = dot(unit_ref[slot, 0], wg_ref[rows, cols_own], NT)
-            value = value + dot(unit_ref[slot, 1], wg_ref[rows, cols_oth], NT)
-            value = value + dot(unit_ref[slot, 2], wu_ref[rows, cols_own], NT)
-            value = value + dot(unit_ref[slot, 3], wu_ref[rows, cols_oth], NT)
-            part[m, p, :, rows] = value.astype(BF16)
+        value = dot(a_ref[at % 2, 0], wide_ref[own_rows, :], NN)
+        part[m, p] = (value + dot(a_ref[at % 2, 1], wide_ref[oth_rows, :], NN)).astype(BF16)
+
+    def grad_cross(m):
+        return line.across(dqkv_own.at[m], dqkv_oth.at[m], cross_sends.at[m], cross_recvs.at[m])
 
     def row_cross(m):
-        return line.across(row_out.at[m], row_in.at[m], cross_sends.at[m], cross_recvs.at[m])
-
-    def grad_cross(m):
         at = batches + m
-        return line.across(dqkv_own.at[m], dqkv_oth.at[m], cross_sends.at[at], cross_recvs.at[at])
-
-    def middle(m):
-        units_rs[m].total(total.at[m])
-        normed_grad, mid, s = total[m], mid_ref[m], s2_ref[m]
-        gain_out_part = jnp.sum(normed_grad * mid * s, axis=0, keepdims=True)
-        gain_out[pl.ds(m, 1), :] = gain_out_part
-        weighted = normed_grad * gain_ref[...]
-        inner = jnp.sum(weighted * mid, axis=1, keepdims=True)
+        return line.across(row_out.at[m], row_in.at[m], cross_sends.at[at], cross_recvs.at[at])
+
+    def store(which, m, src, dst):
+        return pltpu.make_async_copy(src, dst, store_sems.at[which, m])
+
+    def attend_start(m):
+        dk_ref[...] = jnp.zeros_like(dk_ref)
+        dv_ref[...] = jnp.zeros_like(dv_ref)
+        kt_ref[...] = qkv_ref[m, :, pl.ds(k_col, HEAD_DIM)].T
+
+    def attend_back(m, q):
+        at = m * n + q
+        dz_load(at).wait()
+        if at + 1 < len(order):
+            dz_load(at + 1).start()
+        rows = pl.ds(q * tokens, tokens)
+        grads = dot(dz_ref[m, q], wo_ref[0], NT)
+        grads = (grads + dot(dz_oth[at % 2], wo_ref[1], NT)).astype(BF16)
+        cosine, signed = cos_ref[rows, :], sin_ref[rows, :]
+        extent = min(length, max((q + 1) * tokens, PREFIX_TOP))
+        upto = pl.ds(0, extent)
+        keys = qkv_ref[m, upto, pl.ds(k_col, HEAD_DIM)]
+        values = qkv_ref[m, upto, pl.ds(v_col, HEAD_DIM)]
+        key_at = lax.broadcasted_iota(jnp.int32, (extent, tokens), 0)
+        query_at = lax.broadcasted_iota(jnp.int32, (extent, tokens), 1) + q * tokens
+        allowed = (key_at <= query_at) | (key_at < prefix_ref[m, 0])
+        for head in range(heads):
+            cols = pl.ds(head * HEAD_DIM, HEAD_DIM)
+            query = qkv_ref[m, rows, cols]
+            grad = grads[:, head * HEAD_DIM : (head + 1) * HEAD_DIM]
+            raw = dot(keys, query, NT) * scale - log_ref[m, pl.ds(head, 1), rows]
+            probs = jnp.exp(jnp.where(allowed, raw, -1e30))
+            dv_ref[upto, :] += dot(probs.astype(BF16), grad, NN)
+            prob_grad = dot(values, grad, NT)
+            inner = jnp.sum(probs * prob_grad, axis=0, keepdims=True)
+            rounded = (probs * (prob_grad - inner) * scale).astype(BF16)
+            dk_ref[upto, :] += dot(rounded, query, NN)
+            dq = dot(kt_ref[:, upto], rounded, NN).T
+            dqkv_own[m, rows, cols] = rope_back(dq, cosine, signed).astype(BF16)
+
+    def attend_end(m):
+        dk = rope_back(dk_ref[...], cos_ref[...], sin_ref[...])
+        dqkv_own[m, :, pl.ds(k_col, HEAD_DIM)] = dk.astype(BF16)
+        dqkv_own[m, :, pl.ds(v_col, HEAD_DIM)] = dv_ref[...].astype(BF16)
+        grad_cross(m).start()
+
+    def head_part(m):
+        grad_cross(m).wait_recv()
+
+        @pl.loop(0, n)
+        def _(p):
+            rows = rows_at(p * tokens, tokens)
+            value = dot(dqkv_own[m, rows, :], w_own[...], NT)
+            part[m, p] = (value + dot(dqkv_oth[m, rows, :], w_oth[...], NT)).astype(BF16)
+
+    def out_total(m):
+        out_rs[m].total(total.at[m])
+        store(0, m, total.at[m], sum_out.at[m]).start()
+
+    def input_grad(m):
+        store(0, m, total.at[m], sum_out.at[m]).wait()
+        head_rs[m].total(total.at[m])
+        s = scales_ref[0, m][:, :1]
+        x = x_ref[m].astype(F32)
+        gain_out[pl.ds(m, 1), :] = jnp.sum(total[m] * x * s, axis=0, keepdims=True)
+        total[m] = total[m] * gain_ref[...]
+        inner = jnp.sum(total[m] * x, axis=1, keepdims=True)
         row_out[m] = jnp.broadcast_to(inner, (tokens, 128))
         row_cross(m).start()
         row_cross(m).wait_recv()
         inner = row_out[m, :, pl.ds(0, 1)] + row_in[m, :, pl.ds(0, 1)]
-        result = (
-            top_ref[m].astype(F32)
-            + total[m] * gain_ref[...] * s
-            - mid_ref[m] * ((s * s * s) * inner * (1.0 / WIDTH))
-        )
-        total[m] = result
-        dz_own[m, r] = result.astype(BF16)
-        gathers[m].start()
-
-    def store(which, m, src, dst):
-        return pltpu.make_async_copy(src, dst, store_sems.at[which, m])
-
-    def attend_back(m, q):
-        gathers[m].arrive(q)
-        rows = pl.ds(pl.multiple_of(q * tokens, tokens), tokens)
-        grads = dot(dz_own[m, q], wo_ref[0], NT)
-        grads = (grads + dot(dz_oth[m, q], wo_ref[1], NT)).astype(BF16)
-        cosine, signed = cos_ref[rows, :], sin_ref[rows, :]
-
-        def with_keys(extent):
-            upto = pl.ds(0, extent)
-            keys = qkv_ref[m, upto, pl.ds(k_col, HEAD_DIM)]
-            values = qkv_ref[m, upto, pl.ds(v_col, HEAD_DIM)]
-            key_at = lax.broadcasted_iota(jnp.int32, (extent, tokens), 0)
-            query_at = lax.broadcasted_iota(jnp.int32, (extent, tokens), 1) + q * tokens
-            allowed = (key_at <= query_at) | (key_at < prefix_ref[m, 0])
-            for head in range(heads):
-                cols = pl.ds(head * HEAD_DIM, HEAD_DIM)
-                query = qkv_ref[m, rows, cols]
-                grad = grads[:, head * HEAD_DIM : (head + 1) * HEAD_DIM]
-                raw = dot(keys, query, NT) * scale - log_ref[m, pl.ds(head, 1), rows]
-                probs = jnp.exp(jnp.where(allowed, raw, -1e30))
-                dv_ref[upto, :] += dot(probs.astype(BF16), grad, NN)
-                prob_grad = dot(values, grad, NT)
-                inner = jnp.sum(probs * prob_grad, axis=0, keepdims=True)
-                rounded = (probs * (prob_grad - inner) * scale).astype(BF16)
-                dk_ref[upto, :] += dot(rounded, query, NN)
-                dq = dot(kt_ref[:, upto], rounded, NN).T
-                dqkv_own[m, rows, cols] = rope_back(dq, cosine, signed).astype(BF16)
-
-        lower = max(length // 2, min(PREFIX_TOP, length))
-        split = lower // tokens if lower == length // 2 else 0
-
-        @pl.when(q < split)
-        def _():
-            with_keys(lower)
-
-        @pl.when(q >= split)
-        def _():
-            with_keys(length)
-
-    def attention(m, hook):
-        dk_ref[...] = jnp.zeros_like(dk_ref)
-        dv_ref[...] = jnp.zeros_like(dv_ref)
-        kt_ref[...] = qkv_ref[m, :, pl.ds(k_col, HEAD_DIM)].T
-
-        @pl.loop(0, n)
-        def _(k):
-            @pl.when(k > 0)
-            def _():
-                gathers[m].step(k)
-
-            hook(k)
-            q = 0
-            for j in range(n):
-                q = q + line.nearest(j) * (1 - jnp.minimum(jnp.abs(k - j), 1))
-            attend_back(m, q)
-
-        dk = rope_back(dk_ref[...], cos_ref[...], sin_ref[...])
-        dqkv_own[m, :, pl.ds(k_col, HEAD_DIM)] = dk.astype(BF16)
-        dqkv_own[m, :, pl.ds(v_col, HEAD_DIM)] = dv_ref[...].astype(BF16)
-        grad_cross(m).start()
-        store(0, m, dqkv_own.at[m], dqkv_own_out.at[m]).start()
-        grad_cross(m).wait_recv()
-        store(1, m, dqkv_oth.at[m], dqkv_oth_out.at[m]).start()
-        units_rs[m].drain()
-
-        @pl.loop(0, n)
-        def _(p):
-            rows = pl.ds(pl.multiple_of(p * tokens, tokens), tokens)
-            value = dot(dqkv_own[m, rows, :], w_own[...], NT)
-            part[m, p] = (value + dot(dqkv_oth[m, rows, :], w_oth[...], NT)).astype(BF16)
-
-    for copy in loads[:2]:
+        total[m] = mgrad_ref[m] + total[m] * s - x * ((s * s * s) * inner * (1.0 / WIDTH))
+        store(1, m, total.at[m], grad_out.at[m]).start()
+
+    def steps(item, first_step, last_step):
+        for s in range(first_step, last_step):
+            item.step(s)
+
+    half = (n + 1) // 2
+    spread_step(0)
+    loads[0].wait()
+    for at in range(n):
+        down_part(at)
+    out_rs[0].step(1)
+    for copy in loads[1:first]:
         copy.wait()
-    for at in range(n):
-        unit_part(at)
-    units_rs[0].step(1)
+    attend_start(0)
+    for q in range(n // 2):
+        attend_back(0, q)
+    steps(out_rs[0], 2, half + 1)
+    for q in range(n // 2, n):
+        attend_back(0, q)
+    attend_end(0)
     for at in range(n, 2 * n):
-        unit_part(at)
-    for copy in loads[2:]:
+        down_part(at)
+    n1_load.start()
+    steps(out_rs[0], half + 1, n)
+    out_rs[1].step(1)
+    for at in range(1, count):
+        spread_step(at)
+    for copy in loads[first:]:
         copy.wait()
+    out_total(0)
+    out_rs[0].drain()
+    head_part(0)
+    head_rs[0].step(1)
+    attend_start(1)
+    for q in range(n // 2):
+        attend_back(1, q)
+    steps(out_rs[1], 2, half + 1)
+    steps(head_rs[0], 2, half + 1)
+    for q in range(n // 2, n):
+        attend_back(1, q)
+    attend_end(1)
+    steps(out_rs[1], half + 1, n)
+    steps(head_rs[0], half + 1, n)
+    n1_load.wait()
+    grad_cross(1).wait_recv()
+    for side in range(2):
+        place = c if side == 0 else 1 - c
+        dqkv = (dqkv_own if side == 0 else dqkv_oth)[...].reshape(batches * length, width)
+        value = dot(wide_ref[pl.ds(0, batches * length), :], dqkv, TN)
+        qkv_grad[:, lanes(place * width, width)] = value.astype(BF16)
+    total_step((0, 1), 0)
+    out_total(1)
+    out_rs[1].drain()
+
+    @pl.loop(0, n)
+    def _(p):
+        rows = rows_at(p * tokens, tokens)
+        value = dot(dqkv_own[1, rows, :], w_own[...], NT)
+        part[1, p] = (value + dot(dqkv_oth[1, rows, :], w_oth[...], NT)).astype(BF16)
+
+    head_rs[1].step(1)
+    for side in range(2):
+        place = c if side == 0 else 1 - c
+        value = dot(o_ref[side], dz_ref[...].reshape(batches * length, depth), TN)
+        o_grad[rows_at(place * q_width, q_width), :] = value.astype(BF16)
+    total_step((2, 3), 0)
+    input_grad(0)
+    turn, last_turn = 1, 2 * count
     for s in range(2, n):
-        units_rs[0].step(s)
-    units_rs[1].step(1)
-    middle(0)
-    if n > 2:
-        units_rs[1].step(2)
-
-    def hook_first(k):
-        for s in range(3, n):
-
-            @pl.when(k == s - 2)
-            def _(s=s):
-                units_rs[1].step(s)
-
-        @pl.when(k == max(n - 2, 0))
-        def _():
-            middle(1)
-
-    attention(0, hook_first)
-    heads_rs[0].step(1)
-
-    def hook_second(k):
-        for s in range(2, n):
-
-            @pl.when(k == s - 1)
-            def _(s=s):
-                heads_rs[0].step(s)
-
-    attention(1, hook_second)
-    heads_rs[1].step(1)
-    final_stores = [
-        store(2, m, total.at[m], mgrad_out.at[m]) for m in range(batches)
-    ] + [store(3, m, dz_own.at[m], dz_out.at[m]) for m in range(batches)]
-    for copy in final_stores:
+        head_rs[1].step(s)
+        if turn <= last_turn:
+            total_step((0, 1, 2, 3), turn)
+        turn += 1
+    input_grad(1)
+    while turn <= last_turn:
+        total_step((0, 1, 2, 3), turn)
+        turn += 1
+    stores = [
+        pltpu.make_async_copy(qkv_sum, qkv_out, load_sems.at[0]),
+        pltpu.make_async_copy(o_sum, o_out, load_sems.at[1]),
+    ]
+    for copy in stores:
         copy.start()
-    for copy in final_stores[:batches]:
+    spread_step(count)
+    for m in range(batches):
+        grad_cross(m).wait_send()
+        row_cross(m).wait_send()
+        head_rs[m].drain()
+        store(1, m, total.at[m], grad_out.at[m]).wait()
+    for item in spreads + reduces + gatherers:
+        item.drain()
+    for copy in stores:
         copy.wait()
-    heads_rs[0].total(total.at[0])
-    for s in range(2, n):
-        heads_rs[1].step(s)
-    heads_rs[1].total(total.at[1])
-    sums = [store(4, m, total.at[m], fsum_out.at[m]) for m in range(batches)]
-    for copy in sums:
-        copy.start()
-    for m in range(batches):
-        row_cross(m).wait_send()
-        grad_cross(m).wait_send()
-        heads_rs[m].drain()
-        gathers[m].drain()
-        store(0, m, dqkv_own.at[m], dqkv_own_out.at[m]).wait()
-        store(1, m, dqkv_oth.at[m], dqkv_oth_out.at[m]).wait()
-    for copy in final_stores[batches:] + sums:
-        copy.wait()
 
 
 def backward(
-    prefix, mid, s2, top, gain, tables, logs, dg_own, dg_oth, du_own, du_oth,
-    wgate, wup, wo, wo_from, wq, wk, wv, qkv, n, heads, shared_kv,
+    prefix, x, scales, gain, tables, logs, mgrad, dz_own, dz_oth, wo, wo_from, wq, wk, wv, qkv,
+    a_own, a_oth, wdown, n1, o_own, o_oth, down, gate, up, heads, shared_kv, dp_count,
 ):
-    batches, tokens, depth = mid.shape
+    batches, tokens, depth = x.shape
+    n = dz_own.shape[1]
     length, width = qkv.shape[1:]
-    share = wgate.shape[1] // 2
+    rows, q_width = o_own.shape
+    share = a_own.shape[1]
+    bits = list(range(dp_count.bit_length() - 1))
     vmem = pl.BlockSpec(memory_space=pltpu.VMEM)
     anywhere = pl.BlockSpec(memory_space=pl.ANY)
     gathered = (batches, n, tokens, depth)
     boxes = (2, batches, n - 1, tokens, depth)
-    shapes = [
-        (gathered, BF16), (qkv.shape, BF16), (qkv.shape, BF16), (mid.shape, F32), (mid.shape, F32),
-        ((8, depth), F32),
-    ]
+    sums = [(depth, 2 * width), (2 * q_width, depth)]
+    shapes = [(mgrad.shape, F32), (mgrad.shape, F32)] + [(item, BF16) for item in sums]
+    shapes += [(item.shape, BF16) for item in (down, gate, up)] + [((8, depth), F32)]
+    dma = pltpu.SemaphoreType.DMA
     return pl.pallas_call(
-        functools.partial(backward_kernel, n, heads, shared_kv),
-        in_specs=[pl.BlockSpec(memory_space=pltpu.SMEM)] + [vmem] * 7 + [anywhere] * 12,
-        out_specs=[anywhere] * 5 + [vmem],
+        functools.partial(backward_kernel, n, heads, shared_kv, bits),
+        in_specs=[pl.BlockSpec(memory_space=pltpu.SMEM)] + [vmem] * 6 + [anywhere] * 18,
+        out_specs=[anywhere] * 7 + [vmem],
         out_shape=[jax.ShapeDtypeStruct(*item) for item in shapes],
+        input_output_aliases={22: 4, 23: 5, 24: 6},
         scratch_shapes=[
-            pltpu.VMEM(wgate.shape, BF16), pltpu.VMEM(wup.shape, BF16),
-            pltpu.VMEM((2, 4, tokens, share), BF16), pltpu.VMEM((2, heads * HEAD_DIM, depth), BF16),
+            pltpu.VMEM(gathered, BF16), pltpu.VMEM((2, tokens, depth), BF16),
+            pltpu.VMEM((2, q_width, depth), BF16),
             pltpu.VMEM((depth, width), BF16), pltpu.VMEM((depth, width), BF16),
-            pltpu.VMEM(qkv.shape, BF16), pltpu.VMEM(gathered, BF16),
-            pltpu.VMEM(boxes, BF16), pltpu.VMEM(boxes, BF16), pltpu.VMEM(mid.shape, F32),
-            pltpu.VMEM(gathered, BF16), pltpu.VMEM(gathered, BF16),
+            pltpu.VMEM(qkv.shape, BF16),
             pltpu.VMEM((length, HEAD_DIM), F32), pltpu.VMEM((length, HEAD_DIM), F32),
             pltpu.VMEM((HEAD_DIM, length), BF16), pltpu.VMEM(qkv.shape, BF16), pltpu.VMEM(qkv.shape, BF16),
+            pltpu.VMEM(gathered, BF16), pltpu.VMEM(boxes, BF16), pltpu.VMEM(boxes, BF16),
+            pltpu.VMEM(mgrad.shape, F32), pltpu.VMEM(mgrad.shape, F32),
+            pltpu.VMEM((2, 2, tokens, share), BF16),
+            pltpu.VMEM((max(2 * share, rows), depth), BF16), pltpu.VMEM((2, rows, q_width), BF16),
+            pltpu.VMEM(sums[0], BF16), pltpu.VMEM(sums[1], BF16),
+            pltpu.VMEM(sums[0], BF16), pltpu.VMEM(sums[1], BF16),
+            [
+                [pltpu.VMEM((2, item[0] // 2 ** (level + 2), item[1]), BF16) for level in range(len(bits))]
+                for item in sums
+            ],
             pltpu.VMEM((batches, tokens, 128), F32), pltpu.VMEM((batches, tokens, 128), F32),
-            pltpu.SemaphoreType.DMA((11,)), pltpu.SemaphoreType.DMA((2, 4)),
-            pltpu.SemaphoreType.DMA((2, batches, 2, n - 1)), pltpu.SemaphoreType.DMA((2, batches, 2, n - 1)),
-            pltpu.SemaphoreType.DMA((batches, n, 3)), pltpu.SemaphoreType.DMA((batches, n, 2)),
-            pltpu.SemaphoreType.DMA((2 * batches,)), pltpu.SemaphoreType.DMA((2 * batches,)),
-            pltpu.SemaphoreType.DMA((5, batches)),
+            dma((15,)), dma((2,)), dma((2, 2)),
+            dma((2, batches, 2, n - 1)), dma((2, batches, 2, n - 1)),
+            dma((2 * batches,)), dma((2 * batches,)), dma((2, batches)),
+            dma((2, 2, len(bits))), dma((2, 2, len(bits))), dma((2, 2, len(bits))), dma((2, 2, len(bits))),
+            dma((3, 2, len(bits))), dma((3, 2, len(bits))),
         ],
-        compiler_params=communicate(3, 60),
-        cost_estimate=cost(2e11, 300 * MIB),
+        compiler_params=communicate(3, 62),
+        cost_estimate=cost(2e11, 100 * MIB),
     )(
-        prefix, mid, s2, top, gain, *tables, logs, dg_own, dg_oth, du_own, du_oth,
-        wgate, wup, wo, wo_from, wq, wk, wv, qkv,
+        prefix, x, scales, gain, *tables, logs, mgrad, dz_own, dz_oth, wo, wo_from, wq, wk, wv, qkv,
+        a_own, a_oth, wdown, n1, o_own, o_oth, down, gate, up,
     )
-
-
-def other_core(values):
-    count = lax.axis_size("col")
-    return lax.ppermute(values, "col", [(i, (i + 1) % count) for i in range(count)])
 
 
 def butterfly(values, axes):
@@ -1185,7 +1314,6 @@
     out_grad,
 ):
     col_count, row_count = lax.axis_size("col"), lax.axis_size("row")
-    col_index = lax.axis_index("col").astype(jnp.int32)
     batches, tokens, _ = hidden_in.shape
     length = tokens * row_count
     heads = query_weight.shape[1] // HEAD_DIM // col_count
@@ -1193,7 +1321,6 @@
     shared_kv = row_kv < col_count
     q_width = heads * HEAD_DIM
     tables = rope_tables(length)
-    resid = hidden_in.astype(F32)
     (
         n1, n2, g_own, qkv, logs, o_own, o_oth, middle, scales, out_from,
         a_own, a_oth, dg_own, dg_oth, du_own, du_oth,
@@ -1202,36 +1329,24 @@
         query_weight, key_weight, value_weight, output_weight, gate_weight, up_weight, down_weight,
         row_count, heads, shared_kv,
     )
-    scale_one, scale_two = scales[0, :, :, :1], scales[1, :, :, :1]
 
     def flat(*items):
         return tuple(item.reshape(batches * length, item.shape[-1]) for item in items)
 
-    (down_grad,) = weight_grads(col_index, *flat(g_own), [flat(a_own, a_oth)], False)
-    gate_grad, up_grad = weight_grads(
-        col_index, *flat(n2), [flat(dg_own, dg_oth), flat(du_own, du_oth)], True
+    dp_count = lax.axis_size("dp")
+    a_own, a_oth, *grads = flat(a_own, a_oth, dg_own, dg_oth, du_own, du_oth)
+    dz, dz_oth, middle_grad, down_sum, gate_sum, up_sum, ffn_gains = unit_grads(
+        middle, scales, out_grad, ffn_gain.reshape(1, -1), *flat(g_own, n2), (a_own, a_oth, *grads),
+        gate_weight, up_weight, row_count, dp_count,
     )
-    dg_own, down_grad, gate_grad, up_grad = lax.optimization_barrier(
-        (dg_own, down_grad, gate_grad, up_grad)
-    )
-    down_sum, gate_sum, up_sum = lax.psum((down_grad, gate_grad, up_grad), "dp")
-    dz, dqkv_own, dqkv_oth, middle_grad, first_grad, ffn_gains = backward(
-        prefix_len, middle, scale_two, out_grad, ffn_gain.reshape(1, -1), tables, logs,
-        dg_own, dg_oth, du_own, du_oth, gate_weight, up_weight, output_weight, out_from,
-        query_weight, key_weight, value_weight, qkv, row_count, heads, shared_kv,
-    )
-    down_part, qkv_sum, output_sum = tail(
-        a_own, a_oth, down_weight, *flat(n1, dqkv_own, dqkv_oth, dz, o_own, o_oth), lax.axis_size("dp")
+    in_grad, down_part, qkv_sum, output_sum, down_sum, gate_sum, up_sum, attn_gains = backward(
+        prefix_len, hidden_in, scales, attn_gain.reshape(1, -1), tables, logs, middle_grad, dz, dz_oth,
+        output_weight, out_from, query_weight, key_weight, value_weight, qkv, a_own, a_oth, down_weight,
+        *flat(n1, o_own, o_oth), down_sum, gate_sum, up_sum, heads, shared_kv, dp_count,
     )
     result = (middle + down_part).astype(BF16)
-    attn_gain_acc = jnp.sum(first_grad * resid * scale_one, axis=(0, 1))
+    attn_gain_acc = attn_gains[:batches].sum(axis=0)
     ffn_gain_acc = ffn_gains[:batches].sum(axis=0)
-    weighted = first_grad * attn_gain
-    inner = jnp.sum(weighted * resid, axis=2)
-    inner = (inner + other_core(inner))[..., None]
-    cubed = scale_one * scale_one * scale_one
-    in_grad = middle_grad + weighted * scale_one - resid * cubed * inner / WIDTH
-
     width = q_width + 2 * HEAD_DIM
 
     def columns(first, size, shared):

time: 677 us -> 635 us (0.938)
  Pallas kernels: 609 us -> 591 us
  between operations: 14.4 us -> 0.99 us
  local copies, waits for them, and re-layouts: 11.2 us -> 3.5 us
    pallas_call x4 -> x2, Pallas kernels: 354 us -> 336 us  [the longest x1 173 us: backward(): pl.pallas_call(functools.partial(backward_kernel, n, heads, shared_kv, bi...]
  transfers between devices with their start and end apart: 6 -> 4, of which waited for: 2 -> 2; matrix products, arithmetic and copies ran while one was open for 2% -> 4% of each run, Pallas kernels for 46% -> 0%
where the time goes in v3:
time: 635 us; the launch traced here: 632 us
  Pallas kernels  591 us (93%)
  other arithmetic  27.1 us (4%)
    pallas_call x1, Pallas kernels, forward(): pl.pallas_call(functools.partial(forward_kernel, n, heads, shared_kv), in...  256 us
    pallas_call x1, Pallas kernels, backward(): pl.pallas_call(functools.partial(backward_kernel, n, heads, shared_kv, bi...  173 us
    pallas_call x1, Pallas kernels, unit_grads(): pl.pallas_call(functools.partial(unit_grads_kernel, n, bits), in_specs=[v...  163 us
  transfers between devices with their start and end apart: 4, of which 2 were waited for; matrix products, arithmetic and copies ran while one was open for 4% of the time, Pallas kernels for 0%

profile of v3, /device:TPU:0, one launch (start us, length us, event | category | flops | bytes accessed | tf_op | source)
XLA Modules:
  0.0 631.8 jit_solution(2139363172008805092)
XLA Ops:
  0.7 1.3 copy.26.prefix_ref
  2.0 2.0 fusion.2
  3.9 1.3 pad_maximum_fusion
  5.2 255.8 %shard_map.203 = (bf16[2,4,256,1024]{3,2,1,0:T(8,128)(2,1)}, bf16[2,4,256,1024]{3,2,1,0:T(8,128)(2,1)}, bf16[2,4,256,1024]{3,2,1,0:T(8,128)(2,1)}, bf16[2,1024,5...) custom-call(s32[2,1]{1,0:T(2,128)} %copy.26.prefix_ref, ...), custom_call_target="tpu_custom_call" | custom-call | flops 199999995904 | bytes 104857600 | tf_op jit(solution)/shard_map/pallas_call | solution.py:676
  261.0 162.6 %shard_map.204 = (bf16[2,4,256,1024]{3,2,1,0:T(8,128)(2,1)}, bf16[2,4,256,1024]{3,2,1,0:T(8,128)(2,1)}, f32[2,256,1024]{2,1,0:T(8,128)}, bf16[2048,1024]{1,0:T(8...) custom-call(f32[2,256,1024]{2,1,0:T(8,128)} %get-tuple-element.42.mid_ref, ...), custom_call_target="tpu_custom_call" | custom-call | flops 199999995904 | bytes 104857600 | tf_op jit(solution)/shard_map/pallas_call | solution.py:923
  423.7 173.0 %shard_map.205 = (f32[2,256,1024]{2,1,0:T(8,128)}, f32[2,256,1024]{2,1,0:T(8,128)}, bf16[1024,1024]{1,0:T(8,128)(2,1)}, bf16[512,1024]{1,0:T(8,128)(2,1)}, bf16[...) custom-call(s32[2,1]{1,0:T(2,128)} %copy.26.prefix_ref, ...), custom_call_target="tpu_custom_call", output_to_operand_aliasing={{4}: (22, {}), {5}: (23, {}), {6}: (24, {})} | custom-call | flops 199999995904 | bytes 104857600 | tf_op jit(solution)/shard_map/pallas_call | solution.py:1254
  596.7 0.9 slice_reduce_fusion.1
  597.7 0.8 slice_reduce_fusion
  598.5 2.6 collective-permute-start
  601.0 3.5 add_convert_fusion
  604.6 0.2 fusion.4
  604.9 1.6 maximum_convert_fusion
  606.5 2.0 collective-permute-done.1
  608.6 2.0 collective-permute-start.2
  610.6 1.0 maximum_convert_fusion.2
  611.6 0.6 collective-permute-done.2
  612.3 1.4 collective-permute-start.3
  613.7 1.0 maximum_convert_fusion.1
  614.7 1.6 convert_element_type.22
  616.3 4.4 convert_element_type.23
  620.8 4.4 convert_element_type.24
  625.2 4.4 convert_element_type.25
  629.7 0.6 fusion.6
  630.3 1.3 copy.32
  (22 shorter events, 0.2 us)
Async XLA Ops:
  596.7 7.8 %copy-start.4 = (bf16[1024,1024]{1,0:T(8,128)(2,1)S(1)}, bf16[1024,1024]{1,0:T(8,128)(2,1)}, u32[]{:S(2)}) copy-start(bf16[1024,1024]{1,0:T(8,128)(2,1)} %get-tuple-element.68) | copy-start | bytes 6291460
  598.5 6.3 %collective-permute-start = (f32[2,1024]{1,0:T(2,128)S(1)}, f32[2,1024]{1,0:T(2,128)S(1)}, u32[]{:S(2)}, u32[]{:S(2)}) collective-permute-start(f32[2,1024]{1,0:T(2,128)S(1)} %pad_maximum_fusion.2), channel_id=1, source_target_pairs={{0,8},{8,0},{16,24},{24,16},{1,9},{9,1},{17,25},{25,17},{2,10},{10... | collective-permute-start | bytes 24584 | tf_op jit(solution)/shard_map/ppermute | solution.py:1297
  604.6 10.1 %copy-start.5 = (bf16[512,1024]{1,0:T(8,128)(2,1)S(1)}, bf16[512,1024]{1,0:T(8,128)(2,1)}, u32[]{:S(2)}) copy-start(bf16[512,1024]{1,0:T(8,128)(2,1)} %get-tuple-element.69) | copy-start | bytes 3145732
  604.8 3.7 collective-permute-start.1
  604.9 11.4 %copy-start.1 = (bf16[1024,2048]{1,0:T(8,128)(2,1)S(1)}, bf16[1024,2048]{1,0:T(8,128)(2,1)}, u32[]{:S(2)}) copy-start(bf16[1024,2048]{1,0:T(8,128)(2,1)} %get-tuple-element.70) | copy-start | bytes 12582916
  608.6 3.7 collective-permute-start.2
  612.3 17.4 %collective-permute-start.3 = (f32[2,1024]{1,0:T(2,128)S(1)}, f32[2,1024]{1,0:T(2,128)S(1)}, u32[]{:S(2)}, u32[]{:S(2)}) collective-permute-start(f32[2,1024]{1,0:T(2,128)S(1)} %add.18), channel_id=1, source_target_pairs={{0,4},{2,6},{4,0},{6,2},{1,5},{3,7},{5,1},{7,3},{8,12},{10,14},{12... | collective-permute-start | bytes 24584 | tf_op jit(solution)/shard_map/ppermute | solution.py:1297
  616.3 4.5 copy-start.2
  620.8 4.5 copy-start
  625.2 5.1 copy-start.3

commit v4 on v3

--- a/solution.py
+++ b/solution.py
@@ -3,6 +3,7 @@
 
 import jax
 import jax.numpy as jnp
+import numpy as np
 from jax import lax
 from jax.experimental import pallas as pl
 from jax.experimental.pallas import tpu as pltpu
@@ -46,11 +47,11 @@
 
 def rope_tables(length):
     half_size = HEAD_DIM // 2
-    inverse = rope_base ** (-(jnp.arange(half_size, dtype=F32) * 2.0 / HEAD_DIM))
-    angle = jnp.arange(length, dtype=F32)[:, None] * inverse[None, :]
-    cosine = jnp.concatenate([jnp.cos(angle), jnp.cos(angle)], axis=1)
-    signed = jnp.concatenate([-jnp.sin(angle), jnp.sin(angle)], axis=1)
-    return cosine, signed
+    inverse = rope_base ** (-(np.arange(half_size) * 2.0 / HEAD_DIM))
+    angle = np.arange(length)[:, None] * inverse[None, :]
+    cosine = np.concatenate([np.cos(angle), np.cos(angle)], axis=1)
+    signed = np.concatenate([-np.sin(angle), np.sin(angle)], axis=1)
+    return jnp.asarray(cosine, F32), jnp.asarray(signed, F32)
 
 
 def rope(values, cosine, signed):
@@ -113,6 +114,17 @@
         @pl.when(jnp.logical_not(at_end))
         def _():
             pl.semaphore_wait(barrier, 2 + others)
+
+    def wide_barrier(self, dp_count):
+        barrier = pltpu.get_barrier_semaphore()
+        peers = [dict(row=(self.r + at) % self.n) for at in range(1, self.n)]
+        peers += [dict(dp=(self.d + at) % dp_count) for at in range(1, dp_count)]
+        peers += [dict(col=1 - self.c)]
+        for where in peers:
+            pl.semaphore_signal(
+                barrier, inc=1, device_id=where, device_id_type=pl.DeviceIdType.MESH
+            )
+        pl.semaphore_wait(barrier, len(peers))
 
     def side(self, bit):
         return (self.d // 2**bit) % 2
@@ -234,9 +246,12 @@
                 self.hop(kind, s, target).start()
 
     def total(self, out):
+        out[...] = self.part[self.line.r].astype(F32)
+        self.add_received(out)
+
+    def add_received(self, out):
         line = self.line
         last = line.n - 1
-        out[...] = self.part[line.r].astype(F32)
 
         @pl.when(line.r >= 1)
         def _():
@@ -259,6 +274,33 @@
             @pl.when(line.n - 1 - line.r <= s - 1)
             def _(s=s):
                 self.hop(1, s, line.r - (line.n - s)).wait_send()
+
+
+class Everywhere:
+    def __init__(self, line, axis, place, count, ref, boxes, sends, recvs):
+        self.line, self.axis, self.place, self.count = line, axis, place, count
+        self.ref, self.boxes, self.sends, self.recvs = ref, boxes, sends, recvs
+
+    def copy(self, at):
+        return self.line.copy(
+            self.ref, self.boxes.at[at - 1], self.sends.at[at - 1], self.recvs.at[at - 1],
+            **{self.axis: (self.place + at) % self.count},
+        )
+
+    def start(self):
+        for at in range(1, self.count):
+            self.copy(at).start()
+
+    def total(self):
+        value = self.ref[...]
+        for at in range(1, self.count):
+            self.copy(at).wait_recv()
+            value = value + self.boxes[at - 1]
+        return value
+
+    def drain(self):
+        for at in range(1, self.count):
+            self.copy(at).wait_send()
 
 
 def levels_of(line, rows, bits):
@@ -308,8 +350,9 @@
 
 
 class Spread:
-    def __init__(self, line, ref, bits, sends, recvs):
+    def __init__(self, line, ref, bits, sends, recvs, skip=0):
         self.line, self.ref, self.bits, self.sends, self.recvs = line, ref, bits, sends, recvs
+        self.count = len(bits) - skip
         self.levels = levels_of(line, ref.shape[0], bits)
 
     def copy(self, at):
@@ -321,13 +364,13 @@
         )
 
     def step(self, at):
-        if at > 0:
+        if 0 < at <= self.count:
             self.copy(at - 1).wait_recv()
-        if at < len(self.bits):
+        if at < self.count:
             self.copy(at).start()
 
     def drain(self):
-        for at in range(len(self.bits)):
+        for at in range(self.count):
             self.copy(at).wait_send()
 
 
@@ -347,11 +390,11 @@
     prefix_ref, x_ref, gain_one, gain_two, cos_ref, sin_ref,
     grad_in, wq, wk, wv, wo, wgate, wup, wdown,
     n1_out, n2_out, g_out, qkv_out, log_out, o_own_out, o_oth_out, mid_out, scale_out, wo_from,
-    a_own_out, a_oth_out, dg_own_out, dg_oth_out, du_own_out, du_oth_out,
-    n_own, n_oth, g_own, g_oth, w_own, w_from, wo_ref, wg_ref, wu_ref, wd_ref,
+    a_own_out, a_oth_out, dg_own_out, dg_oth_out, du_own_out, du_oth_out, result_out,
+    n_own, n_oth, g_own, g_oth, w_own, w_from, wo_ref, wg_ref, wu_ref, wd_ref, wd_oth, a_ref,
     qkv_ref, vt_ref, o_own, o_oth, log_ref, part, ups, downs, total, scales, row_out, row_in, stage,
     gather_sends, gather_recvs, scatter_sends, scatter_recvs, cross_sends, cross_recvs, local_sems,
-    unit_sends, unit_recvs, unit_stores,
+    unit_sends, unit_recvs, unit_stores, down_sends, down_recvs, a_sems,
 ):
     batches, tokens, depth = x_ref.shape
     length = n * tokens
@@ -393,6 +436,7 @@
         local(wgate.at[:, lanes(c * share, share)], wg_ref.at[0]),
         local(wup.at[:, lanes(c * share, share)], wu_ref.at[0]),
         local(wdown.at[rows_at(c * share, share), :], wd_ref.at[0]),
+        local(wdown.at[rows_at((1 - c) * share, share), :], wd_oth),
     ]
     for m in range(batches):
         x = x_ref[m].astype(F32)
@@ -524,10 +568,14 @@
             stage.at[at % 2, kind], outs[kind][0].at[m, line.nearest(k)], unit_stores.at[at, kind]
         )
 
+    left = set()
+
     def unit_wait(at):
-        for kind in range(3):
-            unit_away(at, kind).wait_send()
-            unit_kept(at, kind).wait()
+        if at in left:
+            left.remove(at)
+            for kind in range(3):
+                unit_away(at, kind).wait_send()
+                unit_kept(at, kind).wait()
 
     def units(at):
         m, k = order[at]
@@ -551,9 +599,36 @@
             stage[slot, 1, :, cols] = (da * up * sigmoid * (1.0 + gate * (1.0 - sigmoid))).astype(BF16)
             stage[slot, 2, :, cols] = (da * silu).astype(BF16)
 
+        left.add(at)
         for kind in range(3):
             unit_away(at, kind).start()
             unit_kept(at, kind).start()
+
+    down_rs = Scatter(line, part.at[0], ups.at[0], downs.at[0], down_sends, down_recvs)
+
+    def down_project():
+        for k in range(n):
+            unit_wait(k)
+            unit_away(k, 0).wait_recv()
+        rs[0].drain()
+
+        def a_loads(p):
+            return [
+                pltpu.make_async_copy(src.at[0, p], a_ref.at[p % 2, side], a_sems.at[p % 2, side])
+                for side, src in enumerate((a_own_out, a_oth_out))
+            ]
+
+        for p in range(n):
+            if p == 0:
+                for copy in a_loads(0):
+                    copy.start()
+            for copy in a_loads(p):
+                copy.wait()
+            if p + 1 < n:
+                for copy in a_loads(p + 1):
+                    copy.start()
+            value = dot(a_ref[p % 2, 0], wd_ref[0], NN) + dot(a_ref[p % 2, 1], wd_oth[...], NN)
+            part[0, p] = value.astype(BF16)
 
     half = (n + 1) // 2
     o_cross = [cross(o_own.at[m], o_oth.at[m]) for m in range(batches)]
@@ -617,7 +692,8 @@
     g_loads[1].wait()
     stores += [local(g_own.at[0], g_out.at[0])]
     stores += [local(qkv_ref, qkv_out), local(log_ref, log_out)]
-    stores += [local(o_own, o_own_out), local(o_oth, o_oth_out), local(total.at[0], mid_out.at[0])]
+    stores += [local(o_own, o_own_out), local(o_oth, o_oth_out)]
+    mid_store = local(total.at[0], mid_out.at[0])
     units(0)
     for k in range(1, half):
         n2[0].step(k)
@@ -635,19 +711,28 @@
     n2[0].step(n - 1)
     units(n - 1)
     units(n)
+    down_project()
+    down_rs.step(1)
     for k in range(1, n):
         g[1].step(k)
         n2[1].step(k)
         units(n + k)
+        if k + 1 < n:
+            down_rs.step(k + 1)
     stores += [local(g_own.at[1], g_out.at[1]), local(n_own, n2_out)]
-    for at in range(2 * n - 2, 2 * n):
+    mid_store.wait()
+    total[0] = total[0] + part[0, r].astype(F32)
+    down_rs.add_received(total.at[0])
+    part[0, r] = total[0].astype(BF16)
+    stores.append(local(part.at[0, r], result_out))
+    for at in range(2 * n):
         unit_wait(at)
-    for at in range(2 * n):
         for kind in range(3):
-            unit_away(at, kind).wait_recv()
+            if at >= n or kind > 0:
+                unit_away(at, kind).wait_recv()
     for copy in crosses + w_cross + o_cross + big_cross:
         copy.wait_send()
-    for item in g + n2 + rs:
+    for item in g + n2 + rs[1:] + [down_rs]:
         item.drain()
     for copy in stores:
         copy.wait()
@@ -670,7 +755,7 @@
         ((batches, length, width), BF16), ((batches, 8, length), F32),
         ((batches, length, q_width), BF16), ((batches, length, q_width), BF16),
         ((batches, tokens, depth), F32), (rows, F32), ((q_width, depth), BF16),
-    ] + [(units, BF16)] * 6
+    ] + [(units, BF16)] * 6 + [((tokens, depth), BF16)]
     boxes = (batches, n - 1, tokens, depth)
     dma = pltpu.SemaphoreType.DMA
     return pl.pallas_call(
@@ -684,7 +769,8 @@
             pltpu.VMEM((depth, width), BF16), pltpu.VMEM((depth, width), BF16),
             pltpu.VMEM(wo.shape, BF16),
             pltpu.VMEM((2, depth, share), BF16), pltpu.VMEM((2, depth, share), BF16),
-            pltpu.VMEM((2, share, depth), BF16),
+            pltpu.VMEM((2, share, depth), BF16), pltpu.VMEM((share, depth), BF16),
+            pltpu.VMEM((2, 2, tokens, share), BF16),
             pltpu.VMEM((batches, length, width), BF16),
             pltpu.VMEM((batches, HEAD_DIM, length), BF16),
             pltpu.VMEM((batches, length, q_width), BF16), pltpu.VMEM((batches, length, q_width), BF16),
@@ -696,8 +782,9 @@
             dma((3, batches, n, 3)), dma((3, batches, n, 2)),
             dma((batches, 2, n - 1)), dma((batches, 2, n - 1)), dma((13,)), dma((13,)), dma((24,)),
             dma((batches * n, 3)), dma((batches * n, 3)), dma((batches * n, 3)),
+            dma((2, n - 1)), dma((2, n - 1)), dma((2, 2)),
         ],
-        compiler_params=communicate(1, 62),
+        compiler_params=communicate(1, 63),
         cost_estimate=cost(2e11, 100 * MIB),
     )(prefix, x, gain_one, gain_two, *tables, grad_in, wq, wk, wv, wo, wgate, wup, wdown)
 
@@ -745,7 +832,8 @@
                 )
                 copy.start() if go else copy.wait()
 
-    for copy in loads[:2] + unit_loads(0) + loads[2:]:
+    moving(0, 0, True)
+    for copy in loads[::-1] + unit_loads(0):
         copy.start()
     line.barrier(bits=bits)
     scatters = [
@@ -756,7 +844,7 @@
         Gather(
             line, dz_out.at[m], dz_oth_out.at[m], gather_sends.at[m], gather_recvs.at[m], dz_ref.at[m]
         )
-        for m in range(batches)
+        for m in range(batches - 1)
     ]
     reduces = []
     for kind, ref in enumerate((down_ref, gate_ref, up_ref)):
@@ -790,8 +878,8 @@
             value = value + dot(unit_ref[slot, 3], wu_ref[rows, cols_oth], NT)
             part[m, p, :, rows] = value.astype(BF16)
 
-    def weight_grad(kind):
-        @pl.loop(0, 2 * nb)
+    def weight_grad(kind, first=0, last=2 * nb):
+        @pl.loop(first, last)
         def _(index):
             moving(kind, index, False)
 
@@ -808,7 +896,7 @@
                 ref = gate_ref if kind == 1 else up_ref
                 ref[:, cols] = dot(shared_ref[...], moving_ref[index % 2], TN).astype(BF16)
 
-        if kind + 1 < len(kinds):
+        if last == 2 * nb and kind + 1 < len(kinds):
             moving(kind + 1, 0, True)
 
     def row_cross(m):
@@ -832,7 +920,8 @@
         )
         total[m] = result
         dz_ref[m] = result.astype(BF16)
-        gathers[m].start()
+        if m < len(gathers):
+            gathers[m].start()
         store(0, m, total.at[m], mgrad_out.at[m]).start()
         store(1, m, dz_ref.at[m], dz_out.at[m, r]).start()
 
@@ -845,40 +934,51 @@
             item.step(at)
 
     half = (n + 1) // 2
+    loads[2].wait()
+    weight_grad(0, 0, nb)
+    for way, item in enumerate(reduces[0]):
+
+        @pl.when(c == way)
+        def _(item=item):
+            item.step(0)
+
+    weight_grad(0, nb, 2 * nb)
+    for way, item in enumerate(reduces[0]):
+
+        @pl.when(c != way)
+        def _(item=item):
+            item.step(0)
+
+    n2_load = pltpu.make_async_copy(n2_in, shared_ref, load_sems.at[3])
+    n2_load.start()
     for copy in loads[:2]:
         copy.wait()
     for at in range(n):
         unit_part(at)
-    moving(0, 0, True)
     scatters[0].step(1)
-    loads[2].wait()
-    weight_grad(0)
-    reduce_step(0, 0)
-    n2_load = pltpu.make_async_copy(n2_in, shared_ref, load_sems.at[3])
-    n2_load.start()
+    n2_load.wait()
+    weight_grad(1)
+    reduce_step(1, 0)
     steps(scatters[0], 2, half + 1)
+    reduce_step(0, 1)
     for at in range(n, 2 * n):
         unit_part(at)
     steps(scatters[0], half + 1, n)
     scatters[1].step(1)
-    n2_load.wait()
-    weight_grad(1)
-    reduce_step(1, 0)
+    weight_grad(2)
+    reduce_step(2, 0)
     middle(0)
     steps(scatters[1], 2, half + 1)
-    weight_grad(2)
-    reduce_step(2, 0)
+    reduce_step(1, 1)
+    steps(gathers[0], 1, half)
     steps(scatters[1], half + 1, n)
-    steps(gathers[0], 1, half)
-    reduce_step(0, 1)
+    steps(gathers[0], half, n - 1)
+    reduce_step(2, 1)
     middle(1)
-    steps(gathers[0], half, n)
-    reduce_step(1, 1)
-    steps(gathers[1], 1, half)
-    for kind in range(3):
-        for at in range(2 if kind < 2 else 1, len(bits)):
+    steps(gathers[0], n - 1, n)
+    for at in range(2, len(bits)):
+        for kind in range(3):
             reduce_step(kind, at)
-    steps(gathers[1], half, n)
     outs = (down_out, gate_out, up_out)
     kept_stores = []
     for kind in range(3):
@@ -891,10 +991,11 @@
             )
             copy.start()
             kept_stores.append(copy)
+    for item in gathers:
+        for q in range(n):
+            item.arrive(q)
+        item.drain()
     for m in range(batches):
-        for q in range(n):
-            gathers[m].arrive(q)
-        gathers[m].drain()
         scatters[m].drain()
         row_cross(m).wait_send()
         store(0, m, total.at[m], mgrad_out.at[m]).wait()
@@ -915,7 +1016,7 @@
     gathered = (batches, n, tokens, depth)
     down_dims, gate_dims = (2 * share, depth), (depth, 2 * share)
     dims = (down_dims, gate_dims, gate_dims)
-    shapes = [(gathered, BF16), (gathered, BF16), (mid.shape, F32)]
+    shapes = [(gathered, BF16), ((batches - 1,) + gathered[1:], BF16), (mid.shape, F32)]
     shapes += [(item, BF16) for item in dims] + [((8, depth), F32)]
     boxes = (batches, n - 1, tokens, depth)
     width = min(256, share)
@@ -948,15 +1049,16 @@
 
 def backward_kernel(
     n, heads, shared_kv, bits,
-    prefix_ref, x_ref, scales_ref, gain_ref, cos_ref, sin_ref, log_ref,
-    mgrad_in, dz_own_in, dz_oth_in, wo, wo_from, wq, wk, wv, qkv_in, a_own_in, a_oth_in, wdown, n1_in,
+    prefix_ref, x_ref, scales_ref, gain_in, cos_ref, sin_ref, log_ref, ffn_gains,
+    mgrad_in, mid_in, dz_own_in, dz_oth_in, wo, wo_from, wq, wk, wv, qkv_in, a_own_in, a_oth_in, wdown, n1_in,
     o_own_in, o_oth_in, down_in, gate_in, up_in,
-    grad_out, sum_out, qkv_out, o_out, down_out, gate_out, up_out, gain_out,
-    dz_ref, dz_oth, wo_ref, w_own, w_oth, qkv_ref, dk_ref, dv_ref, kt_ref, dqkv_own, dqkv_oth,
+    grad_out, result_out, qkv_out, o_out, down_out, gate_out, up_out, gain_out,
+    dz_ref, dz_oth, dz_last, wo_ref, w_own, w_oth, qkv_ref, dk_ref, dv_ref, kt_ref, dqkv_own, dqkv_oth,
     part, ups, downs, total, mgrad_ref, a_ref, wide_ref, o_ref, qkv_grad, o_grad, qkv_sum, o_sum, boxes,
-    row_out, row_in,
+    row_out, row_in, result_ref, gain_ref, row_boxes, dp_boxes,
     load_sems, dz_sems, a_sems, scatter_sends, scatter_recvs, cross_sends, cross_recvs, store_sems,
     reduce_sends, reduce_recvs, spread_sends, spread_recvs, unit_sends, unit_recvs,
+    gather_sends, gather_recvs, gain_sends, gain_recvs,
 ):
     batches, tokens, depth = x_ref.shape
     length = n * tokens
@@ -983,12 +1085,17 @@
 
     pairs = [(wdown, wide_ref.at[pl.ds(0, 2 * share), :]), (qkv_in, qkv_ref)]
     pairs += [(wo.at[rows_at(c * q_width, q_width), :], wo_ref.at[0]), (wo_from, wo_ref.at[1])]
-    pairs += [(dz_own_in, dz_ref)]
+    last = batches - 1
+    pairs += [(dz_own_in.at[m], dz_ref.at[m]) for m in range(last)]
     first = len(pairs)
     pairs += qkv_columns(c, w_own) + qkv_columns(1 - c, w_oth)
     pairs += [(o_own_in, o_ref.at[0]), (o_oth_in, o_ref.at[1]), (mgrad_in, mgrad_ref)]
+    pairs += [(mid_in.at[last], total.at[last])]
     loads = [pltpu.make_async_copy(a, b, load_sems.at[i]) for i, (a, b) in enumerate(pairs)]
     n1_load = pltpu.make_async_copy(n1_in, wide_ref.at[pl.ds(0, batches * length), :], load_sems.at[len(pairs)])
+    shard_load = pltpu.make_async_copy(
+        dz_own_in.at[last, r], dz_ref.at[last, r], load_sems.at[len(pairs) + 1]
+    )
     order = [(m, p) for m in range(batches) for p in range(n)]
 
     def a_loads(at):
@@ -1002,23 +1109,27 @@
         m, p = order[at]
         return pltpu.make_async_copy(dz_oth_in.at[m, p], dz_oth.at[at % 2], dz_sems.at[at % 2])
 
-    for copy in loads[:1] + a_loads(0) + loads[1:first] + [dz_load(0)] + loads[first:]:
+    for copy in [shard_load] + loads[:1] + a_loads(last * n) + loads[1:first] + [dz_load(0)] + loads[first:]:
         copy.start()
-    line.barrier(bits=bits)
+    dp_count = 2 ** len(bits)
+    line.wide_barrier(dp_count)
+    gains = [
+        Everywhere(line, "row", r, n, gain_ref.at[0], row_boxes, gain_sends.at[0], gain_recvs.at[0]),
+        Everywhere(line, "dp", line.d, dp_count, gain_ref.at[1], dp_boxes, gain_sends.at[1], gain_recvs.at[1]),
+    ]
+    gather = Gather(line, dz_ref.at[last], dz_last, gather_sends, gather_recvs)
     spreads = [
-        Spread(line, view, way_bits, unit_sends.at[kind, way], unit_recvs.at[kind, way])
+        Spread(
+            line, view, way_bits, unit_sends.at[kind, way], unit_recvs.at[kind, way], skip=int(kind == 2)
+        )
         for kind, ref in enumerate((down_out, gate_out, up_out))
         for way, (view, way_bits) in enumerate(two_ways(ref, bits))
     ]
-    out_rs, head_rs = (
-        [
-            Scatter(
-                line, part.at[m], ups.at[which, m], downs.at[which, m],
-                scatter_sends.at[which, m], scatter_recvs.at[which, m],
-            )
-            for m in range(batches)
-        ]
-        for which in range(2)
+    *head_rs, out_rs = (
+        Scatter(
+            line, part.at[min(at, last)], ups.at[at], downs.at[at], scatter_sends.at[at], scatter_recvs.at[at]
+        )
+        for at in range(batches + 1)
     )
     reduces, gatherers = [], []
     for kind, (ref, result) in enumerate(((qkv_grad, qkv_sum), (o_grad, o_sum))):
@@ -1044,9 +1155,10 @@
             if at >= count:
                 gatherers[item].step(at - count)
 
-    def spread_step(at):
-        for item in spreads:
-            item.step(at)
+    def spread_step(which, at):
+        for kind in which:
+            for item in spreads[2 * kind : 2 * kind + 2]:
+                item.step(at)
 
     own_rows, oth_rows = rows_at(c * share, share), rows_at((1 - c) * share, share)
 
@@ -1077,12 +1189,16 @@
 
     def attend_back(m, q):
         at = m * n + q
-        dz_load(at).wait()
-        if at + 1 < len(order):
-            dz_load(at + 1).start()
+        if m < last:
+            dz_load(at).wait()
+            if at + 1 < last * n:
+                dz_load(at + 1).start()
+        else:
+            gather.arrive(q)
+        other = dz_oth[at % 2] if m < last else dz_last[q]
         rows = pl.ds(q * tokens, tokens)
         grads = dot(dz_ref[m, q], wo_ref[0], NT)
-        grads = (grads + dot(dz_oth[at % 2], wo_ref[1], NT)).astype(BF16)
+        grads = (grads + dot(other, wo_ref[1], NT)).astype(BF16)
         cosine, signed = cos_ref[rows, :], sin_ref[rows, :]
         extent = min(length, max((q + 1) * tokens, PREFIX_TOP))
         upto = pl.ds(0, extent)
@@ -1120,17 +1236,19 @@
             value = dot(dqkv_own[m, rows, :], w_own[...], NT)
             part[m, p] = (value + dot(dqkv_oth[m, rows, :], w_oth[...], NT)).astype(BF16)
 
-    def out_total(m):
-        out_rs[m].total(total.at[m])
-        store(0, m, total.at[m], sum_out.at[m]).start()
+    def result():
+        total[last] = total[last] + part[last, r].astype(F32)
+        out_rs.add_received(total.at[last])
+        out_rs.drain()
+        result_ref[...] = total[last].astype(BF16)
+        store(0, 0, result_ref, result_out).start()
 
     def input_grad(m):
-        store(0, m, total.at[m], sum_out.at[m]).wait()
         head_rs[m].total(total.at[m])
         s = scales_ref[0, m][:, :1]
         x = x_ref[m].astype(F32)
-        gain_out[pl.ds(m, 1), :] = jnp.sum(total[m] * x * s, axis=0, keepdims=True)
-        total[m] = total[m] * gain_ref[...]
+        gain_ref[0, pl.ds(m, 1), :] = jnp.sum(total[m] * x * s, axis=0, keepdims=True)
+        total[m] = total[m] * gain_in[...]
         inner = jnp.sum(total[m] * x, axis=1, keepdims=True)
         row_out[m] = jnp.broadcast_to(inner, (tokens, 128))
         row_cross(m).start()
@@ -1144,43 +1262,46 @@
             item.step(s)
 
     half = (n + 1) // 2
-    spread_step(0)
-    loads[0].wait()
-    for at in range(n):
-        down_part(at)
-    out_rs[0].step(1)
+    spread_step((0, 1, 2), 0)
+    shard_load.wait()
+    gather.start()
     for copy in loads[1:first]:
         copy.wait()
     attend_start(0)
-    for q in range(n // 2):
-        attend_back(0, q)
-    steps(out_rs[0], 2, half + 1)
-    for q in range(n // 2, n):
+    for q in range(n):
         attend_back(0, q)
     attend_end(0)
-    for at in range(n, 2 * n):
+    steps(gather, 1, half)
+    loads[0].wait()
+    for at in range(last * n, len(order)):
         down_part(at)
+    out_rs.step(1)
     n1_load.start()
-    steps(out_rs[0], half + 1, n)
-    out_rs[1].step(1)
-    for at in range(1, count):
-        spread_step(at)
+    steps(gather, half, n - 1)
     for copy in loads[first:]:
         copy.wait()
-    out_total(0)
-    out_rs[0].drain()
     head_part(0)
     head_rs[0].step(1)
+    for at in range(1, count):
+        spread_step((0,), at)
+    steps(gather, n - 1, n)
+    steps(out_rs, 2, half + 1)
+    for side in range(2):
+        place = c if side == 0 else 1 - c
+        value = dot(o_ref[side], dz_ref[...].reshape(batches * length, depth), TN)
+        o_grad[rows_at(place * q_width, q_width), :] = value.astype(BF16)
+    total_step((2, 3), 0)
     attend_start(1)
     for q in range(n // 2):
         attend_back(1, q)
-    steps(out_rs[1], 2, half + 1)
     steps(head_rs[0], 2, half + 1)
+    for at in range(1, count):
+        spread_step((1,), at)
     for q in range(n // 2, n):
         attend_back(1, q)
     attend_end(1)
-    steps(out_rs[1], half + 1, n)
-    steps(head_rs[0], half + 1, n)
+    steps(out_rs, half + 1, n)
+    total_step((2, 3), 1)
     n1_load.wait()
     grad_cross(1).wait_recv()
     for side in range(2):
@@ -1189,8 +1310,8 @@
         value = dot(wide_ref[pl.ds(0, batches * length), :], dqkv, TN)
         qkv_grad[:, lanes(place * width, width)] = value.astype(BF16)
     total_step((0, 1), 0)
-    out_total(1)
-    out_rs[1].drain()
+    steps(head_rs[0], half + 1, n)
+    result()
 
     @pl.loop(0, n)
     def _(p):
@@ -1199,21 +1320,24 @@
         part[1, p] = (value + dot(dqkv_oth[1, rows, :], w_oth[...], NT)).astype(BF16)
 
     head_rs[1].step(1)
-    for side in range(2):
-        place = c if side == 0 else 1 - c
-        value = dot(o_ref[side], dz_ref[...].reshape(batches * length, depth), TN)
-        o_grad[rows_at(place * q_width, q_width), :] = value.astype(BF16)
-    total_step((2, 3), 0)
+    total_step((2, 3), 2)
     input_grad(0)
-    turn, last_turn = 1, 2 * count
+    total_step((0, 1), 1)
+    turn, last_turn = 2, 2 * count
     for s in range(2, n):
         head_rs[1].step(s)
         if turn <= last_turn:
-            total_step((0, 1, 2, 3), turn)
+            total_step((0, 1), turn)
+        if turn + 1 <= last_turn:
+            total_step((2, 3), turn + 1)
         turn += 1
     input_grad(1)
+    gain_ref[0, pl.ds(batches, batches), :] = ffn_gains[pl.ds(0, batches), :]
+    gains[0].start()
     while turn <= last_turn:
-        total_step((0, 1, 2, 3), turn)
+        total_step((0, 1), turn)
+        if turn + 1 <= last_turn:
+            total_step((2, 3), turn + 1)
         turn += 1
     stores = [
         pltpu.make_async_copy(qkv_sum, qkv_out, load_sems.at[0]),
@@ -1221,12 +1345,21 @@
     ]
     for copy in stores:
         copy.start()
-    spread_step(count)
+    gain_ref[1] = gains[0].total()
+    gains[1].start()
+    for at in range(1, count):
+        spread_step((2,), at)
+    spread_step((0, 1, 2), count)
     for m in range(batches):
         grad_cross(m).wait_send()
         row_cross(m).wait_send()
         head_rs[m].drain()
         store(1, m, total.at[m], grad_out.at[m]).wait()
+    store(0, 0, result_ref, result_out).wait()
+    gather.drain()
+    gain_out[...] = gains[1].total()
+    for item in gains:
+        item.drain()
     for item in spreads + reduces + gatherers:
         item.drain()
     for copy in stores:
@@ -1234,7 +1367,7 @@
 
 
 def backward(
-    prefix, x, scales, gain, tables, logs, mgrad, dz_own, dz_oth, wo, wo_from, wq, wk, wv, qkv,
+    prefix, x, scales, gain, tables, logs, ffn_gains, mgrad, mid, dz_own, dz_oth, wo, wo_from, wq, wk, wv, qkv,
     a_own, a_oth, wdown, n1, o_own, o_oth, down, gate, up, heads, shared_kv, dp_count,
 ):
     batches, tokens, depth = x.shape
@@ -1246,19 +1379,19 @@
     vmem = pl.BlockSpec(memory_space=pltpu.VMEM)
     anywhere = pl.BlockSpec(memory_space=pl.ANY)
     gathered = (batches, n, tokens, depth)
-    boxes = (2, batches, n - 1, tokens, depth)
+    boxes = (batches + 1, n - 1, tokens, depth)
     sums = [(depth, 2 * width), (2 * q_width, depth)]
-    shapes = [(mgrad.shape, F32), (mgrad.shape, F32)] + [(item, BF16) for item in sums]
+    shapes = [(mgrad.shape, F32), ((tokens, depth), BF16)] + [(item, BF16) for item in sums]
     shapes += [(item.shape, BF16) for item in (down, gate, up)] + [((8, depth), F32)]
     dma = pltpu.SemaphoreType.DMA
     return pl.pallas_call(
         functools.partial(backward_kernel, n, heads, shared_kv, bits),
-        in_specs=[pl.BlockSpec(memory_space=pltpu.SMEM)] + [vmem] * 6 + [anywhere] * 18,
+        in_specs=[pl.BlockSpec(memory_space=pltpu.SMEM)] + [vmem] * 7 + [anywhere] * 19,
         out_specs=[anywhere] * 7 + [vmem],
         out_shape=[jax.ShapeDtypeStruct(*item) for item in shapes],
-        input_output_aliases={22: 4, 23: 5, 24: 6},
+        input_output_aliases={24: 4, 25: 5, 26: 6},
         scratch_shapes=[
-            pltpu.VMEM(gathered, BF16), pltpu.VMEM((2, tokens, depth), BF16),
+            pltpu.VMEM(gathered, BF16), pltpu.VMEM((2, tokens, depth), BF16), pltpu.VMEM(gathered[1:], BF16),
             pltpu.VMEM((2, q_width, depth), BF16),
             pltpu.VMEM((depth, width), BF16), pltpu.VMEM((depth, width), BF16),
             pltpu.VMEM(qkv.shape, BF16),
@@ -1275,28 +1408,36 @@
                 for item in sums
             ],
             pltpu.VMEM((batches, tokens, 128), F32), pltpu.VMEM((batches, tokens, 128), F32),
-            dma((15,)), dma((2,)), dma((2, 2)),
-            dma((2, batches, 2, n - 1)), dma((2, batches, 2, n - 1)),
+            pltpu.VMEM((tokens, depth), BF16), pltpu.VMEM((2, 8, depth), F32),
+            pltpu.VMEM((n - 1, 8, depth), F32), pltpu.VMEM((dp_count - 1, 8, depth), F32),
+            dma((20,)), dma((2,)), dma((2, 2)),
+            dma((batches + 1, 2, n - 1)), dma((batches + 1, 2, n - 1)),
             dma((2 * batches,)), dma((2 * batches,)), dma((2, batches)),
             dma((2, 2, len(bits))), dma((2, 2, len(bits))), dma((2, 2, len(bits))), dma((2, 2, len(bits))),
-            dma((3, 2, len(bits))), dma((3, 2, len(bits))),
+            dma((3, 2, len(bits))), dma((3, 2, len(bits))), dma((n, 3)), dma((n, 2)),
+            dma((2, max(n, dp_count) - 1)), dma((2, max(n, dp_count) - 1)),
         ],
         compiler_params=communicate(3, 62),
         cost_estimate=cost(2e11, 100 * MIB),
     )(
-        prefix, x, scales, gain, *tables, logs, mgrad, dz_own, dz_oth, wo, wo_from, wq, wk, wv, qkv,
+        prefix, x, scales, gain, *tables, logs, ffn_gains, mgrad, mid, dz_own, dz_oth, wo, wo_from, wq, wk, wv, qkv,
         a_own, a_oth, wdown, n1, o_own, o_oth, down, gate, up,
     )
 
 
-def butterfly(values, axes):
-    for axis in axes:
-        n = lax.axis_size(axis)
-        reach = 1
-        while reach < n:
-            values = values + lax.ppermute(values, axis, [(i, i ^ reach) for i in range(n)])
-            reach *= 2
-    return values
+def last_spread(values, meanwhile):
+    count = lax.axis_size("dp")
+    half = values.shape[0] // 2
+    size, sides, halves = half // 2, [], []
+    for way, bit in enumerate((0, count.bit_length() - 2)):
+        sides.append((lax.axis_index("dp") >> bit) & 1)
+        own = lax.dynamic_slice_in_dim(values, way * half + sides[-1] * size, size, 0)
+        halves.append((own, lax.ppermute(own, "dp", [(i, i ^ (1 << bit)) for i in range(count)])))
+    halves, meanwhile = lax.optimization_barrier((halves, meanwhile))
+    pieces = []
+    for side, (own, got) in zip(sides, halves):
+        pieces += [jnp.where(side == 0, own, got), jnp.where(side == 0, got, own)]
+    return jnp.concatenate([piece.astype(F32) for piece in pieces]), meanwhile
 
 
 def body(
@@ -1323,7 +1464,7 @@
     tables = rope_tables(length)
     (
         n1, n2, g_own, qkv, logs, o_own, o_oth, middle, scales, out_from,
-        a_own, a_oth, dg_own, dg_oth, du_own, du_oth,
+        a_own, a_oth, dg_own, dg_oth, du_own, du_oth, first_result,
     ) = forward(
         prefix_len, hidden_in, attn_gain.reshape(1, -1), ffn_gain.reshape(1, -1), tables, out_grad,
         query_weight, key_weight, value_weight, output_weight, gate_weight, up_weight, down_weight,
@@ -1339,14 +1480,12 @@
         middle, scales, out_grad, ffn_gain.reshape(1, -1), *flat(g_own, n2), (a_own, a_oth, *grads),
         gate_weight, up_weight, row_count, dp_count,
     )
-    in_grad, down_part, qkv_sum, output_sum, down_sum, gate_sum, up_sum, attn_gains = backward(
-        prefix_len, hidden_in, scales, attn_gain.reshape(1, -1), tables, logs, middle_grad, dz, dz_oth,
-        output_weight, out_from, query_weight, key_weight, value_weight, qkv, a_own, a_oth, down_weight,
+    in_grad, last_result, qkv_sum, output_sum, down_sum, gate_sum, up_sum, gains = backward(
+        prefix_len, hidden_in, scales, attn_gain.reshape(1, -1), tables, logs, ffn_gains, middle_grad,
+        middle, dz, dz_oth, output_weight, out_from, query_weight, key_weight, value_weight, qkv, a_own, a_oth, down_weight,
         *flat(n1, o_own, o_oth), down_sum, gate_sum, up_sum, heads, shared_kv, dp_count,
     )
-    result = (middle + down_part).astype(BF16)
-    attn_gain_acc = attn_gains[:batches].sum(axis=0)
-    ffn_gain_acc = ffn_gains[:batches].sum(axis=0)
+    result = jnp.stack([first_result, last_result])
     width = q_width + 2 * HEAD_DIM
 
     def columns(first, size, shared):
@@ -1356,8 +1495,8 @@
         ]
         return sum(pieces) if shared else jnp.concatenate(pieces, axis=1)
 
-    gain_one, gain_two = butterfly(jnp.stack([attn_gain_acc, ffn_gain_acc]), ("dp", "row"))
-    return (
+    gain_one, gain_two = gains[:batches].sum(axis=0), gains[batches : 2 * batches].sum(axis=0)
+    meanwhile = (
         result,
         in_grad,
         gain_one,
@@ -1367,9 +1506,10 @@
         columns(q_width + HEAD_DIM, HEAD_DIM, shared_kv),
         output_sum.astype(F32),
         gate_sum.astype(F32),
-        up_sum.astype(F32),
         down_sum.astype(F32),
     )
+    up_sum, (*first, down_sum) = last_spread(up_sum, meanwhile)
+    return (*first, up_sum, down_sum)
 
 
 def solution(mesh):

time: 635 us -> 573 us (0.902)
  Pallas kernels: 591 us -> 529 us
    pallas_call x1, Pallas kernels: 163 us -> 128 us  [unit_grads(): pl.pallas_call(functools.partial(unit_grads_kernel, n, bits), in_specs=[v...]
    pallas_call x1, Pallas kernels: 173 us -> 143 us  [backward(): pl.pallas_call(functools.partial(backward_kernel, n, heads, shared_kv, bi...]
    convert_element_type x2 -> x0, other arithmetic: 7.96 us -> none  [the longest x1 4.45 us: body(): up_sum.astype(F32)]
  transfers between devices with their start and end apart: 4 -> 2, of which waited for: 2 -> 2; matrix products, arithmetic and copies ran while one was open for 4% -> 3% of each run, Pallas kernels for 0% -> 0%
where the time goes in v4:
time: 573 us; the launch traced here: 564 us
  Pallas kernels  529 us (92%)
  other arithmetic  23 us (4%)
    pallas_call x1, Pallas kernels, forward(): pl.pallas_call(functools.partial(forward_kernel, n, heads, shared_kv), in...  258 us
    pallas_call x1, Pallas kernels, backward(): pl.pallas_call(functools.partial(backward_kernel, n, heads, shared_kv, bi...  143 us
    pallas_call x1, Pallas kernels, unit_grads(): pl.pallas_call(functools.partial(unit_grads_kernel, n, bits), in_specs=[v...  128 us
  transfers between devices with their start and end apart: 2, of which 2 were waited for; matrix products, arithmetic and copies ran while one was open for 3% of the time, Pallas kernels for 0%

profile of v4, /device:TPU:0, one launch (start us, length us, event | category | flops | bytes accessed | tf_op | source)
XLA Modules:
  0.0 564.2 jit_solution(6482745536710381041)
XLA Ops:
  0.6 1.3 copy.29.prefix_ref
  1.9 258.0 %shard_map.221 = (bf16[2,4,256,1024]{3,2,1,0:T(8,128)(2,1)}, bf16[2,4,256,1024]{3,2,1,0:T(8,128)(2,1)}, bf16[2,4,256,1024]{3,2,1,0:T(8,128)(2,1)}, bf16[2,1024,5...) custom-call(s32[2,1]{1,0:T(2,128)} %copy.29.prefix_ref, ...), custom_call_target="tpu_custom_call" | custom-call | flops 199999995904 | bytes 104857600 | tf_op jit(solution)/shard_map/pallas_call | solution.py:761
  259.9 128.3 %shard_map.222 = (bf16[2,4,256,1024]{3,2,1,0:T(8,128)(2,1)}, bf16[1,4,256,1024]{3,2,1,0:T(8,128)(2,1)}, f32[2,256,1024]{2,1,0:T(8,128)}, bf16[2048,1024]{1,0:T(8...) custom-call(f32[2,256,1024]{2,1,0:T(8,128)} %get-tuple-element.59.mid_ref.mid_in, ...), custom_call_target="tpu_custom_call" | custom-call | flops 199999995904 | bytes 104857600 | tf_op jit(solution)/shard_map/pallas_call | solution.py:1024
  388.2 142.7 %shard_map.223 = (f32[2,256,1024]{2,1,0:T(8,128)}, bf16[256,1024]{1,0:T(8,128)(2,1)}, bf16[1024,1024]{1,0:T(8,128)(2,1)}, bf16[512,1024]{1,0:T(8,128)(2,1)}, bf1...) custom-call(s32[2,1]{1,0:T(2,128)} %copy.29.prefix_ref, ...), custom_call_target="tpu_custom_call", output_to_operand_aliasing={{4}: (24, {}), {5}: (25, {}), {6}: (26, {})} | custom-call | flops 199999995904 | bytes 104857600 | tf_op jit(solution)/shard_map/pallas_call | solution.py:1387
  530.9 1.7 constant_dynamic-slice_fusion
  532.6 1.0 collective-permute-start
  533.6 1.4 collective-permute-start.1
  535.0 6.8 %convert_element_type.7 = f32[1024,2048]{1,0:T(8,128)} convert(bf16[1024,2048]{1,0:T(8,128)(2,1)} %get-tuple-element.87) | non-fusion elementwise | flops 2097152 | bytes 12582912 | tf_op jit(solution)/shard_map/convert_element_type | solution.py:1508
  541.8 0.0 copy-start.5
  541.8 4.4 convert_element_type.8
  546.3 1.6 convert_element_type.6
  547.8 0.0 copy-done.6
  547.8 0.6 slice_reduce_fusion
  548.4 1.1 pad_maximum_fusion
  549.5 0.1 fusion.1
  549.6 1.6 maximum_convert_fusion.1
  551.2 0.2 fusion
  551.4 1.5 maximum_convert_fusion.2
  552.8 3.9 collective-permute-done
  556.8 0.5 collective-permute-done.1
  557.2 1.4 broadcast_select_fusion.3
  558.6 0.1 broadcast_select_fusion.1
  558.8 3.9 maximum_convert_fusion
  562.7 1.3 copy.34
  (12 shorter events, 0.0 us)
Async XLA Ops:
  532.6 24.1 %collective-permute-start = (bf16[256,2048]{1,0:T(8,128)(2,1)S(1)}, bf16[256,2048]{1,0:T(8,128)(2,1)}, u32[]{:S(2)}, u32[]{:S(2)}) collective-permute-start(bf16[256,2048]{1,0:T(8,128)(2,1)S(1)} %get-tuple-element.98), channel_id=1, source_target_pairs={{0,8},{8,0},{16,24},{24,16},{1,9},{9,1},{17,25},{25,17},{2,10},{10... | collective-permute-start | bytes 3145736 | tf_op jit(solution)/shard_map/ppermute | solution.py:1435
  533.6 23.7 %collective-permute-start.1 = (bf16[256,2048]{1,0:T(8,128)(2,1)S(1)}, bf16[256,2048]{1,0:T(8,128)(2,1)S(1)}, u32[]{:S(2)}, u32[]{:S(2)}) collective-permute-start(bf16[256,2048]{1,0:T(8,128)(2,1)S(1)} %get-tuple-element.100), channel_id=1, source_target_pairs={{0,16},{8,24},{16,0},{24,8},{1,17},{9,25},{17,1},{25,9},{2,18},{10... | collective-permute-start | bytes 3145736 | tf_op jit(solution)/shard_map/ppermute | solution.py:1435
  535.0 6.8 %copy-start = (bf16[2048,1024]{1,0:T(8,128)(2,1)S(1)}, bf16[2048,1024]{1,0:T(8,128)(2,1)}, u32[]{:S(2)}) copy-start(bf16[2048,1024]{1,0:T(8,128)(2,1)} %get-tuple-element.88) | copy-start | bytes 12582916
  541.8 4.5 copy-start.3
  541.8 6.0 %copy-start.6 = (f32[8,1024]{1,0:T(8,128)S(1)}, f32[8,1024]{1,0:T(8,128)}, u32[]{:S(2)}) copy-start(f32[8,1024]{1,0:T(8,128)} %get-tuple-element.84) | copy-start | bytes 98308
  541.8 6.6 %copy-start.4 = (bf16[256,1024]{1,0:T(8,128)(2,1)S(1)}, bf16[256,1024]{1,0:T(8,128)(2,1)}, u32[]{:S(2)}) copy-start(bf16[256,1024]{1,0:T(8,128)(2,1)} %get-tuple-element.81) | copy-start | bytes 1572868
  541.8 6.6 %copy-start.5 = (bf16[256,1024]{1,0:T(8,128)(2,1)S(1)}, bf16[256,1024]{1,0:T(8,128)(2,1)}, u32[]{:S(2)}) copy-start(bf16[256,1024]{1,0:T(8,128)(2,1)} %get-tuple-element.82) | copy-start | bytes 1572868
  546.3 3.3 copy-start.2
  558.8 3.9 copy-start.1

commit v5 on v4

--- a/solution.py
+++ b/solution.py
@@ -1050,11 +1050,11 @@
 def backward_kernel(
     n, heads, shared_kv, bits,
     prefix_ref, x_ref, scales_ref, gain_in, cos_ref, sin_ref, log_ref, ffn_gains,
-    mgrad_in, mid_in, dz_own_in, dz_oth_in, wo, wo_from, wq, wk, wv, qkv_in, a_own_in, a_oth_in, wdown, n1_in,
+    mid_in, dz_own_in, dz_oth_in, wo, wo_from, wq, wk, wv, qkv_in, a_own_in, a_oth_in, wdown, n1_in,
     o_own_in, o_oth_in, down_in, gate_in, up_in,
     grad_out, result_out, qkv_out, o_out, down_out, gate_out, up_out, gain_out,
     dz_ref, dz_oth, dz_last, wo_ref, w_own, w_oth, qkv_ref, dk_ref, dv_ref, kt_ref, dqkv_own, dqkv_oth,
-    part, ups, downs, total, mgrad_ref, a_ref, wide_ref, o_ref, qkv_grad, o_grad, qkv_sum, o_sum, boxes,
+    part, ups, downs, total, a_ref, wide_ref, o_ref, qkv_grad, o_grad, qkv_sum, o_sum, boxes,
     row_out, row_in, result_ref, gain_ref, row_boxes, dp_boxes,
     load_sems, dz_sems, a_sems, scatter_sends, scatter_recvs, cross_sends, cross_recvs, store_sems,
     reduce_sends, reduce_recvs, spread_sends, spread_recvs, unit_sends, unit_recvs,
@@ -1089,7 +1089,7 @@
     pairs += [(dz_own_in.at[m], dz_ref.at[m]) for m in range(last)]
     first = len(pairs)
     pairs += qkv_columns(c, w_own) + qkv_columns(1 - c, w_oth)
-    pairs += [(o_own_in, o_ref.at[0]), (o_oth_in, o_ref.at[1]), (mgrad_in, mgrad_ref)]
+    pairs += [(o_own_in, o_ref.at[0]), (o_oth_in, o_ref.at[1])]
     pairs += [(mid_in.at[last], total.at[last])]
     loads = [pltpu.make_async_copy(a, b, load_sems.at[i]) for i, (a, b) in enumerate(pairs)]
     n1_load = pltpu.make_async_copy(n1_in, wide_ref.at[pl.ds(0, batches * length), :], load_sems.at[len(pairs)])
@@ -1127,7 +1127,7 @@
     ]
     *head_rs, out_rs = (
         Scatter(
-            line, part.at[min(at, last)], ups.at[at], downs.at[at], scatter_sends.at[at], scatter_recvs.at[at]
+            line, part.at[at], ups.at[at], downs.at[at], scatter_sends.at[at], scatter_recvs.at[at]
         )
         for at in range(batches + 1)
     )
@@ -1170,7 +1170,7 @@
             for copy in a_loads(at + 1):
                 copy.start()
         value = dot(a_ref[at % 2, 0], wide_ref[own_rows, :], NN)
-        part[m, p] = (value + dot(a_ref[at % 2, 1], wide_ref[oth_rows, :], NN)).astype(BF16)
+        part[batches, p] = (value + dot(a_ref[at % 2, 1], wide_ref[oth_rows, :], NN)).astype(BF16)
 
     def grad_cross(m):
         return line.across(dqkv_own.at[m], dqkv_oth.at[m], cross_sends.at[m], cross_recvs.at[m])
@@ -1237,9 +1237,8 @@
             part[m, p] = (value + dot(dqkv_oth[m, rows, :], w_oth[...], NT)).astype(BF16)
 
     def result():
-        total[last] = total[last] + part[last, r].astype(F32)
+        total[last] = total[last] + part[batches, r].astype(F32)
         out_rs.add_received(total.at[last])
-        out_rs.drain()
         result_ref[...] = total[last].astype(BF16)
         store(0, 0, result_ref, result_out).start()
 
@@ -1254,7 +1253,7 @@
         row_cross(m).start()
         row_cross(m).wait_recv()
         inner = row_out[m, :, pl.ds(0, 1)] + row_in[m, :, pl.ds(0, 1)]
-        total[m] = mgrad_ref[m] + total[m] * s - x * ((s * s * s) * inner * (1.0 / WIDTH))
+        total[m] = total[m] * s - x * ((s * s * s) * inner * (1.0 / WIDTH))
         store(1, m, total.at[m], grad_out.at[m]).start()
 
     def steps(item, first_step, last_step):
@@ -1267,16 +1266,18 @@
     gather.start()
     for copy in loads[1:first]:
         copy.wait()
-    attend_start(0)
-    for q in range(n):
-        attend_back(0, q)
-    attend_end(0)
-    steps(gather, 1, half)
     loads[0].wait()
     for at in range(last * n, len(order)):
         down_part(at)
     out_rs.step(1)
     n1_load.start()
+    attend_start(0)
+    for q in range(n // 2):
+        attend_back(0, q)
+    steps(gather, 1, half)
+    for q in range(n // 2, n):
+        attend_back(0, q)
+    attend_end(0)
     steps(gather, half, n - 1)
     for copy in loads[first:]:
         copy.wait()
@@ -1302,8 +1303,9 @@
     attend_end(1)
     steps(out_rs, half + 1, n)
     total_step((2, 3), 1)
+    head_part(1)
+    head_rs[1].step(1)
     n1_load.wait()
-    grad_cross(1).wait_recv()
     for side in range(2):
         place = c if side == 0 else 1 - c
         dqkv = (dqkv_own if side == 0 else dqkv_oth)[...].reshape(batches * length, width)
@@ -1312,14 +1314,6 @@
     total_step((0, 1), 0)
     steps(head_rs[0], half + 1, n)
     result()
-
-    @pl.loop(0, n)
-    def _(p):
-        rows = rows_at(p * tokens, tokens)
-        value = dot(dqkv_own[1, rows, :], w_own[...], NT)
-        part[1, p] = (value + dot(dqkv_oth[1, rows, :], w_oth[...], NT)).astype(BF16)
-
-    head_rs[1].step(1)
     total_step((2, 3), 2)
     input_grad(0)
     total_step((0, 1), 1)
@@ -1355,6 +1349,7 @@
         row_cross(m).wait_send()
         head_rs[m].drain()
         store(1, m, total.at[m], grad_out.at[m]).wait()
+    out_rs.drain()
     store(0, 0, result_ref, result_out).wait()
     gather.drain()
     gain_out[...] = gains[1].total()
@@ -1367,7 +1362,7 @@
 
 
 def backward(
-    prefix, x, scales, gain, tables, logs, ffn_gains, mgrad, mid, dz_own, dz_oth, wo, wo_from, wq, wk, wv, qkv,
+    prefix, x, scales, gain, tables, logs, ffn_gains, mid, dz_own, dz_oth, wo, wo_from, wq, wk, wv, qkv,
     a_own, a_oth, wdown, n1, o_own, o_oth, down, gate, up, heads, shared_kv, dp_count,
 ):
     batches, tokens, depth = x.shape
@@ -1381,15 +1376,15 @@
     gathered = (batches, n, tokens, depth)
     boxes = (batches + 1, n - 1, tokens, depth)
     sums = [(depth, 2 * width), (2 * q_width, depth)]
-    shapes = [(mgrad.shape, F32), ((tokens, depth), BF16)] + [(item, BF16) for item in sums]
+    shapes = [(mid.shape, F32), ((tokens, depth), BF16)] + [(item, BF16) for item in sums]
     shapes += [(item.shape, BF16) for item in (down, gate, up)] + [((8, depth), F32)]
     dma = pltpu.SemaphoreType.DMA
     return pl.pallas_call(
         functools.partial(backward_kernel, n, heads, shared_kv, bits),
-        in_specs=[pl.BlockSpec(memory_space=pltpu.SMEM)] + [vmem] * 7 + [anywhere] * 19,
+        in_specs=[pl.BlockSpec(memory_space=pltpu.SMEM)] + [vmem] * 7 + [anywhere] * 18,
         out_specs=[anywhere] * 7 + [vmem],
         out_shape=[jax.ShapeDtypeStruct(*item) for item in shapes],
-        input_output_aliases={24: 4, 25: 5, 26: 6},
+        input_output_aliases={23: 4, 24: 5, 25: 6},
         scratch_shapes=[
             pltpu.VMEM(gathered, BF16), pltpu.VMEM((2, tokens, depth), BF16), pltpu.VMEM(gathered[1:], BF16),
             pltpu.VMEM((2, q_width, depth), BF16),
@@ -1397,8 +1392,8 @@
             pltpu.VMEM(qkv.shape, BF16),
             pltpu.VMEM((length, HEAD_DIM), F32), pltpu.VMEM((length, HEAD_DIM), F32),
             pltpu.VMEM((HEAD_DIM, length), BF16), pltpu.VMEM(qkv.shape, BF16), pltpu.VMEM(qkv.shape, BF16),
-            pltpu.VMEM(gathered, BF16), pltpu.VMEM(boxes, BF16), pltpu.VMEM(boxes, BF16),
-            pltpu.VMEM(mgrad.shape, F32), pltpu.VMEM(mgrad.shape, F32),
+            pltpu.VMEM((batches + 1,) + gathered[1:], BF16), pltpu.VMEM(boxes, BF16), pltpu.VMEM(boxes, BF16),
+            pltpu.VMEM(mid.shape, F32),
             pltpu.VMEM((2, 2, tokens, share), BF16),
             pltpu.VMEM((max(2 * share, rows), depth), BF16), pltpu.VMEM((2, rows, q_width), BF16),
             pltpu.VMEM(sums[0], BF16), pltpu.VMEM(sums[1], BF16),
@@ -1420,7 +1415,7 @@
         compiler_params=communicate(3, 62),
         cost_estimate=cost(2e11, 100 * MIB),
     )(
-        prefix, x, scales, gain, *tables, logs, ffn_gains, mgrad, mid, dz_own, dz_oth, wo, wo_from, wq, wk, wv, qkv,
+        prefix, x, scales, gain, *tables, logs, ffn_gains, mid, dz_own, dz_oth, wo, wo_from, wq, wk, wv, qkv,
         a_own, a_oth, wdown, n1, o_own, o_oth, down, gate, up,
     )
 
@@ -1481,7 +1476,7 @@
         gate_weight, up_weight, row_count, dp_count,
     )
     in_grad, last_result, qkv_sum, output_sum, down_sum, gate_sum, up_sum, gains = backward(
-        prefix_len, hidden_in, scales, attn_gain.reshape(1, -1), tables, logs, ffn_gains, middle_grad,
+        prefix_len, hidden_in, scales, attn_gain.reshape(1, -1), tables, logs, ffn_gains,
         middle, dz, dz_oth, output_weight, out_from, query_weight, key_weight, value_weight, qkv, a_own, a_oth, down_weight,
         *flat(n1, o_own, o_oth), down_sum, gate_sum, up_sum, heads, shared_kv, dp_count,
     )
@@ -1498,7 +1493,7 @@
     gain_one, gain_two = gains[:batches].sum(axis=0), gains[batches : 2 * batches].sum(axis=0)
     meanwhile = (
         result,
-        in_grad,
+        middle_grad + in_grad,
         gain_one,
         gain_two,
         columns(0, q_width, False),

time: 573 us -> 571 us (level)
  no operation moved by 1% of the time
where the time goes in v5:
time: 571 us; the launch traced here: 562 us
  Pallas kernels  529 us (93%)
  other arithmetic  24.7 us (4%)
    pallas_call x1, Pallas kernels, forward(): pl.pallas_call(functools.partial(forward_kernel, n, heads, shared_kv), in...  258 us
    pallas_call x1, Pallas kernels, backward(): pl.pallas_call(functools.partial(backward_kernel, n, heads, shared_kv, bi...  143 us
    pallas_call x1, Pallas kernels, unit_grads(): pl.pallas_call(functools.partial(unit_grads_kernel, n, bits), in_specs=[v...  128 us
  transfers between devices with their start and end apart: 2, of which 2 were waited for; matrix products, arithmetic and copies ran while one was open for 3% of the time, Pallas kernels for 0%

profile of v5, /device:TPU:0, one launch (start us, length us, event | category | flops | bytes accessed | tf_op | source)
XLA Modules:
  0.0 562.4 jit_solution(12053899661479286260)
XLA Ops:
  0.6 1.3 copy.29.prefix_ref
  1.9 257.9 %shard_map.221 = (bf16[2,4,256,1024]{3,2,1,0:T(8,128)(2,1)}, bf16[2,4,256,1024]{3,2,1,0:T(8,128)(2,1)}, bf16[2,4,256,1024]{3,2,1,0:T(8,128)(2,1)}, bf16[2,1024,5...) custom-call(s32[2,1]{1,0:T(2,128)} %copy.29.prefix_ref, ...), custom_call_target="tpu_custom_call" | custom-call | flops 199999995904 | bytes 104857600 | tf_op jit(solution)/shard_map/pallas_call | solution.py:761
  259.9 128.3 %shard_map.222 = (bf16[2,4,256,1024]{3,2,1,0:T(8,128)(2,1)}, bf16[1,4,256,1024]{3,2,1,0:T(8,128)(2,1)}, f32[2,256,1024]{2,1,0:T(8,128)}, bf16[2048,1024]{1,0:T(8...) custom-call(f32[2,256,1024]{2,1,0:T(8,128)} %get-tuple-element.59.mid_ref.mid_in, ...), custom_call_target="tpu_custom_call" | custom-call | flops 199999995904 | bytes 104857600 | tf_op jit(solution)/shard_map/pallas_call | solution.py:1024
  388.2 142.7 %shard_map.223 = (f32[2,256,1024]{2,1,0:T(8,128)}, bf16[256,1024]{1,0:T(8,128)(2,1)}, bf16[1024,1024]{1,0:T(8,128)(2,1)}, bf16[512,1024]{1,0:T(8,128)(2,1)}, bf1...) custom-call(s32[2,1]{1,0:T(2,128)} %copy.29.prefix_ref, ...), custom_call_target="tpu_custom_call", output_to_operand_aliasing={{4}: (23, {}), {5}: (24, {}), {6}: (25, {})} | custom-call | flops 199999995904 | bytes 104857600 | tf_op jit(solution)/shard_map/pallas_call | solution.py:1382
  530.9 1.7 constant_dynamic-slice_fusion
  532.6 1.0 collective-permute-start
  533.6 1.4 collective-permute-start.1
  535.0 6.8 %convert_element_type.7 = f32[1024,2048]{1,0:T(8,128)} convert(bf16[1024,2048]{1,0:T(8,128)(2,1)} %get-tuple-element.87) | non-fusion elementwise | flops 2097152 | bytes 12582912 | tf_op jit(solution)/shard_map/convert_element_type | solution.py:1503
  541.8 4.4 convert_element_type.8
  546.2 0.0 copy-start.6
  546.3 1.6 convert_element_type.6
  547.8 0.8 copy-done.1
  548.6 1.7 add.13
  550.3 0.6 slice_reduce_fusion
  550.9 1.1 pad_maximum_fusion
  552.0 0.1 fusion.1
  552.1 1.6 maximum_convert_fusion.1
  553.7 0.2 fusion
  553.8 1.5 maximum_convert_fusion.2
  555.3 0.6 collective-permute-done
  555.9 0.5 collective-permute-done.1
  556.5 1.4 broadcast_select_fusion.3
  557.8 0.1 broadcast_select_fusion.1
  558.0 3.9 maximum_convert_fusion
  (14 shorter events, 0.0 us)
Async XLA Ops:
  532.6 23.3 %collective-permute-start = (bf16[256,2048]{1,0:T(8,128)(2,1)S(1)}, bf16[256,2048]{1,0:T(8,128)(2,1)}, u32[]{:S(2)}, u32[]{:S(2)}) collective-permute-start(bf16[256,2048]{1,0:T(8,128)(2,1)S(1)} %get-tuple-element.98), channel_id=1, source_target_pairs={{0,8},{8,0},{16,24},{24,16},{1,9},{9,1},{17,25},{25,17},{2,10},{10... | collective-permute-start | bytes 3145736 | tf_op jit(solution)/shard_map/ppermute | solution.py:1430
  533.6 22.9 %collective-permute-start.1 = (bf16[256,2048]{1,0:T(8,128)(2,1)S(1)}, bf16[256,2048]{1,0:T(8,128)(2,1)S(1)}, u32[]{:S(2)}, u32[]{:S(2)}) collective-permute-start(bf16[256,2048]{1,0:T(8,128)(2,1)S(1)} %get-tuple-element.100), channel_id=1, source_target_pairs={{0,16},{8,24},{16,0},{24,8},{1,17},{9,25},{17,1},{25,9},{2,18},{10... | collective-permute-start | bytes 3145736 | tf_op jit(solution)/shard_map/ppermute | solution.py:1430
  535.0 6.8 %copy-start = (bf16[2048,1024]{1,0:T(8,128)(2,1)S(1)}, bf16[2048,1024]{1,0:T(8,128)(2,1)}, u32[]{:S(2)}) copy-start(bf16[2048,1024]{1,0:T(8,128)(2,1)} %get-tuple-element.88) | copy-start | bytes 12582916
  541.8 4.4 copy-start.4
  541.8 6.0 %copy-start.2 = (f32[2,256,1024]{2,1,0:T(8,128)S(1)}, f32[2,256,1024]{2,1,0:T(8,128)}, u32[]{:S(2)}) copy-start(f32[2,256,1024]{2,1,0:T(8,128)} %get-tuple-element.83) | copy-start | bytes 6291460
  546.2 2.3 copy-start.1
  546.2 4.1 copy-start.7
  546.2 4.7 copy-start.5
  546.2 4.7 copy-start.6
  548.6 3.4 copy-start.3

commit v6 on v5

--- a/solution.py
+++ b/solution.py
@@ -3,7 +3,6 @@
 
 import jax
 import jax.numpy as jnp
-import numpy as np
 from jax import lax
 from jax.experimental import pallas as pl
 from jax.experimental.pallas import tpu as pltpu
@@ -45,13 +44,13 @@
     return pl.BlockSpec(shape, lambda *_: (0,) * len(shape))
 
 
-def rope_tables(length):
+def rope_tables(first, rows):
     half_size = HEAD_DIM // 2
-    inverse = rope_base ** (-(np.arange(half_size) * 2.0 / HEAD_DIM))
-    angle = np.arange(length)[:, None] * inverse[None, :]
-    cosine = np.concatenate([np.cos(angle), np.cos(angle)], axis=1)
-    signed = np.concatenate([-np.sin(angle), np.sin(angle)], axis=1)
-    return jnp.asarray(cosine, F32), jnp.asarray(signed, F32)
+    lane = lax.broadcasted_iota(jnp.int32, (rows, HEAD_DIM), 1)
+    inverse = jnp.exp((lane & (half_size - 1)).astype(F32) * (-math.log(rope_base) / half_size))
+    angle = (lax.broadcasted_iota(jnp.int32, (rows, HEAD_DIM), 0) + first).astype(F32) * inverse
+    sine = jnp.sin(angle)
+    return jnp.cos(angle), jnp.where(lane < half_size, -sine, sine)
 
 
 def rope(values, cosine, signed):
@@ -387,12 +386,12 @@
 
 def forward_kernel(
     n, heads, shared_kv,
-    prefix_ref, x_ref, gain_one, gain_two, cos_ref, sin_ref,
+    prefix_ref, x_ref, gain_one, gain_two,
     grad_in, wq, wk, wv, wo, wgate, wup, wdown,
-    n1_out, n2_out, g_out, qkv_out, log_out, o_own_out, o_oth_out, mid_out, scale_out, wo_from,
+    cos_out, sin_out, n1_out, n2_out, g_out, qkv_out, log_out, o_own_out, o_oth_out, mid_out, scale_out, wo_from,
     a_own_out, a_oth_out, dg_own_out, dg_oth_out, du_own_out, du_oth_out, result_out,
     n_own, n_oth, g_own, g_oth, w_own, w_from, wo_ref, wg_ref, wu_ref, wd_ref, wd_oth, a_ref,
-    qkv_ref, vt_ref, o_own, o_oth, log_ref, part, ups, downs, total, scales, row_out, row_in, stage,
+    cos_ref, sin_ref, qkv_ref, vt_ref, o_own, o_oth, log_ref, part, ups, downs, total, scales, row_out, row_in, stage,
     gather_sends, gather_recvs, scatter_sends, scatter_recvs, cross_sends, cross_recvs, local_sems,
     unit_sends, unit_recvs, unit_stores, down_sends, down_recvs, a_sems,
 ):
@@ -481,6 +480,12 @@
             n1[0].start()
             for copy in w_cross:
                 copy.start()
+
+    @pl.loop(0, n)
+    def _(p):
+        rows = rows_at(p * tokens, tokens)
+        cos_ref[rows, :], sin_ref[rows, :] = rope_tables(p * tokens, tokens)
+
     for copy in loads:
         copy.wait()
     for copy in w_cross:
@@ -507,7 +512,7 @@
         keys = qkv_ref[m, pl.ds(0, extent), pl.ds(k_col, HEAD_DIM)]
         key_at = lax.broadcasted_iota(jnp.int32, (extent, block), 0)
         query_at = lax.broadcasted_iota(jnp.int32, (extent, block), 1) + first
-        allowed = (key_at <= query_at) | (key_at < prefix_ref[m, 0])
+        allowed = (key_at <= query_at) | (key_at < prefix_ref[:, pl.ds(m, 1)])
         for head in range(heads):
             cols = pl.ds(head * HEAD_DIM, HEAD_DIM)
             query = qkv_ref[m, pl.ds(first, block), cols]
@@ -612,22 +617,16 @@
             unit_away(k, 0).wait_recv()
         rs[0].drain()
 
-        def a_loads(p):
-            return [
-                pltpu.make_async_copy(src.at[0, p], a_ref.at[p % 2, side], a_sems.at[p % 2, side])
+        for p in range(n):
+            a_loads = [
+                pltpu.make_async_copy(src.at[0, p], a_ref.at[side], a_sems.at[side])
                 for side, src in enumerate((a_own_out, a_oth_out))
             ]
-
-        for p in range(n):
-            if p == 0:
-                for copy in a_loads(0):
-                    copy.start()
-            for copy in a_loads(p):
+            for copy in a_loads:
+                copy.start()
+            for copy in a_loads:
                 copy.wait()
-            if p + 1 < n:
-                for copy in a_loads(p + 1):
-                    copy.start()
-            value = dot(a_ref[p % 2, 0], wd_ref[0], NN) + dot(a_ref[p % 2, 1], wd_oth[...], NN)
+            value = dot(a_ref[0], wd_ref[0], NN) + dot(a_ref[1], wd_oth[...], NN)
             part[0, p] = value.astype(BF16)
 
     half = (n + 1) // 2
@@ -692,6 +691,7 @@
     g_loads[1].wait()
     stores += [local(g_own.at[0], g_out.at[0])]
     stores += [local(qkv_ref, qkv_out), local(log_ref, log_out)]
+    stores += [local(cos_ref, cos_out), local(sin_ref, sin_out)]
     stores += [local(o_own, o_own_out), local(o_oth, o_oth_out)]
     mid_store = local(total.at[0], mid_out.at[0])
     units(0)
@@ -739,7 +739,7 @@
 
 
 def forward(
-    prefix, x, gain_one, gain_two, tables, grad_in, wq, wk, wv, wo, wgate, wup, wdown, n, heads, shared_kv
+    prefix, x, gain_one, gain_two, grad_in, wq, wk, wv, wo, wgate, wup, wdown, n, heads, shared_kv
 ):
     batches, tokens, depth = x.shape
     length = n * tokens
@@ -750,8 +750,9 @@
     anywhere = pl.BlockSpec(memory_space=pl.ANY)
     gathered, units = (batches, n, tokens, depth), (batches, n, tokens, share)
     rows = (2, batches, tokens, 128)
+    table = (length, HEAD_DIM)
     shapes = [
-        (gathered, BF16), (gathered, BF16), (gathered, BF16),
+        (table, F32), (table, F32), (gathered, BF16), (gathered, BF16), (gathered, BF16),
         ((batches, length, width), BF16), ((batches, 8, length), F32),
         ((batches, length, q_width), BF16), ((batches, length, q_width), BF16),
         ((batches, tokens, depth), F32), (rows, F32), ((q_width, depth), BF16),
@@ -760,7 +761,7 @@
     dma = pltpu.SemaphoreType.DMA
     return pl.pallas_call(
         functools.partial(forward_kernel, n, heads, shared_kv),
-        in_specs=[pl.BlockSpec(memory_space=pltpu.SMEM)] + [vmem] * 5 + [anywhere] * 8,
+        in_specs=[vmem] * 4 + [anywhere] * 8,
         out_specs=[anywhere] * len(shapes),
         out_shape=[jax.ShapeDtypeStruct(*item) for item in shapes],
         scratch_shapes=[
@@ -770,7 +771,7 @@
             pltpu.VMEM(wo.shape, BF16),
             pltpu.VMEM((2, depth, share), BF16), pltpu.VMEM((2, depth, share), BF16),
             pltpu.VMEM((2, share, depth), BF16), pltpu.VMEM((share, depth), BF16),
-            pltpu.VMEM((2, 2, tokens, share), BF16),
+            pltpu.VMEM((2, tokens, share), BF16), pltpu.VMEM(table, F32), pltpu.VMEM(table, F32),
             pltpu.VMEM((batches, length, width), BF16),
             pltpu.VMEM((batches, HEAD_DIM, length), BF16),
             pltpu.VMEM((batches, length, q_width), BF16), pltpu.VMEM((batches, length, q_width), BF16),
@@ -780,13 +781,13 @@
             pltpu.VMEM(rows, F32), pltpu.VMEM(rows, F32), pltpu.VMEM(rows, F32),
             pltpu.VMEM((2, 3, tokens, share), BF16),
             dma((3, batches, n, 3)), dma((3, batches, n, 2)),
-            dma((batches, 2, n - 1)), dma((batches, 2, n - 1)), dma((13,)), dma((13,)), dma((24,)),
+            dma((batches, 2, n - 1)), dma((batches, 2, n - 1)), dma((13,)), dma((13,)), dma((26,)),
             dma((batches * n, 3)), dma((batches * n, 3)), dma((batches * n, 3)),
-            dma((2, n - 1)), dma((2, n - 1)), dma((2, 2)),
+            dma((2, n - 1)), dma((2, n - 1)), dma((2,)),
         ],
         compiler_params=communicate(1, 63),
         cost_estimate=cost(2e11, 100 * MIB),
-    )(prefix, x, gain_one, gain_two, *tables, grad_in, wq, wk, wv, wo, wgate, wup, wdown)
+    )(prefix, x, gain_one, gain_two, grad_in, wq, wk, wv, wo, wgate, wup, wdown)
 
 
 def unit_grads_kernel(
@@ -867,7 +868,7 @@
             for copy in unit_loads(at + 1):
                 copy.start()
         slot = at % 2
-        block = min(256, depth)
+        block = min(512, depth)
 
         @pl.loop(0, depth // block)
         def _(b):
@@ -1206,7 +1207,7 @@
         values = qkv_ref[m, upto, pl.ds(v_col, HEAD_DIM)]
         key_at = lax.broadcasted_iota(jnp.int32, (extent, tokens), 0)
         query_at = lax.broadcasted_iota(jnp.int32, (extent, tokens), 1) + q * tokens
-        allowed = (key_at <= query_at) | (key_at < prefix_ref[m, 0])
+        allowed = (key_at <= query_at) | (key_at < prefix_ref[:, pl.ds(m, 1)])
         for head in range(heads):
             cols = pl.ds(head * HEAD_DIM, HEAD_DIM)
             query = qkv_ref[m, rows, cols]
@@ -1381,7 +1382,7 @@
     dma = pltpu.SemaphoreType.DMA
     return pl.pallas_call(
         functools.partial(backward_kernel, n, heads, shared_kv, bits),
-        in_specs=[pl.BlockSpec(memory_space=pltpu.SMEM)] + [vmem] * 7 + [anywhere] * 18,
+        in_specs=[vmem] * 8 + [anywhere] * 18,
         out_specs=[anywhere] * 7 + [vmem],
         out_shape=[jax.ShapeDtypeStruct(*item) for item in shapes],
         input_output_aliases={23: 4, 24: 5, 25: 6},
@@ -1456,12 +1457,12 @@
     row_kv = key_weight.shape[1] // HEAD_DIM
     shared_kv = row_kv < col_count
     q_width = heads * HEAD_DIM
-    tables = rope_tables(length)
+    prefix_row = prefix_len.reshape(1, batches)
     (
-        n1, n2, g_own, qkv, logs, o_own, o_oth, middle, scales, out_from,
+        cosine, signed, n1, n2, g_own, qkv, logs, o_own, o_oth, middle, scales, out_from,
         a_own, a_oth, dg_own, dg_oth, du_own, du_oth, first_result,
     ) = forward(
-        prefix_len, hidden_in, attn_gain.reshape(1, -1), ffn_gain.reshape(1, -1), tables, out_grad,
+        prefix_row, hidden_in, attn_gain.reshape(1, -1), ffn_gain.reshape(1, -1), out_grad,
         query_weight, key_weight, value_weight, output_weight, gate_weight, up_weight, down_weight,
         row_count, heads, shared_kv,
     )
@@ -1476,7 +1477,7 @@
         gate_weight, up_weight, row_count, dp_count,
     )
     in_grad, last_result, qkv_sum, output_sum, down_sum, gate_sum, up_sum, gains = backward(
-        prefix_len, hidden_in, scales, attn_gain.reshape(1, -1), tables, logs, ffn_gains,
+        prefix_row, hidden_in, scales, attn_gain.reshape(1, -1), (cosine, signed), logs, ffn_gains,
         middle, dz, dz_oth, output_weight, out_from, query_weight, key_weight, value_weight, qkv, a_own, a_oth, down_weight,
         *flat(n1, o_own, o_oth), down_sum, gate_sum, up_sum, heads, shared_kv, dp_count,
     )

time: 571 us -> 567 us (level)
  no operation moved by 1% of the time
where the time goes in v6:
time: 567 us; the launch traced here: 558 us
  Pallas kernels  526 us (93%)
  other arithmetic  24.7 us (4%)
    pallas_call x1, Pallas kernels, forward(): pl.pallas_call(functools.partial(forward_kernel, n, heads, shared_kv), in...  258 us
    pallas_call x1, Pallas kernels, backward(): pl.pallas_call(functools.partial(backward_kernel, n, heads, shared_kv, bi...  143 us
    pallas_call x1, Pallas kernels, unit_grads(): pl.pallas_call(functools.partial(unit_grads_kernel, n, bits), in_specs=[v...  126 us
  transfers between devices with their start and end apart: 2, of which 2 were waited for; matrix products, arithmetic and copies ran while one was open for 3% of the time, Pallas kernels for 0%

profile of v6, /device:TPU:0, one launch (start us, length us, event | category | flops | bytes accessed | tf_op | source)
XLA Modules:
  0.0 558.4 jit_solution(11513642151326864721)
XLA Ops:
  0.7 257.7 %shard_map.203 = (f32[1024,128]{1,0:T(8,128)}, f32[1024,128]{1,0:T(8,128)}, bf16[2,4,256,1024]{3,2,1,0:T(8,128)(2,1)}, bf16[2,4,256,1024]{3,2,1,0:T(8,128)(2,1)}...) custom-call(s32[1,2]{1,0:T(1,128)} %bitcast.22, ...), custom_call_target="tpu_custom_call" | custom-call | flops 199999995904 | bytes 104857600 | tf_op jit(solution)/shard_map/pallas_call | solution.py:762
  258.4 126.1 %shard_map.204 = (bf16[2,4,256,1024]{3,2,1,0:T(8,128)(2,1)}, bf16[1,4,256,1024]{3,2,1,0:T(8,128)(2,1)}, f32[2,256,1024]{2,1,0:T(8,128)}, bf16[2048,1024]{1,0:T(8...) custom-call(f32[2,256,1024]{2,1,0:T(8,128)} %get-tuple-element.63.mid_ref.mid_in, ...), custom_call_target="tpu_custom_call" | custom-call | flops 199999995904 | bytes 104857600 | tf_op jit(solution)/shard_map/pallas_call | solution.py:1025
  384.5 142.7 %shard_map.205 = (f32[2,256,1024]{2,1,0:T(8,128)}, bf16[256,1024]{1,0:T(8,128)(2,1)}, bf16[1024,1024]{1,0:T(8,128)(2,1)}, bf16[512,1024]{1,0:T(8,128)(2,1)}, bf1...) custom-call(s32[1,2]{1,0:T(1,128)} %bitcast.23, ...), custom_call_target="tpu_custom_call", output_to_operand_aliasing={{4}: (23, {}), {5}: (24, {}), {6}: (25, {})} | custom-call | flops 199999995904 | bytes 104857600 | tf_op jit(solution)/shard_map/pallas_call | solution.py:1383
  527.1 1.7 constant_dynamic-slice_fusion
  528.8 1.0 collective-permute-start
  529.8 1.4 collective-permute-start.1
  531.2 6.8 %convert_element_type.7 = f32[1024,2048]{1,0:T(8,128)} convert(bf16[1024,2048]{1,0:T(8,128)(2,1)} %get-tuple-element.91) | non-fusion elementwise | flops 2097152 | bytes 12582912 | tf_op jit(solution)/shard_map/convert_element_type | solution.py:1504
  538.0 0.0 copy-done
  538.0 4.4 convert_element_type.8
  542.4 0.0 copy-done.4
  542.5 1.6 convert_element_type.6
  544.0 0.8 copy-done.1
  544.8 1.7 add.13
  546.5 0.6 slice_reduce_fusion
  547.1 1.1 pad_maximum_fusion
  548.2 0.1 fusion.1
  548.3 1.6 maximum_convert_fusion.1
  549.9 0.2 fusion
  550.1 1.5 maximum_convert_fusion.2
  551.5 0.6 collective-permute-done
  552.1 0.5 collective-permute-done.1
  552.7 1.4 broadcast_select_fusion.3
  554.0 0.1 broadcast_select_fusion.1
  554.2 3.9 maximum_convert_fusion
  (13 shorter events, 0.0 us)
Async XLA Ops:
  528.8 23.3 %collective-permute-start = (bf16[256,2048]{1,0:T(8,128)(2,1)S(1)}, bf16[256,2048]{1,0:T(8,128)(2,1)}, u32[]{:S(2)}, u32[]{:S(2)}) collective-permute-start(bf16[256,2048]{1,0:T(8,128)(2,1)S(1)} %get-tuple-element.102), channel_id=1, source_target_pairs={{0,8},{8,0},{16,24},{24,16},{1,9},{9,1},{17,25},{25,17},{2,10},{10... | collective-permute-start | bytes 3145736 | tf_op jit(solution)/shard_map/ppermute | solution.py:1431
  529.8 22.9 %collective-permute-start.1 = (bf16[256,2048]{1,0:T(8,128)(2,1)S(1)}, bf16[256,2048]{1,0:T(8,128)(2,1)S(1)}, u32[]{:S(2)}, u32[]{:S(2)}) collective-permute-start(bf16[256,2048]{1,0:T(8,128)(2,1)S(1)} %get-tuple-element.104), channel_id=1, source_target_pairs={{0,16},{8,24},{16,0},{24,8},{1,17},{9,25},{17,1},{25,9},{2,18},{10... | collective-permute-start | bytes 3145736 | tf_op jit(solution)/shard_map/ppermute | solution.py:1431
  531.2 6.8 %copy-start = (bf16[2048,1024]{1,0:T(8,128)(2,1)S(1)}, bf16[2048,1024]{1,0:T(8,128)(2,1)}, u32[]{:S(2)}) copy-start(bf16[2048,1024]{1,0:T(8,128)(2,1)} %get-tuple-element.92) | copy-start | bytes 12582916
  538.0 4.4 copy-start.4
  538.0 6.0 %copy-start.2 = (f32[2,256,1024]{2,1,0:T(8,128)S(1)}, f32[2,256,1024]{2,1,0:T(8,128)}, u32[]{:S(2)}) copy-start(f32[2,256,1024]{2,1,0:T(8,128)} %get-tuple-element.87) | copy-start | bytes 6291460
  542.4 2.3 copy-start.1
  542.4 4.1 copy-start.7
  542.4 4.7 copy-start.5
  542.5 4.7 copy-start.6
  544.8 3.4 copy-start.3

commit v7 on v6

--- a/solution.py
+++ b/solution.py
@@ -710,15 +710,15 @@
     stores.append(local(scales, scale_out))
     n2[0].step(n - 1)
     units(n - 1)
-    units(n)
     down_project()
     down_rs.step(1)
+    units(n)
     for k in range(1, n):
         g[1].step(k)
         n2[1].step(k)
-        units(n + k)
         if k + 1 < n:
             down_rs.step(k + 1)
+        units(n + k)
     stores += [local(g_own.at[1], g_out.at[1]), local(n_own, n2_out)]
     mid_store.wait()
     total[0] = total[0] + part[0, r].astype(F32)

time: 567 us -> 567 us (level)
  no operation moved by 1% of the time
where the time goes in v7:
time: 567 us; the launch traced here: 558 us
  Pallas kernels  526 us (93%)
  other arithmetic  24.7 us (4%)
    pallas_call x1, Pallas kernels, forward(): pl.pallas_call(functools.partial(forward_kernel, n, heads, shared_kv), in...  258 us
    pallas_call x1, Pallas kernels, backward(): pl.pallas_call(functools.partial(backward_kernel, n, heads, shared_kv, bi...  143 us
    pallas_call x1, Pallas kernels, unit_grads(): pl.pallas_call(functools.partial(unit_grads_kernel, n, bits), in_specs=[v...  126 us
  transfers between devices with their start and end apart: 2, of which 2 were waited for; matrix products, arithmetic and copies ran while one was open for 3% of the time, Pallas kernels for 0%

profile of v7, /device:TPU:0, one launch (start us, length us, event | category | flops | bytes accessed | tf_op | source)
XLA Modules:
  0.0 558.4 jit_solution(1924066658886187814)
XLA Ops:
  0.7 257.7 %shard_map.203 = (f32[1024,128]{1,0:T(8,128)}, f32[1024,128]{1,0:T(8,128)}, bf16[2,4,256,1024]{3,2,1,0:T(8,128)(2,1)}, bf16[2,4,256,1024]{3,2,1,0:T(8,128)(2,1)}...) custom-call(s32[1,2]{1,0:T(1,128)} %bitcast.22, ...), custom_call_target="tpu_custom_call" | custom-call | flops 199999995904 | bytes 104857600 | tf_op jit(solution)/shard_map/pallas_call | solution.py:762
  258.4 126.1 %shard_map.204 = (bf16[2,4,256,1024]{3,2,1,0:T(8,128)(2,1)}, bf16[1,4,256,1024]{3,2,1,0:T(8,128)(2,1)}, f32[2,256,1024]{2,1,0:T(8,128)}, bf16[2048,1024]{1,0:T(8...) custom-call(f32[2,256,1024]{2,1,0:T(8,128)} %get-tuple-element.63.mid_ref.mid_in, ...), custom_call_target="tpu_custom_call" | custom-call | flops 199999995904 | bytes 104857600 | tf_op jit(solution)/shard_map/pallas_call | solution.py:1025
  384.5 142.7 %shard_map.205 = (f32[2,256,1024]{2,1,0:T(8,128)}, bf16[256,1024]{1,0:T(8,128)(2,1)}, bf16[1024,1024]{1,0:T(8,128)(2,1)}, bf16[512,1024]{1,0:T(8,128)(2,1)}, bf1...) custom-call(s32[1,2]{1,0:T(1,128)} %bitcast.23, ...), custom_call_target="tpu_custom_call", output_to_operand_aliasing={{4}: (23, {}), {5}: (24, {}), {6}: (25, {})} | custom-call | flops 199999995904 | bytes 104857600 | tf_op jit(solution)/shard_map/pallas_call | solution.py:1383
  527.1 1.7 constant_dynamic-slice_fusion
  528.8 1.0 collective-permute-start
  529.8 1.4 collective-permute-start.1
  531.2 6.8 %convert_element_type.7 = f32[1024,2048]{1,0:T(8,128)} convert(bf16[1024,2048]{1,0:T(8,128)(2,1)} %get-tuple-element.91) | non-fusion elementwise | flops 2097152 | bytes 12582912 | tf_op jit(solution)/shard_map/convert_element_type | solution.py:1504
  538.0 0.0 copy-done
  538.0 4.4 convert_element_type.8
  542.4 0.0 copy-done.4
  542.5 1.6 convert_element_type.6
  544.0 0.8 copy-done.1
  544.8 1.7 add.13
  546.5 0.6 slice_reduce_fusion
  547.1 1.1 pad_maximum_fusion
  548.2 0.1 fusion.1
  548.3 1.6 maximum_convert_fusion.1
  549.9 0.2 fusion
  550.1 1.5 maximum_convert_fusion.2
  551.5 0.6 collective-permute-done
  552.1 0.5 collective-permute-done.1
  552.7 1.4 broadcast_select_fusion.3
  554.0 0.1 broadcast_select_fusion.1
  554.2 3.9 maximum_convert_fusion
  (13 shorter events, 0.0 us)
Async XLA Ops:
  528.8 23.3 %collective-permute-start = (bf16[256,2048]{1,0:T(8,128)(2,1)S(1)}, bf16[256,2048]{1,0:T(8,128)(2,1)}, u32[]{:S(2)}, u32[]{:S(2)}) collective-permute-start(bf16[256,2048]{1,0:T(8,128)(2,1)S(1)} %get-tuple-element.102), channel_id=1, source_target_pairs={{0,8},{8,0},{16,24},{24,16},{1,9},{9,1},{17,25},{25,17},{2,10},{10... | collective-permute-start | bytes 3145736 | tf_op jit(solution)/shard_map/ppermute | solution.py:1431
  529.8 22.9 %collective-permute-start.1 = (bf16[256,2048]{1,0:T(8,128)(2,1)S(1)}, bf16[256,2048]{1,0:T(8,128)(2,1)S(1)}, u32[]{:S(2)}, u32[]{:S(2)}) collective-permute-start(bf16[256,2048]{1,0:T(8,128)(2,1)S(1)} %get-tuple-element.104), channel_id=1, source_target_pairs={{0,16},{8,24},{16,0},{24,8},{1,17},{9,25},{17,1},{25,9},{2,18},{10... | collective-permute-start | bytes 3145736 | tf_op jit(solution)/shard_map/ppermute | solution.py:1431
  531.2 6.8 %copy-start = (bf16[2048,1024]{1,0:T(8,128)(2,1)S(1)}, bf16[2048,1024]{1,0:T(8,128)(2,1)}, u32[]{:S(2)}) copy-start(bf16[2048,1024]{1,0:T(8,128)(2,1)} %get-tuple-element.92) | copy-start | bytes 12582916
  538.0 4.4 copy-start.4
  538.0 6.0 %copy-start.2 = (f32[2,256,1024]{2,1,0:T(8,128)S(1)}, f32[2,256,1024]{2,1,0:T(8,128)}, u32[]{:S(2)}) copy-start(f32[2,256,1024]{2,1,0:T(8,128)} %get-tuple-element.87) | copy-start | bytes 6291460
  542.4 2.3 copy-start.1
  542.4 4.1 copy-start.7
  542.4 4.7 copy-start.5
  542.5 4.7 copy-start.6
  544.8 3.4 copy-start.3
